TPU v7x, 32 devices: a whole 2x2x4 slice. The times are simulated.
32 devices in a mesh: seq: 16 (over z, y, x), head: 2 (over core).
Axes of the slice: x: 2, y: 2, z: 4, core: 2. Of those that a mesh axis runs over, the one named last changes fastest.
Arguments:
- inputs: bfloat16 [2048, 2048], P('seq'), may hold values from -6.3 to 6.3
- doc_starts: int32 [2048], P('seq'), may hold values from 0 to 1, as said below
- decay_rate: float32 [2048, 16], P('seq', 'head'), may hold values from 0.4 to 1
- mixer_gain: bfloat16 [2048], P('seq'), may hold values from 0.5 to 1.5
- w_query: bfloat16 [2048, 2048], P('seq', 'head'), may hold values from -0.125 to 0.125
- w_key: bfloat16 [2048, 2048], P('seq', 'head'), may hold values from -0.125 to 0.125
- w_value: bfloat16 [2048, 4096], P('seq', 'head'), may hold values from -0.125 to 0.125
- w_beta: bfloat16 [2048, 16], P('seq', 'head'), may hold values from -1 to 1
- w_gating: bfloat16 [2048, 4096], P('seq', 'head'), may hold values from -0.125 to 0.125
- conv_query: bfloat16 [4, 2048], P(None, 'head'), may hold values from -3 to 3
- conv_key: bfloat16 [4, 2048], P(None, 'head'), may hold values from -3 to 3
- conv_value: bfloat16 [4, 4096], P(None, 'head'), may hold values from -3 to 3
- head_gain: bfloat16 [256], replicated, may hold values from 0.5 to 1.5
- w_output: bfloat16 [4096, 2048], P('head', 'seq'), may hold values from -0.1875 to 0.1875
- feed_gain: bfloat16 [2048], P('seq'), may hold values from 0.5 to 1.5
- w_gate: bfloat16 [2048, 5632], P('seq', 'head'), may hold values from -0.125 to 0.125
- w_up: bfloat16 [2048, 5632], P('seq', 'head'), may hold values from -0.125 to 0.125
- w_down: bfloat16 [5632, 2048], P('head', 'seq'), may hold values from -0.109375 to 0.109375
- cotangent: bfloat16 [2048, 2048], P('seq'), may hold values from -6 to 6
Outputs:
- block_out: bfloat16 [2048, 2048], P('seq')
- grad_inputs: float32 [2048, 2048], P('seq')
- grad_mixer_gain: float32 [2048], P('seq')
- grad_query: float32 [2048, 2048], P('seq', 'head')
- grad_key: float32 [2048, 2048], P('seq', 'head')
- grad_value: float32 [2048, 4096], P('seq', 'head')
- grad_beta: float32 [2048, 16], P('seq', 'head')
- grad_gating: float32 [2048, 4096], P('seq', 'head')
- grad_conv_query: float32 [4, 2048], P(None, 'head')
- grad_conv_key: float32 [4, 2048], P(None, 'head')
- grad_conv_value: float32 [4, 4096], P(None, 'head')
- grad_head_gain: float32 [256], replicated
- grad_output: float32 [4096, 2048], P('head', 'seq')
- grad_feed_gain: float32 [2048], P('seq')
- grad_gate: float32 [2048, 5632], P('seq', 'head')
- grad_up: float32 [2048, 5632], P('seq', 'head')
- grad_down: float32 [5632, 2048], P('head', 'seq')
Inputs may be any that keep to these rules, and one draw needn't show every extreme that they name: `doc_starts`: document start flags; the first token of the stream always starts a document.
All inputs are finite; a program needn't handle non-finite values.
Results may differ from a plain program's by a relative error of at most 0.02.
Values may be sent and summed in bfloat16 or wider, within the bound.
No kernel may reach another device: no remote copies, remote signals or barrier semaphores. Data moves between devices by JAX's collectives and lax.ppermute only.
A program may use at most 384 MiB of HBM per device.

v0:
```python
import jax
import jax.numpy as jnp
from jax import lax
from jax.sharding import PartitionSpec as P

KEY_SIZE = 128
DV = 256
CONV = 4
BLOCK = 64


EXACT_PRECISION = lax.Precision.HIGHEST
EPSILON = 1e-06


def passed_along(value, axis, steps):
    count = lax.axis_size(axis)
    first, last = (max(0, -steps), min(count, count - steps))
    return lax.ppermute(value, axis, [(source, source + steps) for source in range(first, last)])


def entering(value, axis, join, neutral):
    count, mine = (lax.axis_size(axis), lax.axis_index(axis))
    pieces = jax.tree.map(lambda part: lax.all_gather(part, axis), value)
    subtotal = jax.tree.map(
        lambda part, zero: jnp.full_like(part, 0) + jnp.asarray(zero, part.dtype), value, neutral
    )

    def lap(position, subtotal):
        longer = join(subtotal, jax.tree.map(lambda part: part[position], pieces))
        return jax.tree.map(lambda new, old: jnp.where(position < mine, new, old), longer, subtotal)

    return lax.fori_loop(0, count - 1, lap, subtotal)


def carried_in(shard, axis, join, neutral):
    count = lax.axis_size(axis)
    place = lax.axis_index(axis)
    ahead = count - 1 - place
    gathered = jax.tree.map(
        lambda a, kind: lax.all_gather(a.astype(kind), axis),
        shard,
        jax.tree.map(lambda a: jnp.bfloat16 if a.dtype == jnp.float32 else a.dtype, shard),
    )
    state = jax.tree.map(lambda a, e: jnp.zeros_like(a) + jnp.asarray(e, a.dtype), shard, neutral)

    def one(lap, state):
        source = count - 1 - lap
        return join(
            state,
            jax.tree.map(
                lambda a, own: lax.dynamic_index_in_dim(a, source, 0, False).astype(own.dtype),
                gathered,
                shard,
            ),
        )

    return lax.fori_loop(0, ahead, one, state)


def high_einsum(einsum_form, *arrays):
    return jnp.einsum(
        einsum_form, *arrays, precision=EXACT_PRECISION, preferred_element_type=jnp.float32
    )


def low_dot(left_side, right_side):
    return jnp.dot(left_side, right_side, preferred_element_type=jnp.float32)


def inner_dot(left_side, right_side):
    return lax.dot_general(
        left_side, right_side, (((0,), (0,)), ((), ())), preferred_element_type=jnp.float32
    )


def outer_dot(left_side, right_side):
    return lax.dot_general(
        left_side, right_side, (((1,), (1,)), ((), ())), preferred_element_type=jnp.float32
    )


def rounded(values):
    return lax.optimization_barrier(values.astype(jnp.bfloat16)).astype(jnp.float32)


def scale_norm(values, gain_vec):
    return (
        values * lax.rsqrt(jnp.mean(values * values, axis=-1, keepdims=True) + EPSILON) * gain_vec
    )


def unit_rows(values):
    return values * lax.rsqrt(jnp.sum(values * values, axis=-1, keepdims=True) + EPSILON)


def swiglu(gate_lin, up_lin):
    return jax.nn.silu(gate_lin) * up_lin


def compose_maps(earlier_map, later_map):
    return (
        high_einsum("hde,hef->hdf", later_map[0], earlier_map[0]),
        high_einsum("hde,hef->hdf", later_map[0], earlier_map[1]) + later_map[1],
    )


def per_device(
    inputs,
    doc_starts,
    decay_rate,
    mixer_gain,
    w_query,
    w_key,
    w_value,
    w_beta,
    w_gating,
    conv_query,
    conv_key,
    conv_value,
    head_gain,
    w_output,
    feed_gain,
    w_gate,
    w_up,
    w_down,
    cotangent,
):
    tok_rows = inputs.shape[0]
    head_count = decay_rate.shape[1]
    key_width = w_query.shape[1]
    value_width = w_value.shape[1]
    edge_count = CONV - 1
    block_count = tok_rows // BLOCK
    gathered = (
        lax.all_gather(mixer_gain, "seq", axis=0, tiled=True),
        lax.all_gather(w_query, "seq", axis=0, tiled=True),
        lax.all_gather(w_key, "seq", axis=0, tiled=True),
        lax.all_gather(w_value, "seq", axis=0, tiled=True),
        lax.all_gather(w_beta, "seq", axis=0, tiled=True),
        lax.all_gather(w_gating, "seq", axis=0, tiled=True),
        lax.all_gather(w_output, "seq", axis=1, tiled=True),
        lax.all_gather(feed_gain, "seq", axis=0, tiled=True),
        lax.all_gather(w_gate, "seq", axis=0, tiled=True),
        lax.all_gather(w_up, "seq", axis=0, tiled=True),
        lax.all_gather(w_down, "seq", axis=1, tiled=True),
    )
    (
        gain_one,
        full_query,
        full_key,
        full_value,
        full_beta,
        full_gating,
        full_output,
        gain_two,
        full_gate,
        full_up,
        full_down,
    ) = gathered
    inputs_float = inputs.astype(jnp.float32)
    normed_float, norm_one_back = jax.vjp(scale_norm, inputs_float, gain_one.astype(jnp.float32))
    normed_one = normed_float.astype(jnp.bfloat16)
    query_pre = low_dot(normed_one, full_query).astype(jnp.bfloat16)
    key_pre = low_dot(normed_one, full_key).astype(jnp.bfloat16)
    value_pre = low_dot(normed_one, full_value).astype(jnp.bfloat16)
    gating_pre = low_dot(normed_one, full_gating).astype(jnp.bfloat16)
    beta_logit = low_dot(normed_one, full_beta)
    joined = jnp.concatenate([query_pre, key_pre, value_pre], axis=1)
    tail_starts = doc_starts[tok_rows - edge_count :]
    later_starts = jnp.cumsum(tail_starts[::-1])[::-1] - tail_starts
    sender_keep = (later_starts == 0).astype(jnp.bfloat16)[:, None]
    edge_in = passed_along(joined[tok_rows - edge_count :] * sender_keep, "seq", 1)
    local_doc = jnp.cumsum(doc_starts)
    padded_doc = jnp.concatenate([jnp.zeros((edge_count,), local_doc.dtype), local_doc])
    keep_masks = [
        (
            padded_doc[edge_count - shift_lag : edge_count - shift_lag + tok_rows] == local_doc
        ).astype(jnp.float32)[:, None]
        for shift_lag in range(CONV)
    ]

    def conv_piece(extended, conv_weights):
        mixed = keep_masks[0] * conv_weights[0] * extended[edge_count:]
        for shift_lag in range(1, CONV):
            mixed = (
                mixed
                + keep_masks[shift_lag]
                * conv_weights[shift_lag]
                * extended[edge_count - shift_lag : edge_count - shift_lag + tok_rows]
            )
        activated = jax.nn.silu(mixed)
        query_unit = unit_rows(activated[:, :key_width].reshape(tok_rows, head_count, KEY_SIZE))
        key_unit = unit_rows(
            activated[:, key_width : 2 * key_width].reshape(tok_rows, head_count, KEY_SIZE)
        )
        value_act = activated[:, 2 * key_width :].reshape(tok_rows, head_count, DV)
        return (query_unit, key_unit, value_act)

    extended = jnp.concatenate([edge_in, joined], axis=0).astype(jnp.float32)
    conv_weights = jnp.concatenate([conv_query, conv_key, conv_value], axis=1).astype(jnp.float32)
    (query_unit, key_unit, value_act), conv_back = jax.vjp(conv_piece, extended, conv_weights)

    def to_blocks(values):
        return values.reshape(block_count, BLOCK, head_count, values.shape[-1]).transpose(
            0, 2, 1, 3
        )

    def from_blocks(values):
        return values.transpose(0, 2, 1, 3).reshape(tok_rows, head_count, values.shape[-1])

    log_rate = jnp.log(decay_rate).reshape(block_count, BLOCK, head_count).transpose(0, 2, 1)
    log_level = jnp.cumsum(log_rate, axis=-1)
    segment = jnp.cumsum(doc_starts.reshape(block_count, BLOCK), axis=-1)
    positions = jnp.arange(BLOCK)
    causal = positions[:, None] >= positions[None, :]
    strict = positions[:, None] > positions[None, :]
    linked = (segment[:, None, :, None] == segment[:, None, None, :]) & causal
    spread = jnp.where(causal, log_level[..., :, None] - log_level[..., None, :], 0.0)
    decay_grid = jnp.where(linked, jnp.exp(spread), 0.0)
    carry_in = jnp.where(segment[:, None, :] == 0, jnp.exp(log_level), 0.0)
    tail_decay = decay_grid[..., BLOCK - 1, :]
    key_eye = jnp.eye(KEY_SIZE, dtype=jnp.float32)
    block_eye = jnp.eye(BLOCK, dtype=jnp.float32)

    def block_terms(query_blocks, key_blocks, value_blocks, logit_blocks):
        beta_gate = jax.nn.sigmoid(logit_blocks)
        key_gram = high_einsum("nhcd,nhmd->nhcm", key_blocks, key_blocks)
        system = block_eye + jnp.where(strict, decay_grid * key_gram * beta_gate[..., None, :], 0.0)
        right_side = jnp.concatenate([value_blocks, carry_in[..., None] * key_blocks], axis=-1)
        solved = jax.scipy.linalg.solve_triangular(
            system, right_side, lower=True, unit_diagonal=True
        )
        fresh_values = solved[..., :DV]
        fresh_keys = solved[..., DV:]
        mixing = (
            high_einsum("nhcd,nhmd->nhcm", query_blocks, key_blocks)
            * decay_grid
            * beta_gate[..., None, :]
        )
        weighted = key_blocks * (tail_decay * beta_gate)[..., None]
        block_maps = carry_in[..., BLOCK - 1, None, None] * key_eye - high_einsum(
            "nhcd,nhce->nhde", weighted, fresh_keys
        )
        block_adds = high_einsum("nhcd,nhce->nhde", weighted, fresh_values)

        def chain_step(current, element):
            return (compose_maps(current, element), None)

        start_map = (
            jnp.broadcast_to(key_eye, (head_count, KEY_SIZE, KEY_SIZE)),
            jnp.zeros((head_count, KEY_SIZE, DV), jnp.float32),
        )
        device_pair, _ = lax.scan(chain_step, start_map, (block_maps, block_adds))
        return (
            (fresh_values, fresh_keys, mixing, block_maps, block_adds),
            device_pair[0],
            device_pair[1],
        )

    def block_outputs(block_parts, query_blocks, start_state):

        def step_block(current, element):
            fresh_values, fresh_keys, mixing, block_map, block_add, query_part, carry_part = element
            updated = fresh_values - high_einsum("hcd,hde->hce", fresh_keys, current)
            produced_output = (
                carry_part[..., None] * high_einsum("hcd,hde->hce", query_part, current)
                + high_einsum("hcm,hme->hce", mixing, updated)
            ) * KEY_SIZE ** (-0.5)
            return (high_einsum("hde,hef->hdf", block_map, current) + block_add, produced_output)

        _, emitted_all = lax.scan(step_block, start_state, block_parts + (query_blocks, carry_in))
        return emitted_all

    query_blocks = to_blocks(rounded(query_unit))
    key_blocks = to_blocks(rounded(key_unit))
    value_blocks = to_blocks(rounded(value_act))
    logit_blocks = beta_logit.reshape(block_count, BLOCK, head_count).transpose(0, 2, 1)
    (block_parts, device_map, device_add), terms_back = jax.vjp(
        block_terms, query_blocks, key_blocks, value_blocks, logit_blocks
    )
    identity = (jnp.broadcast_to(key_eye, device_map.shape), jnp.zeros_like(device_add))
    prefix = entering((device_map, device_add), "seq", compose_maps, identity)
    start_state = prefix[1]
    produced_output, emitted_back = jax.vjp(block_outputs, block_parts, query_blocks, start_state)

    def gated_norm(values, gating_values, gain_vec):
        normed_out = values * lax.rsqrt(jnp.mean(values * values, axis=-1, keepdims=True) + EPSILON)
        return (normed_out * gain_vec * jax.nn.silu(gating_values)).reshape(tok_rows, value_width)

    mixer_out = from_blocks(produced_output)
    gated_float, gated_back = jax.vjp(
        gated_norm,
        mixer_out,
        gating_pre.astype(jnp.float32).reshape(tok_rows, head_count, DV),
        head_gain.astype(jnp.float32),
    )
    gated_out = gated_float.astype(jnp.bfloat16)
    middle = inputs_float + lax.psum(
        low_dot(gated_out, full_output).astype(jnp.bfloat16), "head"
    ).astype(jnp.float32)
    normed_middle, norm_two_back = jax.vjp(scale_norm, middle, gain_two.astype(jnp.float32))
    normed_two = normed_middle.astype(jnp.bfloat16)
    gate_lin = low_dot(normed_two, full_gate)
    up_lin = low_dot(normed_two, full_up)
    hidden_float, swiglu_back = jax.vjp(swiglu, gate_lin, up_lin)
    hidden = hidden_float.astype(jnp.bfloat16)
    feed_out = lax.psum(low_dot(hidden, full_down).astype(jnp.bfloat16), "head").astype(jnp.float32)
    block_out = (middle + feed_out).astype(jnp.bfloat16)
    regathered = (
        lax.all_gather(w_query, "seq", axis=0, tiled=True),
        lax.all_gather(w_key, "seq", axis=0, tiled=True),
        lax.all_gather(w_value, "seq", axis=0, tiled=True),
        lax.all_gather(w_beta, "seq", axis=0, tiled=True),
        lax.all_gather(w_gating, "seq", axis=0, tiled=True),
        lax.all_gather(w_output, "seq", axis=1, tiled=True),
        lax.all_gather(w_gate, "seq", axis=0, tiled=True),
        lax.all_gather(w_up, "seq", axis=0, tiled=True),
        lax.all_gather(w_down, "seq", axis=1, tiled=True),
    )
    (
        full_query,
        full_key,
        full_value,
        full_beta,
        full_gating,
        full_output,
        full_gate,
        full_up,
        full_down,
    ) = regathered
    cotangent_float = cotangent.astype(jnp.float32)
    grad_down = inner_dot(hidden, cotangent)
    d_hidden = rounded(outer_dot(cotangent, full_down))
    d_gate_float, d_up_float = swiglu_back(d_hidden)
    d_gate = d_gate_float.astype(jnp.bfloat16)
    d_up = d_up_float.astype(jnp.bfloat16)
    grad_gate = inner_dot(normed_two, d_gate)
    grad_up = inner_dot(normed_two, d_up)
    d_normed_two = lax.psum(
        (outer_dot(d_gate, full_gate) + outer_dot(d_up, full_up)).astype(jnp.bfloat16), "head"
    ).astype(jnp.float32)
    d_middle_norm, grad_gain_two = norm_two_back(d_normed_two)
    d_middle = cotangent_float + d_middle_norm
    d_middle_low = d_middle.astype(jnp.bfloat16)
    grad_output = inner_dot(gated_out, d_middle_low)
    d_gated = rounded(outer_dot(d_middle_low, full_output))
    d_mixer_out, d_gating_float, grad_head_part = gated_back(d_gated)
    d_gating = d_gating_float.reshape(tok_rows, value_width).astype(jnp.bfloat16)
    d_parts, d_query_late, d_start = emitted_back(to_blocks(d_mixer_out))
    chained = carried_in((jnp.swapaxes(device_map, 1, 2), d_start), "seq", compose_maps, identity)
    d_end = chained[1]
    d_map = high_einsum("hde,hfe->hdf", d_end, start_state)
    d_query_early, d_key_blocks, d_value_blocks, d_logit_blocks = terms_back(
        (d_parts, d_map, d_end)
    )
    d_query_unit = rounded(from_blocks(d_query_early + d_query_late))
    d_key_unit = rounded(from_blocks(d_key_blocks))
    d_value_act = rounded(from_blocks(d_value_blocks))
    d_beta_logit = (
        d_logit_blocks.transpose(0, 2, 1).reshape(tok_rows, head_count).astype(jnp.bfloat16)
    )
    d_extended, grad_conv_all = conv_back((d_query_unit, d_key_unit, d_value_act))
    returned = passed_along(d_extended[:edge_count].astype(jnp.bfloat16), "seq", -1).astype(
        jnp.float32
    )
    d_rows = d_extended[edge_count:]
    d_rows = jnp.concatenate(
        [
            d_rows[: tok_rows - edge_count],
            d_rows[tok_rows - edge_count :] + returned * sender_keep.astype(jnp.float32),
        ],
        axis=0,
    )
    d_joined = d_rows.astype(jnp.bfloat16)
    d_query_pre = d_joined[:, :key_width]
    d_key_pre = d_joined[:, key_width : 2 * key_width]
    d_value_pre = d_joined[:, 2 * key_width :]
    grad_query = inner_dot(normed_one, d_query_pre)
    grad_key = inner_dot(normed_one, d_key_pre)
    grad_value = inner_dot(normed_one, d_value_pre)
    grad_gating = inner_dot(normed_one, d_gating)
    grad_beta = inner_dot(normed_one, d_beta_logit)
    d_normed_part = (
        outer_dot(d_query_pre, full_query)
        + outer_dot(d_key_pre, full_key)
        + outer_dot(d_value_pre, full_value)
        + outer_dot(d_gating, full_gating)
        + outer_dot(d_beta_logit, full_beta)
    )
    d_normed_one, head_total = (
        lax.psum(d_normed_part.astype(jnp.bfloat16), "head").astype(jnp.float32),
        lax.psum(grad_head_part.astype(jnp.bfloat16), "head").astype(jnp.float32),
    )
    d_inputs_norm, grad_gain_one = norm_one_back(d_normed_one)
    grad_inputs = d_middle + d_inputs_norm
    small_totals = lax.psum((grad_conv_all, head_total), "seq")
    conv_total = small_totals[0]
    totals = (
        lax.psum_scatter(grad_gain_one, "seq", scatter_dimension=0, tiled=True),
        lax.psum_scatter(grad_query, "seq", scatter_dimension=0, tiled=True),
        lax.psum_scatter(grad_key, "seq", scatter_dimension=0, tiled=True),
        lax.psum_scatter(grad_value, "seq", scatter_dimension=0, tiled=True),
        lax.psum_scatter(grad_beta, "seq", scatter_dimension=0, tiled=True),
        lax.psum_scatter(grad_gating, "seq", scatter_dimension=0, tiled=True),
        lax.psum_scatter(grad_output, "seq", scatter_dimension=1, tiled=True),
        lax.psum_scatter(grad_gain_two, "seq", scatter_dimension=0, tiled=True),
        lax.psum_scatter(grad_gate, "seq", scatter_dimension=0, tiled=True),
        lax.psum_scatter(grad_up, "seq", scatter_dimension=0, tiled=True),
        lax.psum_scatter(grad_down, "seq", scatter_dimension=1, tiled=True),
    )
    return (
        block_out,
        grad_inputs,
        totals[0],
        totals[1],
        totals[2],
        totals[3],
        totals[4],
        totals[5],
        conv_total[:, :key_width],
        conv_total[:, key_width : 2 * key_width],
        conv_total[:, 2 * key_width :],
        small_totals[1],
        totals[6],
        totals[7],
        totals[8],
        totals[9],
        totals[10],
    )


def solution(mesh):
    in_specs = (
        P("seq", None),
        P("seq"),
        P("seq", "head"),
        P("seq"),
        P("seq", "head"),
        P("seq", "head"),
        P("seq", "head"),
        P("seq", "head"),
        P("seq", "head"),
        P(None, "head"),
        P(None, "head"),
        P(None, "head"),
        P(),
        P("head", "seq"),
        P("seq"),
        P("seq", "head"),
        P("seq", "head"),
        P("head", "seq"),
        P("seq", None),
    )
    out_specs = (
        P("seq", None),
        P("seq", None),
        P("seq"),
        P("seq", "head"),
        P("seq", "head"),
        P("seq", "head"),
        P("seq", "head"),
        P("seq", "head"),
        P(None, "head"),
        P(None, "head"),
        P(None, "head"),
        P(),
        P("head", "seq"),
        P("seq"),
        P("seq", "head"),
        P("seq", "head"),
        P("head", "seq"),
    )
    return jax.shard_map(
        per_device, mesh=mesh, in_specs=in_specs, out_specs=out_specs, check_vma=False
    )
```

profile of v0, /device:TPU:0, one launch (start us, length us, event | category | flops | bytes accessed | tf_op | source)
XLA Modules:
  0.0 4850.3 jit_solution(3770805132732038130)
XLA Ops:
  12.8 42.5 all-gather.4
  55.3 36.5 all_gather.70
  97.7 69.8 %all-gather.19.cloned.1.call-done = bf16[2048,1024]{1,0:T(8,128)(2,1)} async-done(((bf16[128,1024]{1,0:T(8,128)(2,1)}), bf16[2048,1024]{1,0:T(8,128)(2,1)}) %all-gather.19.cloned.1.call-update) | async-done | bytes 4194320 | tf_op jit(solution)/shard_map/all_gather | solution.py:137
  170.4 111.3 %all-gather.23.cloned.1.call-done = bf16[2048,2048]{1,0:T(8,128)(2,1)} async-done(((bf16[128,2048]{1,0:T(8,128)(2,1)}), bf16[2048,2048]{1,0:T(8,128)(2,1)}) %all-gather.23.cloned.1.call-update) | async-done | bytes 8388624 | tf_op jit(solution)/shard_map/all_gather | solution.py:139
  301.2 79.7 %custom-call.10 = f32[2,8,1,64,64]{3,4,2,1,0:T(8,128)S(1)} custom-call(f32[2,8,1,64,64]{4,3,2,1,0:T(8,128)} %get-tuple-element.1267), custom_call_target="InvertDiagBlocksLowerTriangular" | custom-call | tf_op jit(solution)/shard_map/jvp(jit(_solve_triangular))/vmap(vmap())/triangular_solve | solution.py:231
  389.5 11.3 while.113
  408.2 106.6 %all-gather.35.cloned.1.call-done = f32[128,128,128]{2,1,0:T(8,128)} async-done(((f32[8,128,128]{2,1,0:T(8,128)}), f32[128,128,128]{2,1,0:T(8,128)}) %all-gather.35.cloned.1.call-update) | async-done | bytes 8388624 | tf_op jit(solution)/shard_map/all_gather | solution.py:24
  514.8 193.0 %all-gather.37.cloned.1.call-done = f32[128,128,256]{2,1,0:T(8,128)} async-done(((f32[8,128,256]{2,1,0:T(8,128)}), f32[128,128,256]{2,1,0:T(8,128)}) %all-gather.37.cloned.1.call-update) | async-done | bytes 16777232 | tf_op jit(solution)/shard_map/all_gather | solution.py:24
  707.8 71.6 %while.114 = (s32[]{:T(128)}, f32[8,128,256]{2,1,0:T(8,128)}, s32[]{:T(128)}, f32[16,8,128,128]{3,2,1,0:T(8,128)}, f32[16,8,128,256]{3,2,1,0:T(8,128)}, /*index=5*/s32[]{:T(128)}, s32[]{:T(128)}) while((s32[]{:T(128)}, f32[8,128,256]{2,1,0:T(8,128)}, s32[]{:T(128)}, f32[16,8,128,128]{3,2,1,0:T(8,128)}, ...), condition=%wide.region_9.10_spmd.clone, body=%wide.region_8.9_spmd.clone.sunk | while | flops 403701760 | bytes 6818407 | solution.py:33
  784.1 14.0 while.110
  803.3 18.2 all-gather.25.cloned.1.call-done
  827.9 136.8 %all-gather.27.cloned.1.call-done = bf16[2048,2048]{1,0:T(8,128)(2,1)} async-done(((bf16[2048,128]{1,0:T(8,128)(2,1)}), bf16[2048,2048]{1,0:T(8,128)(2,1)}) %all-gather.27.cloned.1.call-update) | async-done | bytes 8388624 | tf_op jit(solution)/shard_map/all_gather | solution.py:142
  971.6 38.0 all-gather.5
  1009.6 138.7 %all-gather.33.cloned.1.call-done = bf16[2816,2048]{1,0:T(8,128)(2,1)} async-done(((bf16[2816,128]{1,0:T(8,128)(2,1)}), bf16[2816,2048]{1,0:T(8,128)(2,1)}) %all-gather.33.cloned.1.call-update) | async-done | bytes 11534352 | tf_op jit(solution)/shard_map/all_gather | solution.py:146
  1170.7 143.8 %all-gather.31.cloned.1.call-done = bf16[2048,2816]{1,0:T(8,128)(2,1)} async-done(((bf16[128,2816]{1,0:T(8,128)(2,1)}), bf16[2048,2816]{1,0:T(8,128)(2,1)}) %all-gather.31.cloned.1.call-update) | async-done | bytes 11534352 | tf_op jit(solution)/shard_map/all_gather | solution.py:145
  1321.6 136.5 %all-gather.29.cloned.1.call-done = bf16[2048,2816]{1,0:T(8,128)(2,1)} async-done(((bf16[128,2816]{1,0:T(8,128)(2,1)}), bf16[2048,2816]{1,0:T(8,128)(2,1)}) %all-gather.29.cloned.1.call-update) | async-done | bytes 11534352 | tf_op jit(solution)/shard_map/all_gather | solution.py:144
  1519.5 22.0 while.115
  1562.8 16.8 all-gather.39.cloned.1.call-done
  1579.6 114.7 %all-gather.41.cloned.1.call-done = bf16[128,128,256]{2,1,0:T(8,128)(2,1)} async-done(((bf16[8,128,256]{2,1,0:T(8,128)(2,1)}), bf16[128,128,256]{2,1,0:T(8,128)(2,1)}) %all-gather.41.cloned.1.call-update) | async-done | bytes 8388624 | tf_op jit(solution)/shard_map/all_gather | solution.py:41
  1694.4 28.5 while.111
  1727.4 14.7 while.112
  1829.9 11.0 fusion.243
  1874.7 19.0 all-reduce.29.cloned.1.call-done
  1895.2 77.1 %all-reduce.16 = (f32[2048]{0:T(1024)S(1)}, f32[256]{0:T(256)}, f32[2048]{0:T(1024)S(1)}) all-reduce(f32[2048]{0:T(1024)S(1)} %get-tuple-element.1121, bf16[256]{0:T(256)(128)(2,1)S(1)} %psum.54, f32[2048]{0:T(1024)S(1)} %copy-done.122), channel_id=6, replica_groups=mesh['seq'=16,'head'=2] {'seq'}, use_global_device_ids=true, to_apply=%region_34.35.clone | all-reduce | flops 4352 | bytes 34304
  1976.7 173.7 %reduce-scatter.10.cloned.1.call-done = f32[128,1024]{1,0:T(8,128)} async-done(((f32[2048,1024]{1,0:T(8,128)}), f32[128,1024]{1,0:T(8,128)}) %reduce-scatter.10.cloned.1.call-update) | async-done | bytes 524304 | tf_op jit(solution)/shard_map/reduce_scatter | solution.py:401
  2150.4 183.3 %reduce-scatter.12.cloned.1.call-done = f32[128,1024]{1,0:T(8,128)} async-done(((f32[2048,1024]{1,0:T(8,128)}), f32[128,1024]{1,0:T(8,128)}) %reduce-scatter.12.cloned.1.call-update) | async-done | bytes 524304 | tf_op jit(solution)/shard_map/reduce_scatter | solution.py:402
  2333.6 351.7 %reduce-scatter.18.cloned.1.call-done = f32[128,2048]{1,0:T(8,128)} async-done(((f32[2048,2048]{1,0:T(8,128)}), f32[128,2048]{1,0:T(8,128)}) %reduce-scatter.18.cloned.1.call-update) | async-done | bytes 1048592 | tf_op jit(solution)/shard_map/reduce_scatter | solution.py:405
  2685.3 355.0 %reduce-scatter.20.cloned.1.call-done = f32[2048,128]{1,0:T(8,128)} async-done(((f32[2048,2048]{1,0:T(8,128)}), f32[2048,128]{1,0:T(8,128)}) %reduce-scatter.20.cloned.1.call-update) | async-done | bytes 1048592 | tf_op jit(solution)/shard_map/reduce_scatter | solution.py:406
  3040.3 481.6 %reduce-scatter.22.cloned.1.call-done = f32[128,2816]{1,0:T(8,128)} async-done(((f32[2048,2816]{1,0:T(8,128)}), f32[128,2816]{1,0:T(8,128)}) %reduce-scatter.22.cloned.1.call-update) | async-done | bytes 1441808 | tf_op jit(solution)/shard_map/reduce_scatter | solution.py:408
  3521.9 482.8 %reduce-scatter.24.cloned.1.call-done = f32[128,2816]{1,0:T(8,128)} async-done(((f32[2048,2816]{1,0:T(8,128)}), f32[128,2816]{1,0:T(8,128)}) %reduce-scatter.24.cloned.1.call-update) | async-done | bytes 1441808 | tf_op jit(solution)/shard_map/reduce_scatter | solution.py:409
  4004.7 482.7 %reduce-scatter.26.cloned.1.call-done = f32[2816,128]{1,0:T(8,128)} async-done(((f32[2816,2048]{1,0:T(8,128)}), f32[2816,128]{1,0:T(8,128)}) %reduce-scatter.26.cloned.1.call-update) | async-done | bytes 1441808 | tf_op jit(solution)/shard_map/reduce_scatter | solution.py:410
  4487.4 356.2 %reduce-scatter.14.cloned.1.call-done = f32[128,2048]{1,0:T(8,128)} async-done(((f32[2048,2048]{1,0:T(8,128)}), f32[128,2048]{1,0:T(8,128)}) %reduce-scatter.14.cloned.1.call-update) | async-done | bytes 1048592 | tf_op jit(solution)/shard_map/reduce_scatter | solution.py:403
  (739 shorter events, 474.7 us)
Async XLA Ops:
  7.2 87.5 %all-gather.21.cloned.1.call-start = ((), (), s32[]{:S(2)}) async-start(), calls=%async_computation.10 | async-start | bytes 4456448 | tf_op jit(solution)/shard_map/all_gather | solution.py:138
  8.0 159.5 %all-gather.19.cloned.1.call-start = ((), (), s32[]{:S(2)}) async-start(), calls=%async_computation.9 | async-start | bytes 4456448 | tf_op jit(solution)/shard_map/all_gather | solution.py:137
  8.7 273.0 %all-gather.23.cloned.1.call-start = ((), (), s32[]{:S(2)}) async-start(), calls=%async_computation.11 | async-start | bytes 8912896 | tf_op jit(solution)/shard_map/all_gather | solution.py:139
  9.5 505.3 %all-gather.35.cloned.1.call-start = ((), (), s32[]{:S(2)}) async-start(), calls=%async_computation.29 | async-start | bytes 8912896 | tf_op jit(solution)/shard_map/all_gather | solution.py:24
  94.6 291.2 %copy-start.96 = (f32[2,8,64]{2,1,0:T(8,128)}, f32[2,8,64]{2,1,0:T(8,128)S(1)}, u32[]{:S(2)}) copy-start(f32[2,8,64]{2,1,0:T(8,128)S(1)} %fusion.229) | copy-start | bytes 12292
  286.5 4.8 collective-permute-start
  400.9 307.0 %copy-start.5 = (f32[2,8,128,128]{3,2,1,0:T(8,128)}, f32[2,8,128,128]{3,2,1,0:T(8,128)S(1)}, u32[]{:S(2)}) copy-start(f32[2,8,128,128]{3,2,1,0:T(8,128)S(1)} %get-tuple-element.1849) | copy-start | bytes 3145732
  401.7 306.1 %all-gather.37.cloned.1.call-start = ((), (), s32[]{:S(2)}) async-start(), calls=%async_computation.30 | async-start | bytes 17825792 | tf_op jit(solution)/shard_map/all_gather | solution.py:24
  402.3 419.2 %all-gather.25.cloned.1.call-start = ((), (), s32[]{:S(2)}) async-start(), calls=%async_computation.12 | async-start | bytes 8912896 | tf_op jit(solution)/shard_map/all_gather | solution.py:141
  402.8 561.9 %all-gather.27.cloned.1.call-start = ((), (), s32[]{:S(2)}) async-start(), calls=%async_computation.13 | async-start | bytes 8912896 | tf_op jit(solution)/shard_map/all_gather | solution.py:142
  403.6 744.7 %all-gather.33.cloned.1.call-start = ((), (), s32[]{:S(2)}) async-start(), calls=%async_computation.17 | async-start | bytes 12255232 | tf_op jit(solution)/shard_map/all_gather | solution.py:146
  404.3 763.8 %all-reduce.23.cloned.1.call-start = ((), (), s32[]{:S(2)}) async-start(), calls=%async_computation.14 | async-start | bytes 1048576 | tf_op jit(solution)/shard_map/psum | solution.py:299
  404.4 303.4 %copy-start.130 = (f32[256]{0:T(256)}, f32[256]{0:T(256)S(1)}, u32[]{:S(2)}) copy-start(f32[256]{0:T(256)S(1)} %convert_element_type.234) | copy-start | bytes 3076
  970.2 344.3 %all-gather.31.cloned.1.call-start = ((), (), s32[]{:S(2)}) async-start(), calls=%async_computation.16 | async-start | bytes 12255232 | tf_op jit(solution)/shard_map/all_gather | solution.py:145
  970.8 487.2 %all-gather.29.cloned.1.call-start = ((), (), s32[]{:S(2)}) async-start(), calls=%async_computation.15 | async-start | bytes 12255232 | tf_op jit(solution)/shard_map/all_gather | solution.py:144
  971.6 528.0 %all-reduce.25.cloned.1.call-start = ((), (), s32[]{:S(2)}) async-start(), calls=%async_computation.18 | async-start | bytes 1048576 | tf_op jit(solution)/shard_map/psum | solution.py:340
  1169.5 332.5 %copy-start.128 = (f32[128]{0:T(128)}, f32[128]{0:T(128)S(1)}, u32[]{:S(2)}) copy-start(f32[128]{0:T(128)S(1)} %fusion.219) | copy-start | bytes 1540
  1170.7 287.3 %copy-start.46 = (bf16[128,2048]{1,0:T(8,128)(2,1)}, bf16[128,2048]{1,0:T(8,128)(2,1)S(1)}, u32[]{:S(2)}) copy-start(bf16[128,2048]{1,0:T(8,128)(2,1)S(1)} %multiply_convert_fusion.1) | copy-start | bytes 1572868
  1482.4 97.2 %all-gather.39.cloned.1.call-start = ((), (), s32[]{:S(2)}) async-start(), calls=%async_computation.31 | async-start | bytes 4456448 | tf_op jit(solution)/shard_map/all_gather | solution.py:41
  1483.4 210.9 %all-gather.41.cloned.1.call-start = ((), (), s32[]{:S(2)}) async-start(), calls=%async_computation.32 | async-start | bytes 8912896 | tf_op jit(solution)/shard_map/all_gather | solution.py:41
  1542.4 329.6 %all-reduce.27.cloned.1.call-start = ((), (), s32[]{:S(2)}) async-start(), calls=%async_computation.24 | async-start | bytes 131072 | tf_op jit(solution)/shard_map/psum | solution.py:397
  1769.0 5.8 collective-permute-start.1
  1771.4 122.2 %all-reduce.29.cloned.1.call-start = ((), (), s32[]{:S(2)}) async-start(), calls=%async_computation.33 | async-start | bytes 2097152 | tf_op jit(solution)/shard_map/psum | solution.py:308
  1787.6 189.1 %reduce-scatter.16.cloned.1.call-start = ((), (), s32[]{:S(2)}) async-start(), calls=%async_computation.22 | async-start | bytes 69632 | tf_op jit(solution)/shard_map/reduce_scatter | solution.py:404
  1788.6 361.8 %reduce-scatter.10.cloned.1.call-start = ((), (), s32[]{:S(2)}) async-start(), calls=%async_computation.19 | async-start | bytes 8912896 | tf_op jit(solution)/shard_map/reduce_scatter | solution.py:401
  1793.2 540.4 %reduce-scatter.12.cloned.1.call-start = ((), (), s32[]{:S(2)}) async-start(), calls=%async_computation.20 | async-start | bytes 8912896 | tf_op jit(solution)/shard_map/reduce_scatter | solution.py:402
  1798.3 887.0 %reduce-scatter.18.cloned.1.call-start = ((), (), s32[]{:S(2)}) async-start(), calls=%async_computation.23 | async-start | bytes 17825792 | tf_op jit(solution)/shard_map/reduce_scatter | solution.py:405
  1807.6 1232.7 %reduce-scatter.20.cloned.1.call-start = ((), (), s32[]{:S(2)}) async-start(), calls=%async_computation.25 | async-start | bytes 17825792 | tf_op jit(solution)/shard_map/reduce_scatter | solution.py:406
  1818.3 1703.6 %reduce-scatter.22.cloned.1.call-start = ((), (), s32[]{:S(2)}) async-start(), calls=%async_computation.26 | async-start | bytes 24510464 | tf_op jit(solution)/shard_map/reduce_scatter | solution.py:408
  1829.8 2174.9 %reduce-scatter.24.cloned.1.call-start = ((), (), s32[]{:S(2)}) async-start(), calls=%async_computation.27 | async-start | bytes 24510464 | tf_op jit(solution)/shard_map/reduce_scatter | solution.py:409
  1841.0 2646.5 %reduce-scatter.26.cloned.1.call-start = ((), (), s32[]{:S(2)}) async-start(), calls=%async_computation.28 | async-start | bytes 24510464 | tf_op jit(solution)/shard_map/reduce_scatter | solution.py:410
  1851.4 2992.2 %reduce-scatter.14.cloned.1.call-start = ((), (), s32[]{:S(2)}) async-start(), calls=%async_computation.21 | async-start | bytes 17825792 | tf_op jit(solution)/shard_map/reduce_scatter | solution.py:403
  (182 other events, 3657.0 us)
Sparse Core Ops, SparseCore 0:
  10.8 79.0 all-gather.20
  92.7 74.6 all-gather.18
  170.2 111.4 all-gather.22
  401.8 112.9 all-gather.34
  518.0 189.7 all-gather.36
  710.4 111.0 all-gather.24
  824.2 140.5 all-gather.26
  967.5 180.7 all-gather.32
  1151.2 16.9 all-reduce.22
  1171.1 143.3 all-gather.30
  1317.6 140.3 all-gather.28
  1482.6 16.9 all-reduce.24
  1502.3 77.2 all-gather.38
  1582.8 111.4 all-gather.40
  1771.5 100.3 all-reduce.26
  1874.9 18.7 all-reduce.28
  1896.3 77.0 reduce-scatter.15
  1976.2 174.1 reduce-scatter.9
  2153.3 180.2 reduce-scatter.11
  2336.5 348.8 reduce-scatter.17
  2688.3 351.9 reduce-scatter.19
  3043.3 478.5 reduce-scatter.21
  3524.9 479.7 reduce-scatter.23
  4007.6 479.7 reduce-scatter.25
  4490.4 353.1 reduce-scatter.13
where the time goes:
time: 4860 us; the launch traced here: 4850 us
  waiting for transfers between devices  4110 us (85%)
  matrix products  310 us (6%)
  blocking collectives  196 us (4%)
  other arithmetic  117 us (2%)
  local copies, waits for them, and re-layouts  89.7 us (2%)
    reduce_scatter x1, waiting for transfers between devices, per_device(): lax.psum_scatter(grad_up, 'seq', scatter_dimension=0, tiled=True)  483 us
    reduce_scatter x1, waiting for transfers between devices, per_device(): lax.psum_scatter(grad_down, 'seq', scatter_dimension=1, tiled=True)  483 us
    reduce_scatter x1, waiting for transfers between devices, per_device(): lax.psum_scatter(grad_gate, 'seq', scatter_dimension=0, tiled=True)  482 us
    reduce_scatter x1, waiting for transfers between devices, per_device(): lax.psum_scatter(grad_value, 'seq', scatter_dimension=0, tiled=True)  356 us
    reduce_scatter x1, waiting for transfers between devices, per_device(): lax.psum_scatter(grad_output, 'seq', scatter_dimension=1, tiled=True)  355 us
    reduce_scatter x1, waiting for transfers between devices, per_device(): lax.psum_scatter(grad_gating, 'seq', scatter_dimension=0, tiled=True)  352 us
    all_gather x2, waiting for transfers between devices, entering(): pieces = jax.tree.map(lambda part: lax.all_gather(part, axis), value)  300 us
    reduce_scatter x1, waiting for transfers between devices, per_device(): lax.psum_scatter(grad_key, 'seq', scatter_dimension=0, tiled=True)  183 us
  transfers between devices with their start and end apart: 27, of which 25 were waited for; matrix products, arithmetic and copies ran while one was open for 6% of the time, Pallas kernels for 0%

commit v1 on v0

--- a/solution.py
+++ b/solution.py
@@ -2,15 +2,768 @@
 import jax.numpy as jnp
 from jax import lax
 from jax.sharding import PartitionSpec as P
+from jax.experimental import pallas as pl
+from jax.experimental.pallas import tpu as pltpu
 
 KEY_SIZE = 128
 DV = 256
 CONV = 4
 BLOCK = 64
+EPSILON = 1e-06
+F32 = jnp.float32
+BF16 = jnp.bfloat16
+LOGIT = 2 * KEY_SIZE + 2 * DV
+PACK = LOGIT + 128
+MIXED = 2 * KEY_SIZE + DV
+SCALE = KEY_SIZE**-0.5
+UNROLL = 4
+
+
+def mm(a, b, dims=((1,), (0,))):
+    return lax.dot_general(a, b, (dims, ((), ())), preferred_element_type=F32)
+
+
+NT = ((1,), (1,))
+TN = ((0,), (0,))
+
+
+def halves(a):
+    high = a.astype(BF16)
+    return high, (a - high.astype(F32)).astype(BF16)
+
+
+def mm_left(a, b, dims=((1,), (0,))):
+    high, low = halves(a)
+    return mm(high, b, dims) + mm(low, b, dims)
+
+
+def mm_right(a, b, dims=((1,), (0,))):
+    high, low = halves(b)
+    return mm(a, high, dims) + mm(a, low, dims)
+
+
+def mm_both(a, b, dims=((1,), (0,))):
+    a_high, a_low = halves(a)
+    b_high, b_low = halves(b)
+    return mm(a_high, b_high, dims) + (mm(a_high, b_low, dims) + mm(a_low, b_high, dims))
+
+
+def block_masks():
+    row = lax.broadcasted_iota(jnp.int32, (BLOCK, BLOCK), 0)
+    col = lax.broadcasted_iota(jnp.int32, (BLOCK, BLOCK), 1)
+    strict = row > col
+    levels = []
+    size = 1
+    while size < BLOCK:
+        levels.append(
+            (row // (2 * size) == col // (2 * size)) & (row // size % 2 == 1) & (col // size % 2 == 0)
+        )
+        size *= 2
+    return strict, levels, (row == col).astype(F32)
+
+
+def unit_lower_inverses(systems, levels, eye):
+    inverses = [eye - jnp.where(levels[0], system, 0.0) for system in systems]
+    for level in levels[1:]:
+        inner = [
+            mm_both(jnp.where(level, system, 0.0), inverse)
+            for system, inverse in zip(systems, inverses)
+        ]
+        inverses = [
+            inverse - mm_both(inverse, part) for inverse, part in zip(inverses, inner)
+        ]
+    return inverses
+
+
+def rows_of(index):
+    return pl.ds(pl.multiple_of(index * BLOCK, BLOCK), BLOCK)
+
+
+def row_sums(values):
+    return jnp.sum(values.reshape(values.shape[0] // 8, 8, values.shape[1]), axis=0)
+
+
+def beta_columns(packed):
+    logit = packed[:, :1].astype(F32) + packed[:, 1:2].astype(F32)
+    beta = jax.nn.sigmoid(logit)
+    return beta, jnp.broadcast_to(beta, (BLOCK, 128)).T[:BLOCK]
+
+
+def units_of(mixed):
+    gate = jax.nn.sigmoid(mixed)
+    act = mixed * gate
+    query, key = act[:, :KEY_SIZE], act[:, KEY_SIZE : 2 * KEY_SIZE]
+    query_scale = lax.rsqrt(jnp.sum(query * query, axis=-1, keepdims=True) + EPSILON)
+    key_scale = lax.rsqrt(jnp.sum(key * key, axis=-1, keepdims=True) + EPSILON)
+    return gate, act, query * query_scale, key * key_scale, query_scale, key_scale
+
+
+def forward_kernel(
+    place,
+    pre,
+    decay_grid,
+    cols,
+    rows,
+    taps,
+    head_gain,
+    gated,
+    mixer_out,
+    mixed_out,
+    inverse_out,
+    state_out,
+    fresh_out,
+    carry_out,
+    read_out,
+    both_maps,
+    value_part,
+    out_part,
+    add_part,
+):
+    blocks = decay_grid.shape[0]
+    strict, levels, eye = block_masks()
+    key_eye = (
+        lax.broadcasted_iota(jnp.int32, (KEY_SIZE, KEY_SIZE), 0)
+        == lax.broadcasted_iota(jnp.int32, (KEY_SIZE, KEY_SIZE), 1)
+    ).astype(F32)
+
+    def prepare(group, _):
+        work = []
+        for lane in range(UNROLL):
+            b = group * UNROLL + lane
+            here = rows_of(b)
+            source = place[b]
+            before = place[jnp.maximum(b - 1, 0)]
+            current = pre[rows_of(source), :MIXED].astype(F32)
+            edge = pre[
+                pl.ds(pl.multiple_of(before * BLOCK + BLOCK - 16, 16), 16), :MIXED
+            ].astype(F32)
+            extended = jnp.concatenate([edge[8:], current], axis=0)
+            mixed = taps[0:1] * current
+            for lag in range(1, CONV):
+                mixed = mixed + (taps[lag : lag + 1] * cols[here, 1 + lag : 2 + lag]) * pltpu.roll(
+                    extended, lag, 0
+                )[8:]
+            mixed_out[here, :] = mixed
+            _, act, query, key, _, _ = units_of(mixed)
+            query, key, value = query.astype(BF16), key.astype(BF16), act[:, 2 * KEY_SIZE :].astype(BF16)
+            beta, beta_row = beta_columns(pre[rows_of(source), LOGIT:])
+            link = decay_grid[b] * beta_row
+            system = jnp.where(strict, link * mm(key, key, NT), 0.0)
+            mixing = (SCALE * mm(query, key, NT)) * link
+            work.append((b, here, query, key, value, beta, system, mixing))
+        inverses = unit_lower_inverses([item[6] for item in work], levels, eye)
+        for (b, here, query, key, value, beta, system, mixing), inverse in zip(work, inverses):
+            inverse_out[here, :] = inverse
+            carry = cols[here, 0:1]
+            tail = cols[here, 1:2] * beta
+            fresh_values = mm_left(inverse, value)
+            fresh_keys = mm_left(inverse * rows[b, 0:1, :], key)
+            low_mixing = mixing.astype(BF16)
+            read = (SCALE * carry) * query.astype(F32) - mm(low_mixing, fresh_keys.astype(BF16))
+            value_part[here, :] = fresh_values
+            out_part[here, :] = mm(low_mixing, fresh_values.astype(BF16))
+            read_out[here, :] = read.astype(BF16)
+            both_maps[b, :BLOCK] = read.astype(BF16)
+            both_maps[b, BLOCK:] = fresh_keys.astype(BF16)
+            carry_end = carry[BLOCK - 1 : BLOCK]
+            carry_out[b] = carry_end * key_eye - mm_right(key, tail * fresh_keys, TN)
+            add_part[b] = mm_right(key, tail * fresh_values, TN)
+        return 0
+
+    lax.fori_loop(0, blocks // UNROLL, prepare, 0)
+
+    def chain(b, state):
+        state_out[b] = state.astype(BF16)
+        return mm_both(carry_out[b], state) + add_part[b]
+
+    lax.fori_loop(0, blocks, chain, jnp.zeros((KEY_SIZE, DV), F32))
+
+    def finish(group, _):
+        for lane in range(UNROLL):
+            b = group * UNROLL + lane
+            here = rows_of(b)
+            source = place[b]
+            both = mm(both_maps[b], state_out[b])
+            produced = both[:BLOCK] + out_part[here, :]
+            fresh_out[here, :] = (value_part[here, :] - both[BLOCK:]).astype(BF16)
+            mixer_out[here, :] = produced
+            scale = lax.rsqrt(jnp.mean(produced * produced, axis=-1, keepdims=True) + EPSILON)
+            gate = pre[rows_of(source), MIXED:LOGIT].astype(F32)
+            gated[rows_of(source), :] = (
+                produced * scale * head_gain[0:1] * (gate * jax.nn.sigmoid(gate))
+            ).astype(BF16)
+        return 0
+
+    lax.fori_loop(0, blocks // UNROLL, finish, 0)
+
+
+def backward_kernel(
+    place,
+    d_gated,
+    pre,
+    decay_grid,
+    cols,
+    taps,
+    head_gain,
+    mixer_out,
+    mixed_in,
+    inverse_in,
+    state_in,
+    fresh_in,
+    carry_in,
+    read_in,
+    d_pre,
+    grad_taps,
+    grad_gain,
+    d_out,
+    pull_part,
+    end_state,
+    d_mixed,
+):
+    blocks = decay_grid.shape[0]
+    strict, _, _ = block_masks()
+    lane_index = lax.broadcasted_iota(jnp.int32, (BLOCK, PACK - LOGIT), 1)
+    grad_taps[...] = jnp.zeros_like(grad_taps)
+    grad_gain[...] = jnp.zeros_like(grad_gain)
+    d_mixed[blocks * BLOCK :, :] = jnp.zeros((8, MIXED), F32)
+
+    def prepare(group, _):
+        for lane in range(UNROLL):
+            b = group * UNROLL + lane
+            here = rows_of(b)
+            there = rows_of(place[b])
+            grad = d_gated[there, :].astype(F32)
+            gate = pre[there, MIXED:LOGIT].astype(F32)
+            produced = mixer_out[here, :]
+            scale = lax.rsqrt(jnp.mean(produced * produced, axis=-1, keepdims=True) + EPSILON)
+            normed = produced * scale
+            sig = jax.nn.sigmoid(gate)
+            act = gate * sig
+            weighted = grad * head_gain[0:1]
+            pulled = weighted * act
+            along = jnp.mean(pulled * normed, axis=-1, keepdims=True)
+            low = (scale * (pulled - normed * along)).astype(BF16)
+            grad_gain[...] += row_sums(grad * normed * act)
+            d_pre[there, MIXED:LOGIT] = (
+                weighted * normed * (sig * (1.0 + gate * (1.0 - sig)))
+            ).astype(BF16)
+            d_out[here, :] = low
+            pull_part[b] = mm(read_in[here, :], low, TN)
+        return 0
+
+    lax.fori_loop(0, blocks // UNROLL, prepare, 0)
+
+    def chain(step, state):
+        b = blocks - 1 - step
+        end_state[b] = state.astype(BF16)
+        return mm_both(carry_in[b], state, TN) + pull_part[b]
+
+    lax.fori_loop(0, blocks, chain, jnp.zeros((KEY_SIZE, DV), F32))
+
+    def finish(group, _):
+        for lane in range(UNROLL):
+            b = group * UNROLL + lane
+            here = rows_of(b)
+            there = rows_of(place[b])
+            mixed = mixed_in[here, :]
+            gate, act, query_unit, key_unit, query_scale, key_scale = units_of(mixed)
+            query, key = query_unit.astype(BF16), key_unit.astype(BF16)
+            beta, beta_row = beta_columns(pre[there, LOGIT:])
+            link = decay_grid[b] * beta_row
+            mixing = (SCALE * mm(query, key, NT)) * link
+            carry = cols[here, 0:1]
+            tail = cols[here, 1:2] * beta
+            low = d_out[here, :]
+            end = end_state[b]
+            start = state_in[b]
+            fresh = fresh_in[here, :]
+            d_fresh = mm(mixing.astype(BF16), low, TN) + tail * mm(key, end)
+            d_right = mm_left(inverse_in[here, :], d_fresh.astype(BF16), TN)
+            d_right_low = d_right.astype(BF16)
+            d_logit = (1.0 - beta) * jnp.sum(fresh.astype(F32) * d_right, axis=-1, keepdims=True)
+            pair = jnp.concatenate([low, d_right_low], axis=0)
+            on_state = mm(pair, start, NT)
+            on_fresh = mm(pair, fresh, NT)
+            read_grad = (SCALE * on_fresh[:BLOCK]) * link
+            system_grad = jnp.where(strict, -on_fresh[BLOCK:] * link, 0.0)
+            d_query = (SCALE * carry) * on_state[:BLOCK] + mm(read_grad.astype(BF16), key)
+            d_key = (
+                mm((system_grad + system_grad.T).astype(BF16), key)
+                + mm(read_grad.astype(BF16), query, TN)
+                + tail * mm(fresh, end, NT)
+                - carry * on_state[BLOCK:]
+            )
+            d_query = d_query.astype(BF16).astype(F32)
+            d_key = d_key.astype(BF16).astype(F32)
+            slope = gate * (1.0 + mixed * (1.0 - gate))
+            d_mixed[here, :KEY_SIZE] = (
+                d_query - query_unit * jnp.sum(query_unit * d_query, axis=-1, keepdims=True)
+            ) * (query_scale * slope[:, :KEY_SIZE])
+            d_mixed[here, KEY_SIZE : 2 * KEY_SIZE] = (
+                d_key - key_unit * jnp.sum(key_unit * d_key, axis=-1, keepdims=True)
+            ) * (key_scale * slope[:, KEY_SIZE : 2 * KEY_SIZE])
+            d_mixed[here, 2 * KEY_SIZE :] = d_right_low.astype(F32) * slope[:, 2 * KEY_SIZE :]
+            d_pre[there, LOGIT:] = jnp.where(lane_index == 0, d_logit, 0.0).astype(BF16)
+        return 0
+
+    lax.fori_loop(0, blocks // UNROLL, finish, 0)
+
+    def unmix(group, _):
+        for lane in range(UNROLL):
+            b = group * UNROLL + lane
+            there = rows_of(place[b])
+            longer = pl.ds(pl.multiple_of(b * BLOCK, BLOCK), BLOCK + 8)
+            extended = d_mixed[longer, :]
+            current = pre[there, :MIXED].astype(F32)
+            total = taps[0:1] * extended[:BLOCK]
+            grad_taps[0] += row_sums(current * extended[:BLOCK])
+            for lag in range(1, CONV):
+                kept = cols[longer, 1 + lag : 2 + lag] * extended
+                moved = pltpu.roll(kept, BLOCK + 8 - lag, 0)[:BLOCK]
+                total = total + taps[lag : lag + 1] * moved
+                grad_taps[lag] += row_sums(current * moved)
+            d_pre[there, :MIXED] = total.astype(BF16)
+        return 0
+
+    lax.fori_loop(0, blocks // UNROLL, unmix, 0)
+
+
+VMEM_SPEC = pl.BlockSpec(memory_space=pltpu.VMEM)
+SMEM_SPEC = pl.BlockSpec(memory_space=pltpu.SMEM)
+
+
+def mixer_forward(place, pre, decay_grid, cols, rows, taps, head_gain):
+    tokens, blocks = pre.shape[0], decay_grid.shape[0]
+    shape = jax.ShapeDtypeStruct
+    return pl.pallas_call(
+        forward_kernel,
+        out_shape=(
+            shape((tokens, DV), BF16),
+            shape((tokens, DV), F32),
+            shape((tokens, MIXED), F32),
+            shape((tokens, BLOCK), F32),
+            shape((blocks, KEY_SIZE, DV), BF16),
+            shape((tokens, DV), BF16),
+            shape((blocks, KEY_SIZE, KEY_SIZE), F32),
+            shape((tokens, KEY_SIZE), BF16),
+        ),
+        in_specs=[SMEM_SPEC] + [VMEM_SPEC] * 6,
+        out_specs=[VMEM_SPEC] * 8,
+        scratch_shapes=[
+            pltpu.VMEM((blocks, 2 * BLOCK, KEY_SIZE), BF16),
+            pltpu.VMEM((tokens, DV), F32),
+            pltpu.VMEM((tokens, DV), F32),
+            pltpu.VMEM((blocks, KEY_SIZE, DV), F32),
+        ],
+        compiler_params=pltpu.CompilerParams(vmem_limit_bytes=52 * 1024 * 1024),
+        name="mixer_forward",
+    )(place, pre, decay_grid, cols, rows, taps, head_gain)
+
+
+def mixer_backward(place, d_gated, pre, decay_grid, cols, taps, head_gain, kept):
+    tokens, blocks = pre.shape[0], decay_grid.shape[0]
+    shape = jax.ShapeDtypeStruct
+    return pl.pallas_call(
+        backward_kernel,
+        out_shape=(
+            shape((tokens, PACK), BF16),
+            shape((CONV, 8, MIXED), F32),
+            shape((8, DV), F32),
+        ),
+        in_specs=[SMEM_SPEC] + [VMEM_SPEC] * 13,
+        out_specs=[VMEM_SPEC] * 3,
+        scratch_shapes=[
+            pltpu.VMEM((tokens, DV), BF16),
+            pltpu.VMEM((blocks, KEY_SIZE, DV), F32),
+            pltpu.VMEM((blocks, KEY_SIZE, DV), BF16),
+            pltpu.VMEM((tokens + 8, MIXED), F32),
+        ],
+        compiler_params=pltpu.CompilerParams(vmem_limit_bytes=52 * 1024 * 1024),
+        name="mixer_backward",
+    )(place, d_gated, pre, decay_grid, cols, taps, head_gain, *kept)
+
+
+def stream_tables(rate, starts):
+    blocks = rate.shape[0] // BLOCK
+    level = jnp.cumsum(jnp.log(rate).reshape(blocks, BLOCK), axis=-1)
+    segment = jnp.cumsum(starts.reshape(blocks, BLOCK), axis=-1)
+    positions = jnp.arange(BLOCK)
+    causal = positions[:, None] >= positions[None, :]
+    linked = (segment[:, :, None] == segment[:, None, :]) & causal
+    spread = jnp.where(causal, level[:, :, None] - level[:, None, :], 0.0)
+    decay_grid = jnp.where(linked, jnp.exp(spread), 0.0)
+    carry = jnp.where(segment == 0, jnp.exp(level), 0.0)
+    tail = decay_grid[:, BLOCK - 1, :]
+    keep = 1.0 - starts
+    padded = jnp.concatenate([jnp.zeros((2,), F32), keep])
+    keep_two = keep * padded[1:-1]
+    keep_three = keep_two * padded[:-2]
+    zero = jnp.zeros_like(keep)
+    cols = jnp.stack([carry.reshape(-1), tail.reshape(-1), keep, keep_two, keep_three, zero, zero, zero], axis=1)
+    cols = jnp.concatenate([cols, jnp.zeros((8, 8), F32)], axis=0)
+    rows = jnp.broadcast_to(carry[:, None, :], (blocks, 8, BLOCK))
+    return decay_grid, cols, rows
+
+
+CHIPS = 16
+CORES = 2
+MIXER_HEADS = 16
+BOTH = ("seq", "head")
+
+
+def along_x(index):
+    return index ^ 1
+
+
+def along_y(index):
+    return index ^ 2
+
+
+def along_z(steps):
+    return lambda index: (index + 4 * steps) % CHIPS
+
+
+def send(value, target):
+    return lax.ppermute(value, "seq", [(index, target(index)) for index in range(CHIPS)])
+
+
+def swap_cores(value):
+    return lax.ppermute(value, "head", [(0, 1), (1, 0)])
+
+
+def stacked(values):
+    return jnp.concatenate(values, axis=0)
+
+
+def total_of(*values):
+    total = values[0].astype(F32)
+    for value in values[1:]:
+        total = total + value.astype(F32)
+    return total
+
+
+def plane_gather(block):
+    half = block.shape[0] // 2
+    from_x, from_y = send(block, along_x), send(block, along_y)
+    far_low, far_high = send(from_y[:half], along_x), send(from_x[half:], along_y)
+    return [block, from_x, from_y, stacked([far_low, far_high])]
+
+
+def gather_rows(block):
+    levels = [block] + [send(block, along_z(steps)) for steps in (1, 2, 3)]
+    planes = [plane_gather(level) for level in levels]
+    return stacked([planes[j][p] for p in range(4) for j in range(4)])
+
+
+def plane_scatter(own, for_x, for_y, far):
+    half = own.shape[0] // 2
+    low, high = send(far[:half], along_x), send(far[half:], along_y)
+    for_y = stacked([total_of(for_y[:half], low).astype(BF16), for_y[half:]])
+    for_x = stacked([for_x[:half], total_of(for_x[half:], high).astype(BF16)])
+    return total_of(own, send(for_x, along_x), send(for_y, along_y))
+
+
+def scatter_rows(parts):
+    rows = parts.shape[0] // CHIPS
+    pieces = [[parts[(4 * p + j) * rows : (4 * p + j + 1) * rows] for p in range(4)] for j in range(4)]
+    arrived = []
+    for j in (1, 2, 3):
+        arrived.append(send(plane_scatter(*pieces[j]).astype(BF16), along_z(-j)))
+    return total_of(plane_scatter(*pieces[0]), *arrived)
+
+
+def head_routes(step):
+    return [
+        (
+            chip * CORES + core,
+            ((CHIPS // CORES) * core + (chip + step) % (CHIPS // CORES)) * CORES + chip // (CHIPS // CORES),
+        )
+        for chip in range(CHIPS)
+        for core in range(CORES)
+    ]
+
+
+def to_heads(pieces):
+    steps = CHIPS // CORES
+    chip = lax.axis_index("seq")
+    moved = [
+        lax.ppermute(
+            lax.dynamic_index_in_dim(pieces, (chip + step) % steps, 0, False), BOTH, head_routes(step)
+        )
+        for step in range(steps)
+    ]
+    order = jnp.stack(moved)
+    return jnp.take(order, (chip % steps - jnp.arange(steps)) % steps, axis=0)
+
+
+def from_heads(pieces):
+    steps = CHIPS // CORES
+    chip = lax.axis_index("seq")
+    moved = []
+    for step in range(steps):
+        back = [(target, source) for source, target in head_routes(step)]
+        moved.append(
+            lax.ppermute(
+                lax.dynamic_index_in_dim(pieces, (chip - step) % steps, 0, False), BOTH, back
+            )
+        )
+    order = jnp.stack(moved)
+    return jnp.take(order, (jnp.arange(steps) - chip) % steps, axis=0)
+
+
+def nn(a, b):
+    return mm(a, b)
+
+
+def nt(a, b):
+    return mm(a, b, NT)
+
+
+def tn(a, b):
+    return mm(a, b, TN)
+
+
+def head_plan(
+    inputs,
+    doc_starts,
+    decay_rate,
+    mixer_gain,
+    w_query,
+    w_key,
+    w_value,
+    w_beta,
+    w_gating,
+    conv_query,
+    conv_key,
+    conv_value,
+    head_gain,
+    w_output,
+    feed_gain,
+    w_gate,
+    w_up,
+    w_down,
+    cotangent,
+):
+    chip, core = lax.axis_index("seq"), lax.axis_index("head")
+    first = core == 0
+    tok_rows, width = inputs.shape
+    half_rows, half_width = tok_rows // CORES, width // CORES
+    row_count = w_query.shape[0]
+    head_count = w_query.shape[1] // KEY_SIZE
+    units = w_gate.shape[1] // CHIPS
+
+    def own_rows(values):
+        return lax.dynamic_slice_in_dim(values, core * half_rows, half_rows, 0)
+
+    def turned(values):
+        return jnp.where(
+            first,
+            values,
+            jnp.concatenate([values[:, half_width:], values[:, :half_width]], axis=1),
+        )
+
+    def both_rows(own):
+        other = swap_cores(own)
+        return stacked([jnp.where(first, own, other), jnp.where(first, other, own)])
+
+    gain_one = mixer_gain.astype(F32)[:, None]
+    gain_two = feed_gain.astype(F32)[:, None]
+
+    def by_head(weights, size):
+        return weights.reshape(row_count, head_count, size).transpose(1, 0, 2)
+
+    beta_pair = jnp.broadcast_to(w_beta.T[:, :, None], (head_count, row_count, 2))
+    packed_in = jnp.concatenate(
+        [
+            by_head(w_query, KEY_SIZE),
+            by_head(w_key, KEY_SIZE),
+            by_head(w_value, DV),
+            by_head(w_gating, DV),
+            beta_pair,
+            jnp.zeros((head_count, row_count, PACK - LOGIT - 2), BF16),
+        ],
+        axis=2,
+    )
+    packed_in = (packed_in.astype(F32) * gain_one).astype(BF16)
+    out_pieces = w_output.reshape(head_count, DV, row_count).transpose(0, 2, 1)
+
+    inputs_own = own_rows(inputs).astype(F32)
+    scale_one = lax.rsqrt(jnp.mean(inputs_own * inputs_own, axis=-1, keepdims=True) + EPSILON)
+    normed_own = (inputs_own * scale_one).astype(BF16)
+    normed_all = gather_rows(turned(normed_own))
+    mine_in = to_heads(packed_in).reshape(half_width, PACK)
+    weights_in = stacked([mine_in, swap_cores(mine_in)])
+
+    notes = stacked(
+        [decay_rate.T, doc_starts.astype(F32)[None], jnp.zeros((7, tok_rows), F32)]
+    )
+    notes = lax.all_gather(notes, BOTH, axis=0).reshape(CHIPS, CORES, 16, tok_rows)
+    rate = lax.dynamic_index_in_dim(
+        lax.dynamic_index_in_dim(notes, chip // head_count, 1, False), chip % head_count, 1, False
+    ).reshape(-1)
+    starts = notes[:, 0, 8].reshape(-1)
+    decay_grid, cols, rows = stream_tables(rate, starts)
+    taps_here = jnp.concatenate(
+        [
+            conv_query.reshape(CONV, head_count, KEY_SIZE),
+            conv_key.reshape(CONV, head_count, KEY_SIZE),
+            conv_value.reshape(CONV, head_count, DV),
+        ],
+        axis=2,
+    ).transpose(1, 0, 2)
+    taps_there = swap_cores(taps_here)
+    taps = lax.dynamic_index_in_dim(
+        jnp.where(chip // head_count == core, taps_here, taps_there), chip % head_count, 0, False
+    ).astype(F32)
+    taps = stacked([taps, jnp.zeros_like(taps)])
+    gain_head = jnp.broadcast_to(head_gain.astype(F32)[None], (8, DV))
+
+    blocks = jnp.arange(CHIPS * CORES)
+    far = blocks // CORES
+    place = (
+        4 * ((far ^ chip) % 4) + (chip // 4 - far // 4) % 4 + CHIPS * (blocks % CORES != core)
+    ).astype(jnp.int32)
+
+    feed = jnp.concatenate(
+        [
+            (w_gate.astype(F32) * gain_two).astype(BF16).T.reshape(CHIPS, units, row_count),
+            (w_up.astype(F32) * gain_two).astype(BF16).T.reshape(CHIPS, units, row_count),
+            w_down.reshape(CHIPS, units, row_count),
+        ],
+        axis=1,
+    )
+
+    raw = nn(normed_all, weights_in)
+    column = lax.broadcasted_iota(jnp.int32, raw.shape, 1)
+    pre_own = jnp.where(
+        column == LOGIT + 1,
+        raw - lax.reduce_precision(raw, exponent_bits=8, mantissa_bits=7),
+        raw,
+    ).astype(BF16)
+    pre = stacked([pre_own, swap_cores(pre_own)])
+    mine_out = to_heads(out_pieces).reshape(half_width, DV)
+    weights_out = stacked([mine_out, swap_cores(mine_out)])
+    feed_mine = lax.all_to_all(feed, "seq", split_axis=0, concat_axis=0, tiled=True)
+    feed_other = swap_cores(feed_mine)
+
+    def unit_rows(position):
+        return stacked(
+            [
+                part[:, position * units : (position + 1) * units].transpose(1, 0, 2).reshape(units, width)
+                for part in (feed_mine, feed_other)
+            ]
+        )
+
+    gate_rows, up_rows, down_rows = unit_rows(0), unit_rows(1), unit_rows(2)
+    cot_own = own_rows(cotangent)
+    cot_all = lax.all_gather(cot_own, "seq", axis=0, tiled=False)
+    relative = jnp.arange(CHIPS)
+    order = 4 * ((chip // 4 - relative % 4) % 4) + ((chip % 4) ^ (relative // 4))
+    cot_all = jnp.take(cot_all, order, axis=0).reshape(CHIPS * half_rows, width)
+    gated, *kept = mixer_forward(place, pre, decay_grid, cols, rows, taps, gain_head)
+    own_count = CHIPS * half_rows
+    mixed_sum = scatter_rows(nt(gated[:own_count], weights_out).astype(BF16))
+    middle = inputs_own + turned(mixed_sum)
+    scale_two = lax.rsqrt(jnp.mean(middle * middle, axis=-1, keepdims=True) + EPSILON)
+    normed_mid = middle * scale_two
+    mid_all = gather_rows(normed_mid.astype(BF16))
+
+    gate_lin = nt(mid_all, gate_rows)
+    up_lin = nt(mid_all, up_rows)
+    d_hidden = nt(cot_all, down_rows).astype(BF16).astype(F32)
+    sig = jax.nn.sigmoid(gate_lin)
+    act = gate_lin * sig
+    hidden = (act * up_lin).astype(BF16)
+    d_gate = (d_hidden * up_lin * (sig * (1.0 + gate_lin * (1.0 - sig)))).astype(BF16)
+    d_up = (d_hidden * act).astype(BF16)
+    e_two = scatter_rows((nn(d_gate, gate_rows) + nn(d_up, up_rows)).astype(BF16))
+    d_middle = cot_own.astype(F32) + scale_two * (
+        e_two - normed_mid * jnp.mean(e_two * normed_mid, axis=-1, keepdims=True)
+    )
+    d_mid_all = gather_rows(turned(d_middle.astype(BF16)))
+
+    d_gated_own = nn(d_mid_all, weights_out).astype(BF16)
+    d_gated = stacked([d_gated_own, swap_cores(d_gated_own)])
+    d_pre, grad_taps, grad_gain = mixer_backward(
+        place, d_gated, pre, decay_grid, cols, taps, gain_head, kept
+    )
+
+    feed_out = scatter_rows(nn(hidden, down_rows).astype(BF16))
+    block_out = both_rows((middle + feed_out).astype(BF16))
+    parts = [tn(d_gate, mid_all), tn(d_up, mid_all), tn(hidden, cot_all)]
+    keep_part = jnp.concatenate([part[:units] for part in parts], axis=0)
+    give_part = jnp.concatenate([part[units:] for part in parts], axis=0).astype(BF16)
+    feed_grad = (keep_part + swap_cores(give_part).astype(F32)).astype(BF16)
+    feed_grad = feed_grad.reshape(3 * units, CHIPS, row_count).transpose(1, 0, 2)
+    feed_back = lax.all_to_all(feed_grad, "seq", split_axis=0, concat_axis=0, tiled=True).astype(F32)
+    raw_gate = feed_back[:, :units].reshape(CHIPS * units, row_count).T
+    raw_up = feed_back[:, units : 2 * units].reshape(CHIPS * units, row_count).T
+    grad_down = feed_back[:, 2 * units :].reshape(CHIPS * units, row_count)
+    grad_gate, grad_up = raw_gate * gain_two, raw_up * gain_two
+    feed_gain_part = jnp.sum(
+        raw_gate * w_gate.astype(F32) + raw_up * w_up.astype(F32), axis=1
+    )
+
+    e_one = scatter_rows(nt(d_pre[:own_count], weights_in).astype(BF16))
+    e_one = turned(e_one)
+    normed_one = inputs_own * scale_one
+    grad_own = d_middle + scale_one * (
+        e_one - normed_one * jnp.mean(e_one * normed_one, axis=-1, keepdims=True)
+    )
+    grad_inputs = both_rows(grad_own)
+    normed_other = swap_cores(normed_all[:, half_width:])
+    grad_in = tn(normed_all[:, :half_width], d_pre[:own_count]) + tn(normed_other, d_pre[own_count:])
+    grad_in = from_heads(grad_in.astype(BF16).reshape(CHIPS // CORES, row_count, PACK))
+    d_mid_other = swap_cores(d_mid_all[:, half_width:])
+    grad_out = tn(d_mid_all[:, :half_width], gated[:own_count]) + tn(d_mid_other, gated[own_count:])
+    grad_out = from_heads(grad_out.astype(BF16).reshape(CHIPS // CORES, row_count, DV))
+    grad_output = grad_out.astype(F32).transpose(0, 2, 1).reshape(head_count * DV, row_count)
+
+    def by_rows(start, size):
+        part = grad_in[:, :, start : start + size].astype(F32)
+        return part.transpose(1, 0, 2).reshape(row_count, head_count * size)
+
+    raw_query = by_rows(0, KEY_SIZE)
+    raw_key = by_rows(KEY_SIZE, KEY_SIZE)
+    raw_value = by_rows(2 * KEY_SIZE, DV)
+    raw_gating = by_rows(MIXED, DV)
+    raw_beta = by_rows(LOGIT, 1)
+    mixer_gain_part = (
+        jnp.sum(raw_query * w_query.astype(F32), axis=1)
+        + jnp.sum(raw_key * w_key.astype(F32), axis=1)
+        + jnp.sum(raw_value * w_value.astype(F32), axis=1)
+        + jnp.sum(raw_gating * w_gating.astype(F32), axis=1)
+        + jnp.sum(raw_beta * w_beta.astype(F32), axis=1)
+    )
+    gain_parts = jnp.stack([mixer_gain_part, feed_gain_part])
+    gain_totals = gain_parts + swap_cores(gain_parts)
+
+    small = jnp.concatenate([jnp.sum(grad_taps, axis=1).reshape(-1), jnp.sum(grad_gain, axis=0)])
+    small = lax.all_gather(small.reshape(-1, 128), "seq", axis=0).reshape(CHIPS, -1)
+    taps_all = lax.dynamic_slice_in_dim(small[:, : CONV * MIXED], core * head_count, head_count, 0)
+    taps_all = taps_all.reshape(head_count, CONV, MIXED).transpose(1, 0, 2)
+    return (
+        block_out,
+        grad_inputs,
+        gain_totals[0],
+        raw_query * gain_one,
+        raw_key * gain_one,
+        raw_value * gain_one,
+        raw_beta * gain_one,
+        raw_gating * gain_one,
+        taps_all[:, :, :KEY_SIZE].reshape(CONV, head_count * KEY_SIZE),
+        taps_all[:, :, KEY_SIZE : 2 * KEY_SIZE].reshape(CONV, head_count * KEY_SIZE),
+        taps_all[:, :, 2 * KEY_SIZE :].reshape(CONV, head_count * DV),
+        jnp.sum(small[:, CONV * MIXED :], axis=0),
+        grad_output,
+        gain_totals[1],
+        grad_gate,
+        grad_up,
+        grad_down,
+    )
 
 
 EXACT_PRECISION = lax.Precision.HIGHEST
-EPSILON = 1e-06
 
 
 def passed_along(value, axis, steps):
@@ -105,7 +858,7 @@
     )
 
 
-def per_device(
+def gather_plan(
     inputs,
     doc_starts,
     decay_rate,
@@ -471,6 +1224,8 @@
         P("seq", "head"),
         P("head", "seq"),
     )
+    whole_heads = mesh.shape["seq"] == CHIPS and mesh.shape["head"] == CORES
+    per_device = head_plan if whole_heads else gather_plan
     return jax.shard_map(
         per_device, mesh=mesh, in_specs=in_specs, out_specs=out_specs, check_vma=False
     )

time: 4860 us -> 1050 us (0.22)
  waiting for transfers between devices: 4110 us -> 335 us
  matrix products: 310 us -> 47.3 us
  starting transfers between devices: 6.74 us -> 259 us
  Pallas kernels: 0 us -> 88 us
  blocking collectives: 196 us -> 119 us
  other arithmetic: 117 us -> 66.1 us
    reduce_scatter x9 -> x0, waiting for transfers between devices: 2870 us -> none  [the longest x1 483 us: per_device(): lax.psum_scatter(grad_up, 'seq', scatter_dimension=0, tiled=True)]
    all_gather x12 -> x1, waiting for transfers between devices: 1190 us -> 0.01 us  [head_plan(): cot_all = lax.all_gather(cot_own, 'seq', axis=0, tiled=False)]
    ppermute x2 -> x177, waiting for transfers between devices: 4.2 us -> 335 us  [the longest x133 253 us: send(): lax.ppermute(value, 'seq', [(index, target(index)) for index in range(CHI...]
    dot_general x107 -> x17, matrix products: 305 us -> 47.3 us  [mm(): return lax.dot_general(a, b, (dims, ((), ())), preferred_element_type=F32)]
    ppermute x2 -> x177, starting transfers between devices: 4.47 us -> 249 us  [the longest x133 176 us: send(): lax.ppermute(value, 'seq', [(index, target(index)) for index in range(CHI...]
    pallas_call x0 -> x2, Pallas kernels: none -> 88 us  [the longest x1 45.3 us: mixer_backward(): pl.pallas_call(backward_kernel, out_shape=(shape((tokens, PACK), BF16), s...]
    another operation x10 -> x4, other arithmetic: 84 us -> 0.46 us  [the longest x1 0.23 us: stream_tables(): segment = jnp.cumsum(starts.reshape(blocks, BLOCK), axis=-1)]
    unnamed x1 -> x0, blocking collectives: 77.1 us -> none
  transfers between devices with their start and end apart: 27 -> 180, of which waited for: 25 -> 81; matrix products, arithmetic and copies ran while one was open for 6% -> 16% of each run, Pallas kernels for 0% -> 8%
where the time goes in v1:
time: 1050 us; the launch traced here: 1040 us
  waiting for transfers between devices  335 us (32%)
  starting transfers between devices  259 us (25%)
  blocking collectives  119 us (11%)
  local copies, waits for them, and re-layouts  107 us (10%)
  Pallas kernels  88 us (8%)
  other arithmetic  66.1 us (6%)
  matrix products  47.3 us (5%)
  between operations  17.6 us (2%)
    ppermute x133, waiting for transfers between devices, send(): lax.ppermute(value, 'seq', [(index, target(index)) for index in range(CHI...  253 us
    ppermute x133, starting transfers between devices, send(): lax.ppermute(value, 'seq', [(index, target(index)) for index in range(CHI...  176 us
    all_gather x1, blocking collectives, head_plan(): lax.all_gather(notes, BOTH, axis=0).reshape(CHIPS, CORES, 16, tok_rows)  81 us
    unnamed x295, local copies, waits for them, and re-layouts  60.6 us
    dot_general x17, matrix products, mm(): return lax.dot_general(a, b, (dims, ((), ())), preferred_element_type=F32)  47.3 us
    pallas_call x1, Pallas kernels, mixer_backward(): pl.pallas_call(backward_kernel, out_shape=(shape((tokens, PACK), BF16), s...  45.3 us
    ppermute x16, waiting for transfers between devices, to_heads(): lax.ppermute(lax.dynamic_index_in_dim(pieces, (chip + step) % steps, 0, F...  43 us
    pallas_call x1, Pallas kernels, mixer_forward(): pl.pallas_call(forward_kernel, out_shape=(shape((tokens, DV), BF16), shap...  42.7 us
  transfers between devices with their start and end apart: 180, of which 81 were waited for; matrix products, arithmetic and copies ran while one was open for 16% of the time, Pallas kernels for 8%

profile of v1, /device:TPU:0, one launch (start us, length us, event | category | flops | bytes accessed | tf_op | source)
XLA Modules:
  0.0 1038.6 jit_solution(15535827376355088306)
XLA Ops:
  28.3 5.6 all-to-all-start
  35.9 81.0 %all-gather = f32[512,128]{1,0:T(8,128)S(1)} all-gather(f32[16,128]{1,0:T(8,128)S(1)} %maximum_maximum_fusion), channel_id=2, replica_groups=mesh['seq'=16,'head'=2] {'seq','head'}, dimensions={0}, use_global_device_ids=true | all-gather | bytes 270336 | tf_op jit(solution)/shard_map/all_gather | solution.py:600
  126.9 6.2 concatenate.179
  137.3 17.7 %collective-permute-start.1 = (bf16[64,2048]{1,0:T(8,128)(2,1)}, bf16[64,2048]{1,0:T(8,128)(2,1)S(1)}, u32[]{:S(2)}, u32[]{:S(2)}) collective-permute-start(bf16[64,2048]{1,0:T(8,128)(2,1)} %get-tuple-element.122), channel_id=1, source_target_pairs={{0,16},{2,18},{4,20},{6,22},{8,24},{10,26},{12,28},{14,30},{16,0},... | collective-permute-start | bytes 786440 | tf_op jit(solution)/shard_map/ppermute | solution.py:427
  164.4 9.5 collective-permute-done.21
  174.6 6.3 collective-permute-done.22
  191.0 5.9 collective-permute-done.24
  209.3 5.3 collective-permute-done.26
  220.0 19.1 %collective-permute-done = bf16[64,2048]{1,0:T(8,128)(2,1)} collective-permute-done((bf16[64,2048]{1,0:T(8,128)(2,1)}, bf16[64,2048]{1,0:T(8,128)(2,1)}, u32[]{:S(2)}, u32[]{:S(2)}) %collective-permute-start) | collective-permute-done | bytes 262176 | tf_op jit(solution)/shard_map/ppermute | solution.py:427
  268.0 5.8 collective-permute-done.8
  276.2 5.1 collective-permute-done.10
  325.0 8.2 fusion.1
  348.8 42.7 %mixer_forward.1 = (bf16[2048,256]{1,0:T(8,128)(2,1)S(1)}, f32[2048,256]{1,0:T(8,128)}, f32[2048,512]{1,0:T(8,128)}, f32[2048,64]{1,0:T(8,128)}, bf16[32,128,256...) custom-call(s32[32]{0:T(128)S(1)} %fusion.53.place, ...), custom_call_target="tpu_custom_call" | custom-call | tf_op jit(solution)/shard_map/mixer_forward/pallas_call | solution.py:338
  439.8 6.4 collective-permute-done.47
  450.4 7.3 collective-permute-done.52
  461.0 6.0 collective-permute-start.58
  470.9 8.5 collective-permute-done.59
  483.0 9.8 collective-permute-done.62
  501.3 5.2 collective-permute-done.66
  633.9 6.2 collective-permute-start.96
  647.4 15.6 %collective-permute-done.91 = bf16[64,2048]{1,0:T(8,128)(2,1)S(1)} collective-permute-done((bf16[64,2048]{1,0:T(8,128)(2,1)S(1)}, bf16[64,2048]{1,0:T(8,128)(2,1)S(1)}, u32[]{:S(2)}, u32[]{:S(2)}) %collective-permute-start.91) | collective-permute-done | bytes 262176 | tf_op jit(solution)/shard_map/ppermute | solution.py:427
  671.5 8.4 collective-permute-done.118
  720.6 45.3 %mixer_backward.1 = (bf16[2048,896]{1,0:T(8,128)(2,1)}, f32[4,8,512]{2,1,0:T(8,128)S(1)}, f32[8,256]{1,0:T(8,128)S(1)}) custom-call(s32[32]{0:T(128)S(1)} %fusion.53.place, bf16[2048,256]{1,0:T(8,128)(2,1)S(1)} %pad_maximum_fusion.9.d_gated, bf16[2048,896]{1,0:T(8,128)(2,1)} %pad_maximum_fusion.1.pre, f32[32,64,64]{2,1,0:T(8,128)} %copy-done.1, ...), custom_call_target="tpu_custom_call" | custom-call | tf_op jit(solution)/shard_map/mixer_backward/pallas_call | solution.py:366
  766.0 37.9 %all_gather.19 = f32[16,18,128]{2,1,0:T(8,128)S(1)} all-gather(f32[1,18,128]{2,1,0:T(8,128)S(1)} %maximum_bitcast_fusion.1), channel_id=1, replica_groups=mesh['seq'=16,'head'=2] {'seq'}, dimensions={0}, use_global_device_ids=true | all-gather | bytes 156672 | tf_op jit(solution)/shard_map/all_gather | solution.py:742
  811.3 6.1 convolution_convert_fusion.2
  848.7 5.9 collective-permute-done.160
  854.6 8.0 collective-permute-start.161
  862.7 8.2 collective-permute-done.161
  870.8 8.3 collective-permute-done.162
  919.8 10.6 %collective-permute-start.145 = (bf16[64,2048]{1,0:T(8,128)(2,1)}, bf16[64,2048]{1,0:T(8,128)(2,1)}, u32[]{:S(2)}, u32[]{:S(2)}) collective-permute-start(bf16[64,2048]{1,0:T(8,128)(2,1)} %get-tuple-element.147), channel_id=1, source_target_pairs={{0,24},{2,26},{4,28},{6,30},{8,0},{10,2},{12,4},{14,6},{16,8},{18,... | collective-permute-start | bytes 786440 | tf_op jit(solution)/shard_map/ppermute | solution.py:427
  943.2 31.0 %collective-permute-done.150 = bf16[64,2048]{1,0:T(8,128)(2,1)} collective-permute-done((bf16[64,2048]{1,0:T(8,128)(2,1)S(1)}, bf16[64,2048]{1,0:T(8,128)(2,1)}, u32[]{:S(2)}, u32[]{:S(2)}) %collective-permute-start.150) | collective-permute-done | bytes 262176 | tf_op jit(solution)/shard_map/ppermute | solution.py:427
  1012.9 12.0 %collective-permute-start.167 = (f32[2,128]{1,0:T(2,128)S(1)}, f32[2,128]{1,0:T(2,128)S(1)}, u32[]{:S(2)}, u32[]{:S(2)}) collective-permute-start(f32[2,128]{1,0:T(2,128)S(1)} %pad_maximum_fusion.46), channel_id=1, source_target_pairs={{0,1},{1,0},{2,3},{3,2},{4,5},{5,4},{6,7},{7,6},{8,9},{9,8},{10,11... | collective-permute-start | bytes 3080 | tf_op jit(solution)/shard_map/ppermute | solution.py:431
  (855 shorter events, 555.8 us)
Async XLA Ops:
  7.2 525.1 %all-gather.4.cloned.1.call-start = ((), (), s32[]{:S(2)}) async-start(), calls=%async_computation.2 | async-start | bytes 4456448 | tf_op jit(solution)/shard_map/all_gather | solution.py:659
  11.5 238.6 %collective-permute-start.7 = (bf16[64,2048]{1,0:T(8,128)(2,1)}, bf16[64,2048]{1,0:T(8,128)(2,1)}, u32[]{:S(2)}, u32[]{:S(2)}) collective-permute-start(bf16[64,2048]{1,0:T(8,128)(2,1)} %get-tuple-element.122), channel_id=1, source_target_pairs={{0,4},{2,6},{4,0},{6,2},{8,12},{10,14},{12,8},{14,10},{16,20},{18,... | collective-permute-start | bytes 786440 | tf_op jit(solution)/shard_map/ppermute | solution.py:427
  14.5 233.1 %collective-permute-start.3 = (bf16[64,2048]{1,0:T(8,128)(2,1)}, bf16[64,2048]{1,0:T(8,128)(2,1)}, u32[]{:S(2)}, u32[]{:S(2)}) collective-permute-start(bf16[64,2048]{1,0:T(8,128)(2,1)} %get-tuple-element.122), channel_id=1, source_target_pairs={{0,2},{2,0},{4,6},{6,4},{8,10},{10,8},{12,14},{14,12},{16,18},{18,... | collective-permute-start | bytes 786440 | tf_op jit(solution)/shard_map/ppermute | solution.py:427
  16.0 227.8 %collective-permute-start.2 = (bf16[64,2048]{1,0:T(8,128)(2,1)}, bf16[64,2048]{1,0:T(8,128)(2,1)}, u32[]{:S(2)}, u32[]{:S(2)}) collective-permute-start(bf16[64,2048]{1,0:T(8,128)(2,1)} %get-tuple-element.122), channel_id=1, source_target_pairs={{0,24},{2,26},{4,28},{6,30},{8,0},{10,2},{12,4},{14,6},{16,8},{18,... | collective-permute-start | bytes 786440 | tf_op jit(solution)/shard_map/ppermute | solution.py:427
  22.2 113.6 %collective-permute-start.30 = (bf16[128,256]{1,0:T(8,128)(2,1)}, bf16[128,256]{1,0:T(8,128)(2,1)}, u32[]{:S(2)}, u32[]{:S(2)}) collective-permute-start(bf16[128,256]{1,0:T(8,128)(2,1)} %bitcast.40), channel_id=1, source_target_pairs={{0,0},{1,16},{2,2},{3,18},{4,4},{5,20},{6,6},{7,22},{8,8},{9,24},{... | collective-permute-start | bytes 196616 | tf_op jit(solution)/shard_map/ppermute | solution.py:490
  25.1 112.3 %collective-permute-start.31 = (bf16[128,256]{1,0:T(8,128)(2,1)}, bf16[128,256]{1,0:T(8,128)(2,1)}, u32[]{:S(2)}, u32[]{:S(2)}) collective-permute-start(bf16[128,256]{1,0:T(8,128)(2,1)} %bitcast.43), channel_id=1, source_target_pairs={{0,2},{1,18},{2,4},{3,20},{4,6},{5,22},{6,8},{7,24},{8,10},{9,26},... | collective-permute-start | bytes 196616 | tf_op jit(solution)/shard_map/ppermute | solution.py:490
  28.3 395.8 %all-to-all-start = ((bf16[16,528,128]{2,1,0:T(8,128)(2,1)}), bf16[16,528,128]{2,1,0:T(8,128)(2,1)}, u32[]{:S(2)}, u32[]{:S(2)}) async-start(bf16[16,528,128]{2,1,0:T(8,128)(2,1)} %pad_maximum_fusion.4), calls=%async_computation | async-start | bytes 4325376 | tf_op jit(solution)/shard_map/all_to_all | solution.py:646
  137.3 104.7 %collective-permute-start.1 = (bf16[64,2048]{1,0:T(8,128)(2,1)}, bf16[64,2048]{1,0:T(8,128)(2,1)S(1)}, u32[]{:S(2)}, u32[]{:S(2)}) collective-permute-start(bf16[64,2048]{1,0:T(8,128)(2,1)} %get-tuple-element.122), channel_id=1, source_target_pairs={{0,16},{2,18},{4,20},{6,22},{8,24},{10,26},{12,28},{14,30},{16,0},... | collective-permute-start | bytes 786440 | tf_op jit(solution)/shard_map/ppermute | solution.py:427
  214.5 24.6 %collective-permute-start = (bf16[64,2048]{1,0:T(8,128)(2,1)}, bf16[64,2048]{1,0:T(8,128)(2,1)}, u32[]{:S(2)}, u32[]{:S(2)}) collective-permute-start(bf16[64,2048]{1,0:T(8,128)(2,1)} %get-tuple-element.122), channel_id=1, source_target_pairs={{0,8},{2,10},{4,12},{6,14},{8,16},{10,18},{12,20},{14,22},{16,24},... | collective-permute-start | bytes 786440 | tf_op jit(solution)/shard_map/ppermute | solution.py:427
  239.1 104.7 %collective-permute-start.29 = (bf16[8,4,512]{2,1,0:T(4,128)(2,1)}, bf16[8,4,512]{2,1,0:T(4,128)(2,1)S(1)}, u32[]{:S(2)}, u32[]{:S(2)}) collective-permute-start(bf16[8,4,512]{2,1,0:T(4,128)(2,1)} %maximum_bitcast_fusion), channel_id=1, source_target_pairs={{0,1},{1,0},{2,3},{3,2},{4,5},{5,4},{6,7},{7,6},{8,9},{9,8},{10,11... | collective-permute-start | bytes 98312 | tf_op jit(solution)/shard_map/ppermute | solution.py:431
  242.1 91.1 %collective-permute-start.32 = (bf16[128,256]{1,0:T(8,128)(2,1)}, bf16[128,256]{1,0:T(8,128)(2,1)S(1)}, u32[]{:S(2)}, u32[]{:S(2)}) collective-permute-start(bf16[128,256]{1,0:T(8,128)(2,1)} %bitcast.46), channel_id=1, source_target_pairs={{0,4},{1,20},{2,6},{3,22},{4,8},{5,24},{6,10},{7,26},{8,12},{9,28}... | collective-permute-start | bytes 196616 | tf_op jit(solution)/shard_map/ppermute | solution.py:490
  250.2 83.2 %collective-permute-start.33 = (bf16[128,256]{1,0:T(8,128)(2,1)S(1)}, bf16[128,256]{1,0:T(8,128)(2,1)S(1)}, u32[]{:S(2)}, u32[]{:S(2)}) collective-permute-start(bf16[128,256]{1,0:T(8,128)(2,1)S(1)} %bitcast.343), channel_id=1, source_target_pairs={{0,6},{1,22},{2,8},{3,24},{4,10},{5,26},{6,12},{7,28},{8,14},{9,30... | collective-permute-start | bytes 196616 | tf_op jit(solution)/shard_map/ppermute | solution.py:490
  275.5 47.9 %collective-permute-start.27 = (bf16[1024,896]{1,0:T(8,128)(2,1)S(1)}, bf16[1024,896]{1,0:T(8,128)(2,1)S(1)}, u32[]{:S(2)}, u32[]{:S(2)}) collective-permute-start(bf16[1024,896]{1,0:T(8,128)(2,1)S(1)} %bitcast.316), channel_id=1, source_target_pairs={{0,1},{1,0},{2,3},{3,2},{4,5},{5,4},{6,7},{7,6},{8,9},{9,8},{10,11... | collective-permute-start | bytes 5505032 | tf_op jit(solution)/shard_map/ppermute | solution.py:431
  340.6 51.0 %collective-permute-start.38 = (bf16[1024,256]{1,0:T(8,128)(2,1)S(1)}, bf16[1024,256]{1,0:T(8,128)(2,1)S(1)}, u32[]{:S(2)}, u32[]{:S(2)}) collective-permute-start(bf16[1024,256]{1,0:T(8,128)(2,1)S(1)} %bitcast.313), channel_id=1, source_target_pairs={{0,1},{1,0},{2,3},{3,2},{4,5},{5,4},{6,7},{7,6},{8,9},{9,8},{10,11... | collective-permute-start | bytes 1572872 | tf_op jit(solution)/shard_map/ppermute | solution.py:431
  439.7 85.8 %collective-permute-start.77 = (bf16[16,528,128]{2,1,0:T(8,128)(2,1)}, bf16[16,528,128]{2,1,0:T(8,128)(2,1)S(1)}, u32[]{:S(2)}, u32[]{:S(2)}) collective-permute-start(bf16[16,528,128]{2,1,0:T(8,128)(2,1)} %all-to-all-done), channel_id=1, source_target_pairs={{0,1},{1,0},{2,3},{3,2},{4,5},{5,4},{6,7},{7,6},{8,9},{9,8},{10,11... | collective-permute-start | bytes 6488072 | tf_op jit(solution)/shard_map/ppermute | solution.py:431
  479.4 29.6 %collective-permute-start.69 = (bf16[32,2048]{1,0:T(8,128)(2,1)S(1)}, bf16[32,2048]{1,0:T(8,128)(2,1)S(1)}, u32[]{:S(2)}, u32[]{:S(2)}) collective-permute-start(bf16[32,2048]{1,0:T(8,128)(2,1)S(1)} %slice.933), channel_id=1, source_target_pairs={{0,2},{2,0},{4,6},{6,4},{8,10},{10,8},{12,14},{14,12},{16,18},{18,... | collective-permute-start | bytes 393224 | tf_op jit(solution)/shard_map/ppermute | solution.py:427
  686.3 117.7 %collective-permute-start.157 = (bf16[1024,1024]{1,0:T(8,128)(2,1)}, bf16[1024,1024]{1,0:T(8,128)(2,1)}, u32[]{:S(2)}, u32[]{:S(2)}) collective-permute-start(bf16[1024,1024]{1,0:T(8,128)(2,1)} %slice.1044), channel_id=1, source_target_pairs={{0,1},{1,0},{2,3},{3,2},{4,5},{5,4},{6,7},{7,6},{8,9},{9,8},{10,11... | collective-permute-start | bytes 6291464 | tf_op jit(solution)/shard_map/ppermute | solution.py:431
  686.3 31.7 %collective-permute-start.97 = (bf16[64,2048]{1,0:T(8,128)(2,1)S(1)}, bf16[64,2048]{1,0:T(8,128)(2,1)S(1)}, u32[]{:S(2)}, u32[]{:S(2)}) collective-permute-start(bf16[64,2048]{1,0:T(8,128)(2,1)S(1)} %get-tuple-element.285), channel_id=1, source_target_pairs={{0,1},{1,0},{2,3},{3,2},{4,5},{5,4},{6,7},{7,6},{8,9},{9,8},{10,11... | collective-permute-start | bytes 786440 | tf_op jit(solution)/shard_map/ppermute | solution.py:431
  828.5 102.0 %collective-permute-start.166 = (bf16[528,2048]{1,0:T(8,128)(2,1)}, bf16[528,2048]{1,0:T(8,128)(2,1)}, u32[]{:S(2)}, u32[]{:S(2)}) collective-permute-start(bf16[528,2048]{1,0:T(8,128)(2,1)} %pad_maximum_fusion.5), channel_id=1, source_target_pairs={{0,1},{1,0},{2,3},{3,2},{4,5},{5,4},{6,7},{7,6},{8,9},{9,8},{10,11... | collective-permute-start | bytes 6488072 | tf_op jit(solution)/shard_map/ppermute | solution.py:431
  828.5 53.8 %collective-permute-start.165 = (bf16[128,896]{1,0:T(8,128)(2,1)S(1)}, bf16[128,896]{1,0:T(8,128)(2,1)S(1)}, u32[]{:S(2)}, u32[]{:S(2)}) collective-permute-start(bf16[128,896]{1,0:T(8,128)(2,1)S(1)} %get-tuple-element.246), channel_id=1, source_target_pairs={{14,0},{30,1},{0,2},{16,3},{2,4},{18,5},{4,6},{20,7},{6,8},{22,9},... | collective-permute-start | bytes 688136 | tf_op jit(solution)/shard_map/ppermute | solution.py:506
  829.4 52.7 %collective-permute-start.164 = (bf16[128,896]{1,0:T(8,128)(2,1)S(1)}, bf16[128,896]{1,0:T(8,128)(2,1)S(1)}, u32[]{:S(2)}, u32[]{:S(2)}) collective-permute-start(bf16[128,896]{1,0:T(8,128)(2,1)S(1)} %get-tuple-element.247), channel_id=1, source_target_pairs={{12,0},{28,1},{14,2},{30,3},{0,4},{16,5},{2,6},{18,7},{4,8},{20,9}... | collective-permute-start | bytes 688136 | tf_op jit(solution)/shard_map/ppermute | solution.py:506
  830.3 49.5 %collective-permute-start.163 = (bf16[128,896]{1,0:T(8,128)(2,1)S(1)}, bf16[128,896]{1,0:T(8,128)(2,1)S(1)}, u32[]{:S(2)}, u32[]{:S(2)}) collective-permute-start(bf16[128,896]{1,0:T(8,128)(2,1)S(1)} %get-tuple-element.248), channel_id=1, source_target_pairs={{10,0},{26,1},{12,2},{28,3},{14,4},{30,5},{0,6},{16,7},{2,8},{18,9... | collective-permute-start | bytes 688136 | tf_op jit(solution)/shard_map/ppermute | solution.py:506
  879.1 25.5 %collective-permute-start.142 = (bf16[64,2048]{1,0:T(8,128)(2,1)}, bf16[64,2048]{1,0:T(8,128)(2,1)}, u32[]{:S(2)}, u32[]{:S(2)}) collective-permute-start(bf16[64,2048]{1,0:T(8,128)(2,1)} %pad_maximum_fusion.40), channel_id=1, source_target_pairs={{0,2},{2,0},{4,6},{6,4},{8,10},{10,8},{12,14},{14,12},{16,18},{18,... | collective-permute-start | bytes 786440 | tf_op jit(solution)/shard_map/ppermute | solution.py:427
  879.9 25.7 %collective-permute-start.144 = (bf16[64,2048]{1,0:T(8,128)(2,1)}, bf16[64,2048]{1,0:T(8,128)(2,1)}, u32[]{:S(2)}, u32[]{:S(2)}) collective-permute-start(bf16[64,2048]{1,0:T(8,128)(2,1)} %pad_maximum_fusion.41), channel_id=1, source_target_pairs={{0,4},{2,6},{4,0},{6,2},{8,12},{10,14},{12,8},{14,10},{16,20},{18,... | collective-permute-start | bytes 786440 | tf_op jit(solution)/shard_map/ppermute | solution.py:427
  882.2 33.8 %collective-permute-start.147 = (bf16[64,2048]{1,0:T(8,128)(2,1)}, bf16[64,2048]{1,0:T(8,128)(2,1)}, u32[]{:S(2)}, u32[]{:S(2)}) collective-permute-start(bf16[64,2048]{1,0:T(8,128)(2,1)} %pad_maximum_fusion.42), channel_id=1, source_target_pairs={{0,2},{2,0},{4,6},{6,4},{8,10},{10,8},{12,14},{14,12},{16,18},{18,... | collective-permute-start | bytes 786440 | tf_op jit(solution)/shard_map/ppermute | solution.py:427
  882.3 33.7 %collective-permute-start.149 = (bf16[64,2048]{1,0:T(8,128)(2,1)}, bf16[64,2048]{1,0:T(8,128)(2,1)}, u32[]{:S(2)}, u32[]{:S(2)}) collective-permute-start(bf16[64,2048]{1,0:T(8,128)(2,1)} %pad_maximum_fusion.43), channel_id=1, source_target_pairs={{0,4},{2,6},{4,0},{6,2},{8,12},{10,14},{12,8},{14,10},{16,20},{18,... | collective-permute-start | bytes 786440 | tf_op jit(solution)/shard_map/ppermute | solution.py:427
  916.0 23.9 %collective-permute-start.140 = (bf16[64,2048]{1,0:T(8,128)(2,1)}, bf16[64,2048]{1,0:T(8,128)(2,1)}, u32[]{:S(2)}, u32[]{:S(2)}) collective-permute-start(bf16[64,2048]{1,0:T(8,128)(2,1)} %pad_maximum_fusion.39), channel_id=1, source_target_pairs={{0,4},{2,6},{4,0},{6,2},{8,12},{10,14},{12,8},{14,10},{16,20},{18,... | collective-permute-start | bytes 786440 | tf_op jit(solution)/shard_map/ppermute | solution.py:427
  916.0 23.9 %collective-permute-start.138 = (bf16[64,2048]{1,0:T(8,128)(2,1)}, bf16[64,2048]{1,0:T(8,128)(2,1)}, u32[]{:S(2)}, u32[]{:S(2)}) collective-permute-start(bf16[64,2048]{1,0:T(8,128)(2,1)} %pad_maximum_fusion.38), channel_id=1, source_target_pairs={{0,2},{2,0},{4,6},{6,4},{8,10},{10,8},{12,14},{14,12},{16,18},{18,... | collective-permute-start | bytes 786440 | tf_op jit(solution)/shard_map/ppermute | solution.py:427
  930.5 43.8 %collective-permute-start.150 = (bf16[64,2048]{1,0:T(8,128)(2,1)S(1)}, bf16[64,2048]{1,0:T(8,128)(2,1)}, u32[]{:S(2)}, u32[]{:S(2)}) collective-permute-start(bf16[64,2048]{1,0:T(8,128)(2,1)S(1)} %get-tuple-element.149), channel_id=1, source_target_pairs={{0,16},{2,18},{4,20},{6,22},{8,24},{10,26},{12,28},{14,30},{16,0},... | collective-permute-start | bytes 786440 | tf_op jit(solution)/shard_map/ppermute | solution.py:427
  935.3 74.5 %all-to-all-start.1 = ((bf16[16,528,128]{2,1,0:T(8,128)(2,1)}), bf16[16,528,128]{2,1,0:T(8,128)(2,1)S(1)}, u32[]{:S(2)}, u32[]{:S(2)}) async-start(bf16[16,528,128]{2,1,0:T(8,128)(2,1)} %bitcast_bitcast_fusion), calls=%async_computation.1 | async-start | bytes 4325376 | tf_op jit(solution)/shard_map/all_to_all | solution.py:698
  939.9 39.6 %collective-permute-start.168 = (bf16[1024,1024]{1,0:T(8,128)(2,1)}, bf16[1024,1024]{1,0:T(8,128)(2,1)S(1)}, u32[]{:S(2)}, u32[]{:S(2)}) collective-permute-start(bf16[1024,1024]{1,0:T(8,128)(2,1)} %slice.1064), channel_id=1, source_target_pairs={{0,1},{1,0},{2,3},{3,2},{4,5},{5,4},{6,7},{7,6},{8,9},{9,8},{10,11... | collective-permute-start | bytes 6291464 | tf_op jit(solution)/shard_map/ppermute | solution.py:431
  983.9 24.5 %collective-permute-start.176 = (bf16[128,256]{1,0:T(8,128)(2,1)S(1)}, bf16[128,256]{1,0:T(8,128)(2,1)S(1)}, u32[]{:S(2)}, u32[]{:S(2)}) collective-permute-start(bf16[128,256]{1,0:T(8,128)(2,1)S(1)} %get-tuple-element.271), channel_id=1, source_target_pairs={{14,0},{30,1},{0,2},{16,3},{2,4},{18,5},{4,6},{20,7},{6,8},{22,9},... | collective-permute-start | bytes 196616 | tf_op jit(solution)/shard_map/ppermute | solution.py:506
  (242 other events, 3167.4 us)
Sparse Core Ops, SparseCore 0:
  21.4 101.2 all-gather.3

commit v2 on v1

--- a/solution.py
+++ b/solution.py
@@ -100,13 +100,15 @@
 
 def forward_kernel(
     place,
-    pre,
+    pre_own,
+    pre_other,
     decay_grid,
     cols,
     rows,
     taps,
     head_gain,
-    gated,
+    gated_own,
+    gated_other,
     mixer_out,
     mixed_out,
     inverse_out,
@@ -118,8 +120,13 @@
     value_part,
     out_part,
     add_part,
+    pre,
+    gated,
 ):
     blocks = decay_grid.shape[0]
+    half = pre_own.shape[0]
+    pre[:half] = pre_own[...]
+    pre[half:] = pre_other[...]
     strict, levels, eye = block_masks()
     key_eye = (
         lax.broadcasted_iota(jnp.int32, (KEY_SIZE, KEY_SIZE), 0)
@@ -195,12 +202,16 @@
         return 0
 
     lax.fori_loop(0, blocks // UNROLL, finish, 0)
+    gated_own[...] = gated[:half]
+    gated_other[...] = gated[half:]
 
 
 def backward_kernel(
     place,
-    d_gated,
-    pre,
+    d_gated_own,
+    d_gated_other,
+    pre_own,
+    pre_other,
     decay_grid,
     cols,
     taps,
@@ -212,15 +223,24 @@
     fresh_in,
     carry_in,
     read_in,
-    d_pre,
+    d_pre_own,
+    d_pre_other,
     grad_taps,
     grad_gain,
     d_out,
     pull_part,
     end_state,
     d_mixed,
+    d_gated,
+    pre,
+    d_pre,
 ):
     blocks = decay_grid.shape[0]
+    half = pre_own.shape[0]
+    pre[:half] = pre_own[...]
+    pre[half:] = pre_other[...]
+    d_gated[:half] = d_gated_own[...]
+    d_gated[half:] = d_gated_other[...]
     strict, _, _ = block_masks()
     lane_index = lax.broadcasted_iota(jnp.int32, (BLOCK, PACK - LOGIT), 1)
     grad_taps[...] = jnp.zeros_like(grad_taps)
@@ -326,19 +346,24 @@
         return 0
 
     lax.fori_loop(0, blocks // UNROLL, unmix, 0)
+    d_pre_own[...] = d_pre[:half]
+    d_pre_other[...] = d_pre[half:]
 
 
 VMEM_SPEC = pl.BlockSpec(memory_space=pltpu.VMEM)
 SMEM_SPEC = pl.BlockSpec(memory_space=pltpu.SMEM)
-
-
-def mixer_forward(place, pre, decay_grid, cols, rows, taps, head_gain):
-    tokens, blocks = pre.shape[0], decay_grid.shape[0]
+KERNEL_COST = pl.CostEstimate(flops=30_000_000_000, bytes_accessed=100_000_000, transcendentals=0)
+
+
+def mixer_forward(place, pre_own, pre_other, decay_grid, cols, rows, taps, head_gain):
+    blocks = decay_grid.shape[0]
+    half, tokens = pre_own.shape[0], blocks * BLOCK
     shape = jax.ShapeDtypeStruct
     return pl.pallas_call(
         forward_kernel,
         out_shape=(
-            shape((tokens, DV), BF16),
+            shape((half, DV), BF16),
+            shape((half, DV), BF16),
             shape((tokens, DV), F32),
             shape((tokens, MIXED), F32),
             shape((tokens, BLOCK), F32),
@@ -347,40 +372,49 @@
             shape((blocks, KEY_SIZE, KEY_SIZE), F32),
             shape((tokens, KEY_SIZE), BF16),
         ),
-        in_specs=[SMEM_SPEC] + [VMEM_SPEC] * 6,
-        out_specs=[VMEM_SPEC] * 8,
+        in_specs=[SMEM_SPEC] + [VMEM_SPEC] * 7,
+        out_specs=[VMEM_SPEC] * 9,
         scratch_shapes=[
             pltpu.VMEM((blocks, 2 * BLOCK, KEY_SIZE), BF16),
             pltpu.VMEM((tokens, DV), F32),
             pltpu.VMEM((tokens, DV), F32),
             pltpu.VMEM((blocks, KEY_SIZE, DV), F32),
+            pltpu.VMEM((tokens, PACK), BF16),
+            pltpu.VMEM((tokens, DV), BF16),
         ],
         compiler_params=pltpu.CompilerParams(vmem_limit_bytes=52 * 1024 * 1024),
+        cost_estimate=KERNEL_COST,
         name="mixer_forward",
-    )(place, pre, decay_grid, cols, rows, taps, head_gain)
+    )(place, pre_own, pre_other, decay_grid, cols, rows, taps, head_gain)
 
 
 def mixer_backward(place, d_gated, pre, decay_grid, cols, taps, head_gain, kept):
-    tokens, blocks = pre.shape[0], decay_grid.shape[0]
+    blocks = decay_grid.shape[0]
+    half, tokens = pre[0].shape[0], blocks * BLOCK
     shape = jax.ShapeDtypeStruct
     return pl.pallas_call(
         backward_kernel,
         out_shape=(
-            shape((tokens, PACK), BF16),
+            shape((half, PACK), BF16),
+            shape((half, PACK), BF16),
             shape((CONV, 8, MIXED), F32),
             shape((8, DV), F32),
         ),
-        in_specs=[SMEM_SPEC] + [VMEM_SPEC] * 13,
-        out_specs=[VMEM_SPEC] * 3,
+        in_specs=[SMEM_SPEC] + [VMEM_SPEC] * 15,
+        out_specs=[VMEM_SPEC] * 4,
         scratch_shapes=[
             pltpu.VMEM((tokens, DV), BF16),
             pltpu.VMEM((blocks, KEY_SIZE, DV), F32),
             pltpu.VMEM((blocks, KEY_SIZE, DV), BF16),
             pltpu.VMEM((tokens + 8, MIXED), F32),
+            pltpu.VMEM((tokens, DV), BF16),
+            pltpu.VMEM((tokens, PACK), BF16),
+            pltpu.VMEM((tokens, PACK), BF16),
         ],
         compiler_params=pltpu.CompilerParams(vmem_limit_bytes=52 * 1024 * 1024),
+        cost_estimate=KERNEL_COST,
         name="mixer_backward",
-    )(place, d_gated, pre, decay_grid, cols, taps, head_gain, *kept)
+    )(place, *d_gated, *pre, decay_grid, cols, taps, head_gain, *kept)
 
 
 def stream_tables(rate, starts):
@@ -405,9 +439,113 @@
     return decay_grid, cols, rows
 
 
+def unpack_kernel(
+    grads, gain, w_query, w_key, w_value, w_gating, w_beta, query, key, value, gating, beta, gain_part
+):
+    heads = grads.shape[0]
+    scale = gain[...]
+    total = jnp.zeros((grads.shape[1], 128), F32)
+
+    def lane_sums(values):
+        part = values[:, :128]
+        for start in range(128, values.shape[1], 128):
+            part = part + values[:, start : start + 128]
+        return part
+
+    columns = []
+    for head in range(heads):
+        start = 0
+        for out, weights, size in (
+            (query, w_query, KEY_SIZE),
+            (key, w_key, KEY_SIZE),
+            (value, w_value, DV),
+            (gating, w_gating, DV),
+        ):
+            place = slice(head * size, (head + 1) * size)
+            part = grads[head, :, start : start + size].astype(F32)
+            out[:, place] = part * scale
+            total = total + lane_sums(part * weights[:, place].astype(F32))
+            start += size
+        columns.append(grads[head, :, LOGIT : LOGIT + 1].astype(F32))
+    columns = jnp.concatenate(columns, axis=1)
+    beta[...] = columns * scale
+    gain_part[...] = jnp.sum(total, axis=1, keepdims=True) + jnp.sum(
+        columns * w_beta[...].astype(F32), axis=1, keepdims=True
+    )
+
+
+def unpack_heads(grads, gain, w_query, w_key, w_value, w_gating, w_beta):
+    shape = jax.ShapeDtypeStruct
+    weights = (w_query, w_key, w_value, w_gating, w_beta)
+    query, key, value, gating, beta, gain_part = pl.pallas_call(
+        unpack_kernel,
+        out_shape=tuple(shape(w.shape, F32) for w in weights) + (shape((gain.shape[0], 1), F32),),
+        in_specs=[VMEM_SPEC] * 7,
+        out_specs=[VMEM_SPEC] * 6,
+        compiler_params=pltpu.CompilerParams(vmem_limit_bytes=32 * 1024 * 1024),
+        name="unpack_heads",
+    )(grads, gain, *weights)
+    return query, key, value, gating, beta, gain_part[:, 0]
+
+
+def pack_kernel(
+    core, gain, w_query, w_key, w_value, w_gating, w_beta, w_output, rates, starts, kept, given
+):
+    heads = kept.shape[0]
+    half = kept.shape[1]
+    first = core[0] == 0
+    scale = gain[...]
+    lanes = lax.broadcasted_iota(jnp.int32, (2 * half, 128), 1)
+    blank = jnp.zeros((half - 8, 128), F32)
+
+    def two_rows(values):
+        right = lanes[: values.shape[0]] >= half
+        return jnp.where(right, pltpu.roll(values, half, 1), 0.0), jnp.where(right, values, 0.0)
+
+    rate = rates[...]
+    high = rate.astype(BF16).astype(F32)
+    middle = (rate - high).astype(BF16).astype(F32)
+    notes = [*two_rows(high), *two_rows(middle), *two_rows(rate - high - middle)]
+    start_rows = two_rows(jnp.broadcast_to(starts[...], (8, 2 * half)))
+
+    def place(head, columns, values):
+        low, high = values[:half], values[half:]
+        kept[head, :, columns] = jnp.where(first, low, high).astype(BF16)
+        given[head, :, columns] = jnp.where(first, high, low).astype(BF16)
+
+    for head in range(heads):
+        start = 0
+        for weights, size in ((w_query, KEY_SIZE), (w_key, KEY_SIZE), (w_value, DV), (w_gating, DV)):
+            part = weights[:, head * size : (head + 1) * size].astype(F32) * scale
+            place(head, slice(start, start + size), part)
+            start += size
+        beta = w_beta[:, head : head + 1].astype(F32) * scale
+        place(
+            head, slice(PACK, PACK + DV), w_output[head * DV : (head + 1) * DV, :].astype(F32).T
+        )
+        note = [part[head : head + 1] for part in notes] + [part[:1] for part in start_rows]
+        note = jnp.concatenate(note + [blank], axis=0)
+        place(
+            head, slice(LOGIT, PACK), jnp.where(lanes < 2, beta, 0.0) + jnp.concatenate([note, note], axis=0)
+        )
+
+
+def pack_heads(core, gain, w_query, w_key, w_value, w_gating, w_beta, w_output, rates, starts):
+    rows = gain.shape[0]
+    heads = w_query.shape[1] // KEY_SIZE
+    shape = jax.ShapeDtypeStruct((heads, rows // 2, PACK + DV), BF16)
+    return pl.pallas_call(
+        pack_kernel,
+        out_shape=(shape, shape),
+        in_specs=[SMEM_SPEC] + [VMEM_SPEC] * 9,
+        out_specs=[VMEM_SPEC] * 2,
+        compiler_params=pltpu.CompilerParams(vmem_limit_bytes=32 * 1024 * 1024),
+        name="pack_heads",
+    )(core, gain, w_query, w_key, w_value, w_gating, w_beta, w_output, rates, starts)
+
+
 CHIPS = 16
 CORES = 2
-MIXER_HEADS = 16
 BOTH = ("seq", "head")
 
 
@@ -429,6 +567,14 @@
 
 def swap_cores(value):
     return lax.ppermute(value, "head", [(0, 1), (1, 0)])
+
+
+def exchange(pieces):
+    return lax.all_to_all(pieces, "seq", split_axis=0, concat_axis=0, tiled=True)
+
+
+def after(values, *earlier):
+    return lax.optimization_barrier((values, earlier))[0]
 
 
 def stacked(values):
@@ -442,73 +588,58 @@
     return total
 
 
-def plane_gather(block):
-    half = block.shape[0] // 2
-    from_x, from_y = send(block, along_x), send(block, along_y)
-    far_low, far_high = send(from_y[:half], along_x), send(from_x[half:], along_y)
-    return [block, from_x, from_y, stacked([far_low, far_high])]
-
-
-def gather_rows(block):
-    levels = [block] + [send(block, along_z(steps)) for steps in (1, 2, 3)]
-    planes = [plane_gather(level) for level in levels]
-    return stacked([planes[j][p] for p in range(4) for j in range(4)])
-
-
-def plane_scatter(own, for_x, for_y, far):
-    half = own.shape[0] // 2
-    low, high = send(far[:half], along_x), send(far[half:], along_y)
-    for_y = stacked([total_of(for_y[:half], low).astype(BF16), for_y[half:]])
-    for_x = stacked([for_x[:half], total_of(for_x[half:], high).astype(BF16)])
-    return total_of(own, send(for_x, along_x), send(for_y, along_y))
-
-
-def scatter_rows(parts):
+def gather_levels(block):
+    return [block] + [send(block, along_z(steps)) for steps in (1, 2, 3)]
+
+
+def gather_near(levels):
+    blocks = [levels[0], stacked(levels[1:])]
+    return [(block, send(block, along_x), send(block, along_y)) for block in blocks]
+
+
+def gather_far(near):
+    own, others = [
+        (
+            [block],
+            [from_x],
+            [from_y],
+            [
+                send(from_y[: block.shape[0] // 2], along_x),
+                send(from_x[block.shape[0] // 2 :], along_y),
+            ],
+        )
+        for block, from_x, from_y in near
+    ]
+    return stacked([piece for pair in zip(own, others) for part in pair for piece in part])
+
+
+def scatter_begin(parts):
     rows = parts.shape[0] // CHIPS
-    pieces = [[parts[(4 * p + j) * rows : (4 * p + j + 1) * rows] for p in range(4)] for j in range(4)]
-    arrived = []
-    for j in (1, 2, 3):
-        arrived.append(send(plane_scatter(*pieces[j]).astype(BF16), along_z(-j)))
-    return total_of(plane_scatter(*pieces[0]), *arrived)
-
-
-def head_routes(step):
-    return [
-        (
-            chip * CORES + core,
-            ((CHIPS // CORES) * core + (chip + step) % (CHIPS // CORES)) * CORES + chip // (CHIPS // CORES),
+    groups = []
+    for first, last in ((0, 1), (1, 4)):
+        own, for_x, for_y, far = [
+            parts[(4 * plane + first) * rows : (4 * plane + last) * rows] for plane in range(4)
+        ]
+        half = far.shape[0] // 2
+        groups.append(
+            (own, for_x, for_y, send(far[:half], along_x), send(far[half:], along_y))
         )
-        for chip in range(CHIPS)
-        for core in range(CORES)
-    ]
-
-
-def to_heads(pieces):
-    steps = CHIPS // CORES
-    chip = lax.axis_index("seq")
-    moved = [
-        lax.ppermute(
-            lax.dynamic_index_in_dim(pieces, (chip + step) % steps, 0, False), BOTH, head_routes(step)
-        )
-        for step in range(steps)
-    ]
-    order = jnp.stack(moved)
-    return jnp.take(order, (chip % steps - jnp.arange(steps)) % steps, axis=0)
-
-
-def from_heads(pieces):
-    steps = CHIPS // CORES
-    chip = lax.axis_index("seq")
-    moved = []
-    for step in range(steps):
-        back = [(target, source) for source, target in head_routes(step)]
-        moved.append(
-            lax.ppermute(
-                lax.dynamic_index_in_dim(pieces, (chip - step) % steps, 0, False), BOTH, back
-            )
-        )
-    order = jnp.stack(moved)
-    return jnp.take(order, (jnp.arange(steps) - chip) % steps, axis=0)
+    return groups
+
+
+def scatter_near(groups):
+    totals = []
+    for own, for_x, for_y, low, high in groups:
+        half = own.shape[0] // 2
+        for_y = stacked([total_of(for_y[:half], low).astype(BF16), for_y[half:]])
+        for_x = stacked([for_x[:half], total_of(for_x[half:], high).astype(BF16)])
+        totals.append(total_of(own, send(for_x, along_x), send(for_y, along_y)))
+    return totals[0], totals[1].astype(BF16)
+
+
+def scatter_levels(own, away):
+    rows = own.shape[0]
+    return [own] + [send(away[(j - 1) * rows : j * rows], along_z(-j)) for j in (1, 2, 3)]
 
 
 def nn(a, b):
@@ -547,62 +678,54 @@
     chip, core = lax.axis_index("seq"), lax.axis_index("head")
     first = core == 0
     tok_rows, width = inputs.shape
-    half_rows, half_width = tok_rows // CORES, width // CORES
+    half_rows = tok_rows // CORES
     row_count = w_query.shape[0]
+    half_count = row_count // CORES
     head_count = w_query.shape[1] // KEY_SIZE
     units = w_gate.shape[1] // CHIPS
+    own_count = CHIPS * half_rows
 
     def own_rows(values):
         return lax.dynamic_slice_in_dim(values, core * half_rows, half_rows, 0)
 
-    def turned(values):
-        return jnp.where(
-            first,
-            values,
-            jnp.concatenate([values[:, half_width:], values[:, :half_width]], axis=1),
-        )
-
-    def both_rows(own):
-        other = swap_cores(own)
-        return stacked([jnp.where(first, own, other), jnp.where(first, other, own)])
-
+    def in_order(own, other, axis):
+        return jnp.concatenate([jnp.where(first, own, other), jnp.where(first, other, own)], axis=axis)
+
+    def split_by_core(pieces):
+        kept = lax.dynamic_slice_in_dim(pieces, core * half_count, half_count, 1)
+        given = lax.dynamic_slice_in_dim(pieces, (1 - core) * half_count, half_count, 1)
+        return in_order(kept, swap_cores(given), 0)
+
+    def joined_by_core(mine):
+        both = in_order(mine[:, None], swap_cores(mine)[:, None], 1)
+        return both.reshape(width, mine.shape[-1])
+
+    inputs_own = own_rows(inputs).astype(F32)
+    scale_one = lax.rsqrt(jnp.mean(inputs_own * inputs_own, axis=-1, keepdims=True) + EPSILON)
+    normed_one = inputs_own * scale_one
     gain_one = mixer_gain.astype(F32)[:, None]
     gain_two = feed_gain.astype(F32)[:, None]
 
-    def by_head(weights, size):
-        return weights.reshape(row_count, head_count, size).transpose(1, 0, 2)
-
-    beta_pair = jnp.broadcast_to(w_beta.T[:, :, None], (head_count, row_count, 2))
-    packed_in = jnp.concatenate(
-        [
-            by_head(w_query, KEY_SIZE),
-            by_head(w_key, KEY_SIZE),
-            by_head(w_value, DV),
-            by_head(w_gating, DV),
-            beta_pair,
-            jnp.zeros((head_count, row_count, PACK - LOGIT - 2), BF16),
-        ],
-        axis=2,
-    )
-    packed_in = (packed_in.astype(F32) * gain_one).astype(BF16)
-    out_pieces = w_output.reshape(head_count, DV, row_count).transpose(0, 2, 1)
-
-    inputs_own = own_rows(inputs).astype(F32)
-    scale_one = lax.rsqrt(jnp.mean(inputs_own * inputs_own, axis=-1, keepdims=True) + EPSILON)
-    normed_own = (inputs_own * scale_one).astype(BF16)
-    normed_all = gather_rows(turned(normed_own))
-    mine_in = to_heads(packed_in).reshape(half_width, PACK)
-    weights_in = stacked([mine_in, swap_cores(mine_in)])
-
-    notes = stacked(
-        [decay_rate.T, doc_starts.astype(F32)[None], jnp.zeros((7, tok_rows), F32)]
-    )
-    notes = lax.all_gather(notes, BOTH, axis=0).reshape(CHIPS, CORES, 16, tok_rows)
-    rate = lax.dynamic_index_in_dim(
-        lax.dynamic_index_in_dim(notes, chip // head_count, 1, False), chip % head_count, 1, False
-    ).reshape(-1)
-    starts = notes[:, 0, 8].reshape(-1)
-    decay_grid, cols, rows = stream_tables(rate, starts)
+    in_kept, in_given = pack_heads(
+        core.astype(jnp.int32)[None],
+        gain_one,
+        w_query,
+        w_key,
+        w_value,
+        w_gating,
+        w_beta,
+        w_output,
+        decay_rate.T,
+        doc_starts.astype(F32)[None],
+    )
+    in_payload = in_order(in_kept, swap_cores(in_given), 0)
+    one_levels = gather_levels(normed_one.astype(BF16))
+    in_mine = exchange(after(in_payload, one_levels))
+    normed_all = gather_far(gather_near(one_levels))
+    in_mine = after(in_mine, normed_all)
+    weights_all = joined_by_core(in_mine)
+    weights_in, weights_out = weights_all[:, :PACK], weights_all[:, PACK:]
+
     taps_here = jnp.concatenate(
         [
             conv_query.reshape(CONV, head_count, KEY_SIZE),
@@ -617,12 +740,25 @@
     ).astype(F32)
     taps = stacked([taps, jnp.zeros_like(taps)])
     gain_head = jnp.broadcast_to(head_gain.astype(F32)[None], (8, DV))
+    seen = in_mine[:, :8, PACK - tok_rows // 2 : PACK].astype(F32).reshape(CHIPS, 4, tok_rows)
+    rate = (seen[:, 0] + seen[:, 1] + seen[:, 2]).reshape(-1)
+    starts = seen[:, 3].reshape(-1)
+    decay_grid, cols, rows = stream_tables(rate, starts)
 
     blocks = jnp.arange(CHIPS * CORES)
     far = blocks // CORES
     place = (
         4 * ((far ^ chip) % 4) + (chip // 4 - far // 4) % 4 + CHIPS * (blocks % CORES != core)
     ).astype(jnp.int32)
+
+    raw = nn(normed_all, weights_in)
+    column = lax.broadcasted_iota(jnp.int32, raw.shape, 1)
+    pre_own = jnp.where(
+        column == LOGIT + 1,
+        raw - lax.reduce_precision(raw, exponent_bits=8, mantissa_bits=7),
+        raw,
+    ).astype(BF16)
+    pre = (pre_own, swap_cores(pre_own))
 
     feed = jnp.concatenate(
         [
@@ -632,18 +768,19 @@
         ],
         axis=1,
     )
-
-    raw = nn(normed_all, weights_in)
-    column = lax.broadcasted_iota(jnp.int32, raw.shape, 1)
-    pre_own = jnp.where(
-        column == LOGIT + 1,
-        raw - lax.reduce_precision(raw, exponent_bits=8, mantissa_bits=7),
-        raw,
-    ).astype(BF16)
-    pre = stacked([pre_own, swap_cores(pre_own)])
-    mine_out = to_heads(out_pieces).reshape(half_width, DV)
-    weights_out = stacked([mine_out, swap_cores(mine_out)])
-    feed_mine = lax.all_to_all(feed, "seq", split_axis=0, concat_axis=0, tiled=True)
+    feed = after(feed, normed_all, weights_in, cols)
+    feed_mine = exchange(feed)
+    cot_own = own_rows(cotangent)
+    cot_gathered = lax.all_gather(cot_own, "seq", axis=0, tiled=False)
+    gated_own, gated_other, *kept = mixer_forward(place, *pre, decay_grid, cols, rows, taps, gain_head)
+    mixed_parts = nt(gated_own, weights_out).astype(BF16)
+    mixed_sums = scatter_begin(mixed_parts)
+
+    mixed_sums = scatter_near(mixed_sums)
+    feed_mine, normed_late, cot_all = after((feed_mine, normed_all, cot_gathered), mixed_sums)
+    relative = jnp.arange(CHIPS)
+    order = 4 * ((chip // 4 - relative % 4) % 4) + ((chip % 4) ^ (relative // 4))
+    cot_all = cot_all.at[order].get(mode="promise_in_bounds").reshape(own_count, width)
     feed_other = swap_cores(feed_mine)
 
     def unit_rows(position):
@@ -655,110 +792,128 @@
         )
 
     gate_rows, up_rows, down_rows = unit_rows(0), unit_rows(1), unit_rows(2)
-    cot_own = own_rows(cotangent)
-    cot_all = lax.all_gather(cot_own, "seq", axis=0, tiled=False)
-    relative = jnp.arange(CHIPS)
-    order = 4 * ((chip // 4 - relative % 4) % 4) + ((chip % 4) ^ (relative // 4))
-    cot_all = jnp.take(cot_all, order, axis=0).reshape(CHIPS * half_rows, width)
-    gated, *kept = mixer_forward(place, pre, decay_grid, cols, rows, taps, gain_head)
-    own_count = CHIPS * half_rows
-    mixed_sum = scatter_rows(nt(gated[:own_count], weights_out).astype(BF16))
-    middle = inputs_own + turned(mixed_sum)
+    cut = normed_late.reshape(own_count, CHIPS, CORES, half_count)
+    cut_mine = lax.dynamic_index_in_dim(cut, core, 2, False).reshape(own_count, width // CORES)
+    cut_given = lax.dynamic_index_in_dim(cut, 1 - core, 2, False).reshape(own_count, width // CORES)
+    cut_other = swap_cores(cut_given)
+
+    d_hidden = nt(cot_all, down_rows).astype(BF16)
+    middle = inputs_own + total_of(*scatter_levels(*mixed_sums))
     scale_two = lax.rsqrt(jnp.mean(middle * middle, axis=-1, keepdims=True) + EPSILON)
     normed_mid = middle * scale_two
-    mid_all = gather_rows(normed_mid.astype(BF16))
+    levels = gather_levels(normed_mid.astype(BF16))
+    levels[1:] = after(levels[1:], gate_rows, up_rows, d_hidden, cut_mine, cut_other)
+    mid_all = gather_far(gather_near(levels))
 
     gate_lin = nt(mid_all, gate_rows)
     up_lin = nt(mid_all, up_rows)
-    d_hidden = nt(cot_all, down_rows).astype(BF16).astype(F32)
+    d_hidden = d_hidden.astype(F32)
     sig = jax.nn.sigmoid(gate_lin)
     act = gate_lin * sig
     hidden = (act * up_lin).astype(BF16)
     d_gate = (d_hidden * up_lin * (sig * (1.0 + gate_lin * (1.0 - sig)))).astype(BF16)
     d_up = (d_hidden * act).astype(BF16)
-    e_two = scatter_rows((nn(d_gate, gate_rows) + nn(d_up, up_rows)).astype(BF16))
+    e_sums = scatter_near(scatter_begin((nn(d_gate, gate_rows) + nn(d_up, up_rows)).astype(BF16)))
+
+    feed_parts = after(nn(hidden, down_rows).astype(BF16), e_sums)
+    e_two = total_of(*scatter_levels(*e_sums))
     d_middle = cot_own.astype(F32) + scale_two * (
         e_two - normed_mid * jnp.mean(e_two * normed_mid, axis=-1, keepdims=True)
     )
-    d_mid_all = gather_rows(turned(d_middle.astype(BF16)))
-
-    d_gated_own = nn(d_mid_all, weights_out).astype(BF16)
-    d_gated = stacked([d_gated_own, swap_cores(d_gated_own)])
-    d_pre, grad_taps, grad_gain = mixer_backward(
-        place, d_gated, pre, decay_grid, cols, taps, gain_head, kept
-    )
-
-    feed_out = scatter_rows(nn(hidden, down_rows).astype(BF16))
-    block_out = both_rows((middle + feed_out).astype(BF16))
+    levels = gather_levels(d_middle.astype(BF16))
+
     parts = [tn(d_gate, mid_all), tn(d_up, mid_all), tn(hidden, cot_all)]
-    keep_part = jnp.concatenate([part[:units] for part in parts], axis=0)
-    give_part = jnp.concatenate([part[units:] for part in parts], axis=0).astype(BF16)
+    keep_part = stacked([part[:units] for part in parts])
+    give_part = stacked([part[units:] for part in parts]).astype(BF16)
     feed_grad = (keep_part + swap_cores(give_part).astype(F32)).astype(BF16)
     feed_grad = feed_grad.reshape(3 * units, CHIPS, row_count).transpose(1, 0, 2)
-    feed_back = lax.all_to_all(feed_grad, "seq", split_axis=0, concat_axis=0, tiled=True).astype(F32)
+    feed_grad = jnp.pad(feed_grad, ((0, 0), (0, half_count * DV // row_count), (0, 0)))
+    levels[1:] = after(levels[1:], feed_grad)
+    seats = jnp.arange(CHIPS)
+    seat = 4 * ((seats % 4) ^ (chip % 4)) + (chip // 4 - seats // 4) % 4
+    feed_parts = feed_parts.reshape(CHIPS, half_rows, width)
+    feed_parts = feed_parts.at[seat].get(mode="promise_in_bounds").reshape(own_count, width)
+    near = after(gather_near(levels), feed_parts)
+    d_mid_all = gather_far(near)
+    feed_out = lax.psum_scatter(after(feed_parts, d_mid_all), "seq", scatter_dimension=0, tiled=True)
+
+    d_gated_own = nn(d_mid_all, weights_out).astype(BF16)
+    d_gated = (d_gated_own, swap_cores(d_gated_own))
+    grad_out = tn(d_mid_all, gated_own).astype(BF16).reshape(CHIPS, CORES, half_count, DV)
+    grad_out = total_of(
+        lax.dynamic_index_in_dim(grad_out, core, 1, False),
+        swap_cores(lax.dynamic_index_in_dim(grad_out, 1 - core, 1, False)),
+    ).astype(BF16)
+    feed_grad = lax.dynamic_update_slice(
+        feed_grad, grad_out.reshape(CHIPS, half_count * DV // row_count, row_count), (0, 3 * units, 0)
+    )
+    feed_back = exchange(feed_grad)
+    d_pre_own, d_pre_other, grad_taps, grad_gain = mixer_backward(
+        place, d_gated, pre, decay_grid, cols, taps, gain_head, kept
+    )
+
+    d_pre_own, d_pre_other, feed_back = after((d_pre_own, d_pre_other, feed_back))
+
+
+    small = jnp.concatenate([jnp.sum(grad_taps, axis=1).reshape(-1), jnp.sum(grad_gain, axis=0)])
+    small = small.reshape(-1, 64)
+    small_rows = small.shape[0]
+    grad_in = tn(cut_mine, d_pre_own) + tn(cut_other, d_pre_other)
+    small = jnp.pad(small, ((0, half_count - small_rows), (PACK - 64, 0)))
+    grad_in = (grad_in.reshape(CHIPS, half_count, PACK) + small).astype(BF16)
+    e_parts = nt(after(d_pre_own, grad_in), weights_in).astype(BF16)
+    grad_in = exchange(grad_in)
+    e_sums = scatter_near(scatter_begin(e_parts))
+    e_sums, grad_in = after((e_sums, grad_in))
+    small = grad_in[:, :small_rows, PACK - 64 :].astype(F32).reshape(CHIPS, -1)
+    taps_all = lax.dynamic_slice_in_dim(small[:, : CONV * MIXED], core * head_count, head_count, 0)
+    taps_all = taps_all.reshape(head_count, CONV, MIXED).transpose(1, 0, 2)
+
+    def heads_here(back):
+        mine = lax.dynamic_slice_in_dim(back, core * head_count, head_count, 0)
+        given = lax.dynamic_slice_in_dim(back, (1 - core) * head_count, head_count, 0)
+        return in_order(mine, swap_cores(given), 1)
+
+    grad_in = heads_here(grad_in)
+    block_out_own = (middle + feed_out.astype(F32)).astype(BF16)
+    block_out = in_order(block_out_own, swap_cores(block_out_own), 0)
+    e_one = total_of(*scatter_levels(*e_sums))
+    grad_own = d_middle + scale_one * (
+        e_one - normed_one * jnp.mean(e_one * normed_one, axis=-1, keepdims=True)
+    )
+    grad_inputs = in_order(grad_own, swap_cores(grad_own), 0)
+
+    grad_out = heads_here(feed_back[:, 3 * units :].reshape(CHIPS, half_count, DV))
+    grad_output = grad_out.astype(F32).transpose(0, 2, 1).reshape(head_count * DV, row_count)
+    feed_back = feed_back[:, : 3 * units].astype(F32)
     raw_gate = feed_back[:, :units].reshape(CHIPS * units, row_count).T
     raw_up = feed_back[:, units : 2 * units].reshape(CHIPS * units, row_count).T
     grad_down = feed_back[:, 2 * units :].reshape(CHIPS * units, row_count)
-    grad_gate, grad_up = raw_gate * gain_two, raw_up * gain_two
-    feed_gain_part = jnp.sum(
-        raw_gate * w_gate.astype(F32) + raw_up * w_up.astype(F32), axis=1
-    )
-
-    e_one = scatter_rows(nt(d_pre[:own_count], weights_in).astype(BF16))
-    e_one = turned(e_one)
-    normed_one = inputs_own * scale_one
-    grad_own = d_middle + scale_one * (
-        e_one - normed_one * jnp.mean(e_one * normed_one, axis=-1, keepdims=True)
-    )
-    grad_inputs = both_rows(grad_own)
-    normed_other = swap_cores(normed_all[:, half_width:])
-    grad_in = tn(normed_all[:, :half_width], d_pre[:own_count]) + tn(normed_other, d_pre[own_count:])
-    grad_in = from_heads(grad_in.astype(BF16).reshape(CHIPS // CORES, row_count, PACK))
-    d_mid_other = swap_cores(d_mid_all[:, half_width:])
-    grad_out = tn(d_mid_all[:, :half_width], gated[:own_count]) + tn(d_mid_other, gated[own_count:])
-    grad_out = from_heads(grad_out.astype(BF16).reshape(CHIPS // CORES, row_count, DV))
-    grad_output = grad_out.astype(F32).transpose(0, 2, 1).reshape(head_count * DV, row_count)
-
-    def by_rows(start, size):
-        part = grad_in[:, :, start : start + size].astype(F32)
-        return part.transpose(1, 0, 2).reshape(row_count, head_count * size)
-
-    raw_query = by_rows(0, KEY_SIZE)
-    raw_key = by_rows(KEY_SIZE, KEY_SIZE)
-    raw_value = by_rows(2 * KEY_SIZE, DV)
-    raw_gating = by_rows(MIXED, DV)
-    raw_beta = by_rows(LOGIT, 1)
-    mixer_gain_part = (
-        jnp.sum(raw_query * w_query.astype(F32), axis=1)
-        + jnp.sum(raw_key * w_key.astype(F32), axis=1)
-        + jnp.sum(raw_value * w_value.astype(F32), axis=1)
-        + jnp.sum(raw_gating * w_gating.astype(F32), axis=1)
-        + jnp.sum(raw_beta * w_beta.astype(F32), axis=1)
+    feed_gain_part = jnp.sum(raw_gate * w_gate.astype(F32) + raw_up * w_up.astype(F32), axis=1)
+
+    raw_query, raw_key, raw_value, raw_gating, raw_beta, mixer_gain_part = unpack_heads(
+        grad_in, gain_one, w_query, w_key, w_value, w_gating, w_beta
     )
     gain_parts = jnp.stack([mixer_gain_part, feed_gain_part])
     gain_totals = gain_parts + swap_cores(gain_parts)
 
-    small = jnp.concatenate([jnp.sum(grad_taps, axis=1).reshape(-1), jnp.sum(grad_gain, axis=0)])
-    small = lax.all_gather(small.reshape(-1, 128), "seq", axis=0).reshape(CHIPS, -1)
-    taps_all = lax.dynamic_slice_in_dim(small[:, : CONV * MIXED], core * head_count, head_count, 0)
-    taps_all = taps_all.reshape(head_count, CONV, MIXED).transpose(1, 0, 2)
     return (
         block_out,
         grad_inputs,
         gain_totals[0],
-        raw_query * gain_one,
-        raw_key * gain_one,
-        raw_value * gain_one,
-        raw_beta * gain_one,
-        raw_gating * gain_one,
+        raw_query,
+        raw_key,
+        raw_value,
+        raw_beta,
+        raw_gating,
         taps_all[:, :, :KEY_SIZE].reshape(CONV, head_count * KEY_SIZE),
         taps_all[:, :, KEY_SIZE : 2 * KEY_SIZE].reshape(CONV, head_count * KEY_SIZE),
         taps_all[:, :, 2 * KEY_SIZE :].reshape(CONV, head_count * DV),
         jnp.sum(small[:, CONV * MIXED :], axis=0),
         grad_output,
         gain_totals[1],
-        grad_gate,
-        grad_up,
+        raw_gate * gain_two,
+        raw_up * gain_two,
         grad_down,
     )
 

time: 1050 us -> 738 us (0.70)
  starting transfers between devices: 259 us -> 134 us
  blocking collectives: 119 us -> 0 us
  waiting for transfers between devices: 335 us -> 293 us
  local copies, waits for them, and re-layouts: 107 us -> 91.8 us
  other arithmetic: 66.1 us -> 53.1 us
    all_gather x2 -> x0, blocking collectives: 119 us -> none  [the longest x1 81 us: head_plan(): lax.all_gather(notes, BOTH, axis=0).reshape(CHIPS, CORES, 16, tok_rows)]
    ppermute x133 -> x66, starting transfers between devices: 176 us -> 81.9 us  [send(): lax.ppermute(value, 'seq', [(index, target(index)) for index in range(CHI...]
    ppermute x32 -> x0, waiting for transfers between devices: 81 us -> none  [the longest x16 43 us: to_heads(): lax.ppermute(lax.dynamic_index_in_dim(pieces, (chip + step) % steps, 0, F...]
    ppermute x32 -> x0, starting transfers between devices: 55.3 us -> none  [the longest x16 31.4 us: from_heads(): lax.ppermute(lax.dynamic_index_in_dim(pieces, (chip - step) % steps, 0, F...]
    all_to_all x2 -> x4, starting transfers between devices: 10.1 us -> 49.3 us  [exchange(): lax.all_to_all(pieces, 'seq', split_axis=0, concat_axis=0, tiled=True)]
    ppermute x133 -> x66, waiting for transfers between devices: 253 us -> 275 us  [send(): lax.ppermute(value, 'seq', [(index, target(index)) for index in range(CHI...]
    unnamed x295 -> x131, local copies, waits for them, and re-layouts: 60.6 us -> 43 us
    ppermute x12 -> x14, starting transfers between devices: 17.5 us -> 2.29 us  [swap_cores(): return lax.ppermute(value, 'head', [(0, 1), (1, 0)])]
  transfers between devices with their start and end apart: 180 -> 86, of which waited for: 81 -> 39; matrix products, arithmetic and copies ran while one was open for 16% -> 21% of each run, Pallas kernels for 8% -> 12%
where the time goes in v2:
time: 738 us; the launch traced here: 729 us
  waiting for transfers between devices  293 us (40%)
  starting transfers between devices  134 us (18%)
  Pallas kernels  92.1 us (12%)
  local copies, waits for them, and re-layouts  91.8 us (12%)
  other arithmetic  53.1 us (7%)
  matrix products  49.1 us (7%)
  between operations  16.1 us (2%)
    ppermute x66, waiting for transfers between devices, send(): lax.ppermute(value, 'seq', [(index, target(index)) for index in range(CHI...  275 us
    ppermute x66, starting transfers between devices, send(): lax.ppermute(value, 'seq', [(index, target(index)) for index in range(CHI...  81.9 us
    all_to_all x4, starting transfers between devices, exchange(): lax.all_to_all(pieces, 'seq', split_axis=0, concat_axis=0, tiled=True)  49.3 us
    dot_general x16, matrix products, mm(): return lax.dot_general(a, b, (dims, ((), ())), preferred_element_type=F32)  49.1 us
    pallas_call x1, Pallas kernels, mixer_backward(): pl.pallas_call(backward_kernel, out_shape=(shape((half, PACK), BF16), sha...  45.6 us
    unnamed x131, local copies, waits for them, and re-layouts  43 us
    pallas_call x1, Pallas kernels, mixer_forward(): pl.pallas_call(forward_kernel, out_shape=(shape((half, DV), BF16), shape(...  42.9 us
    all_to_all x4, waiting for transfers between devices, exchange(): lax.all_to_all(pieces, 'seq', split_axis=0, concat_axis=0, tiled=True)  15.2 us
  transfers between devices with their start and end apart: 86, of which 39 were waited for; matrix products, arithmetic and copies ran while one was open for 21% of the time, Pallas kernels for 12%

profile of v2, /device:TPU:0, one launch (start us, length us, event | category | flops | bytes accessed | tf_op | source)
XLA Modules:
  0.0 728.9 jit_solution(7634684925433211465)
XLA Ops:
  19.9 4.6 collective-permute-start.2
  31.2 16.3 %collective-permute-done.1 = bf16[64,2048]{1,0:T(8,128)(2,1)S(1)} collective-permute-done((bf16[64,2048]{1,0:T(8,128)(2,1)S(1)}, bf16[64,2048]{1,0:T(8,128)(2,1)S(1)}, u32[]{:S(2)}, u32[]{:S(2)}) %collective-permute-start.1) | collective-permute-done | bytes 262176 | tf_op jit(solution)/shard_map/ppermute | solution.py:565
  47.5 6.1 all-to-all-start
  60.0 43.1 %collective-permute-done.5 = bf16[64,2048]{1,0:T(8,128)(2,1)S(1)} collective-permute-done((bf16[64,2048]{1,0:T(8,128)(2,1)S(1)}, bf16[64,2048]{1,0:T(8,128)(2,1)S(1)}, u32[]{:S(2)}, u32[]{:S(2)}) %collective-permute-start.5) | collective-permute-done | bytes 262176 | tf_op jit(solution)/shard_map/ppermute | solution.py:565
  133.1 5.7 fusion.1.pre_own
  142.2 6.0 all-to-all-start.1
  148.2 42.9 %mixer_forward.1 = (bf16[1024,256]{1,0:T(8,128)(2,1)S(1)}, bf16[1024,256]{1,0:T(8,128)(2,1)}, f32[2048,256]{1,0:T(8,128)}, f32[2048,512]{1,0:T(8,128)}, f32[2048...) custom-call(s32[32]{0:T(128)S(1)} %fusion.28.place, ...), custom_call_target="tpu_custom_call" | custom-call | flops 30000001024 | bytes 100000000 | tf_op jit(solution)/shard_map/mixer_forward/pallas_call | solution.py:362
  198.1 20.8 %collective-permute-done.21 = bf16[96,2048]{1,0:T(8,128)(2,1)S(1)} collective-permute-done((bf16[96,2048]{1,0:T(8,128)(2,1)S(1)}, bf16[96,2048]{1,0:T(8,128)(2,1)S(1)}, u32[]{:S(2)}, u32[]{:S(2)}) %collective-permute-start.21) | collective-permute-done | bytes 393248 | tf_op jit(solution)/shard_map/ppermute | solution.py:565
  224.4 15.4 %collective-permute-done.22 = bf16[192,2048]{1,0:T(8,128)(2,1)S(1)} collective-permute-done((bf16[192,2048]{1,0:T(8,128)(2,1)S(1)}, bf16[192,2048]{1,0:T(8,128)(2,1)S(1)}, u32[]{:S(2)}, u32[]{:S(2)}) %collective-permute-start.22) | collective-permute-done | bytes 786464 | tf_op jit(solution)/shard_map/ppermute | solution.py:565
  241.2 5.9 collective-permute-start.23
  254.1 9.1 %collective-permute-done.25 = bf16[64,2048]{1,0:T(8,128)(2,1)S(1)} collective-permute-done((bf16[64,2048]{1,0:T(8,128)(2,1)}, bf16[64,2048]{1,0:T(8,128)(2,1)S(1)}, u32[]{:S(2)}, u32[]{:S(2)}) %collective-permute-start.25) | collective-permute-done | bytes 262176 | tf_op jit(solution)/shard_map/ppermute | solution.py:565
  263.2 7.2 collective-permute-done.24
  275.9 6.8 copy.122
  282.7 5.1 constant_dynamic-slice_fusion.3
  287.7 5.1 gather_fusion
  304.0 21.5 %collective-permute-done.33 = bf16[64,2048]{1,0:T(8,128)(2,1)S(1)} collective-permute-done((bf16[64,2048]{1,0:T(8,128)(2,1)S(1)}, bf16[64,2048]{1,0:T(8,128)(2,1)S(1)}, u32[]{:S(2)}, u32[]{:S(2)}) %collective-permute-start.33) | collective-permute-done | bytes 262176 | tf_op jit(solution)/shard_map/ppermute | solution.py:565
  332.6 6.6 collective-permute-done.37
  353.5 7.0 collective-permute-done.45
  367.2 15.2 %collective-permute-done.46 = bf16[192,2048]{1,0:T(8,128)(2,1)S(1)} collective-permute-done((bf16[192,2048]{1,0:T(8,128)(2,1)S(1)}, bf16[192,2048]{1,0:T(8,128)(2,1)S(1)}, u32[]{:S(2)}, u32[]{:S(2)}) %collective-permute-start.46) | collective-permute-done | bytes 786464 | tf_op jit(solution)/shard_map/ppermute | solution.py:565
  395.4 8.7 %collective-permute-done.48 = bf16[64,2048]{1,0:T(8,128)(2,1)S(1)} collective-permute-done((bf16[64,2048]{1,0:T(8,128)(2,1)S(1)}, bf16[64,2048]{1,0:T(8,128)(2,1)S(1)}, u32[]{:S(2)}, u32[]{:S(2)}) %collective-permute-start.48) | collective-permute-done | bytes 262176 | tf_op jit(solution)/shard_map/ppermute | solution.py:565
  414.9 12.9 %collective-permute-done.53 = bf16[64,2048]{1,0:T(8,128)(2,1)S(1)} collective-permute-done((bf16[64,2048]{1,0:T(8,128)(2,1)S(1)}, bf16[64,2048]{1,0:T(8,128)(2,1)S(1)}, u32[]{:S(2)}, u32[]{:S(2)}) %collective-permute-start.53) | collective-permute-done | bytes 262176 | tf_op jit(solution)/shard_map/ppermute | solution.py:565
  443.5 5.0 gather_fusion.1
  478.0 8.9 %all-to-all-start.2 = ((bf16[16,656,128]{2,1,0:T(8,128)(2,1)}), bf16[16,656,128]{2,1,0:T(8,128)(2,1)}, u32[]{:S(2)}, u32[]{:S(2)}) async-start(bf16[16,656,128]{2,1,0:T(8,128)(2,1)} %pad_maximum_fusion.1), calls=%async_computation.3 | async-start | bytes 5373952 | tf_op jit(solution)/shard_map/all_to_all | solution.py:573
  492.8 45.6 %mixer_backward.1 = (bf16[1024,896]{1,0:T(8,128)(2,1)}, bf16[1024,896]{1,0:T(8,128)(2,1)}, f32[4,8,512]{2,1,0:T(8,128)S(1)}, f32[8,256]{1,0:T(8,128)S(1)}) custom-call(s32[32]{0:T(128)S(1)} %fusion.28.place, bf16[1024,256]{1,0:T(8,128)(2,1)S(1)} %convolution_convert_fusion.5.d_gated_own, bf16[1024,256]{1,0:T(8,128)(2,1)S(1)} %collective-permute-done.62.d_gated_other, ...), custom_call_target="tpu_custom_call" | custom-call | flops 30000001024 | bytes 100000000 | tf_op jit(solution)/shard_map/mixer_backward/pallas_call | solution.py:395
  538.7 15.2 %all-to-all-done.2 = bf16[16,656,128]{2,1,0:T(8,128)(2,1)} async-done(((bf16[16,656,128]{2,1,0:T(8,128)(2,1)}), bf16[16,656,128]{2,1,0:T(8,128)(2,1)}, u32[]{:S(2)}, u32[]{:S(2)}) %all-to-all-start.2) | async-done | bytes 2687008 | tf_op jit(solution)/shard_map/all_to_all | solution.py:573
  564.2 28.4 %all-to-all-start.3 = ((bf16[16,64,896]{2,1,0:T(8,128)(2,1)}), bf16[16,64,896]{2,1,0:T(8,128)(2,1)S(1)}, u32[]{:S(2)}, u32[]{:S(2)}) async-start(bf16[16,64,896]{2,1,0:T(8,128)(2,1)} %add_convert_fusion.1), calls=%async_computation.4 | async-start | bytes 3670016 | tf_op jit(solution)/shard_map/all_to_all | solution.py:573
  594.6 7.1 convolution_convert_fusion.2
  619.0 6.9 collective-permute-done.67
  633.1 15.2 %collective-permute-done.71 = bf16[96,2048]{1,0:T(8,128)(2,1)} collective-permute-done((bf16[96,2048]{1,0:T(8,128)(2,1)}, bf16[96,2048]{1,0:T(8,128)(2,1)}, u32[]{:S(2)}, u32[]{:S(2)}) %collective-permute-start.71) | collective-permute-done | bytes 393248 | tf_op jit(solution)/shard_map/ppermute | solution.py:565
  659.8 13.3 %collective-permute-done.72 = bf16[192,2048]{1,0:T(8,128)(2,1)} collective-permute-done((bf16[192,2048]{1,0:T(8,128)(2,1)}, bf16[192,2048]{1,0:T(8,128)(2,1)}, u32[]{:S(2)}, u32[]{:S(2)}) %collective-permute-start.72) | collective-permute-done | bytes 786464 | tf_op jit(solution)/shard_map/ppermute | solution.py:565
  693.0 5.5 collective-permute-done.75
  698.5 10.4 %collective-permute-done.74 = bf16[64,2048]{1,0:T(8,128)(2,1)} collective-permute-done((bf16[64,2048]{1,0:T(8,128)(2,1)}, bf16[64,2048]{1,0:T(8,128)(2,1)}, u32[]{:S(2)}, u32[]{:S(2)}) %collective-permute-start.74) | collective-permute-done | bytes 262176 | tf_op jit(solution)/shard_map/ppermute | solution.py:565
  (450 shorter events, 279.5 us)
Async XLA Ops:
  47.5 70.6 %all-to-all-start = ((bf16[16,64,1152]{2,1,0:T(8,128)(2,1)}), bf16[16,64,1152]{2,1,0:T(8,128)(2,1)S(1)}, u32[]{:S(2)}, u32[]{:S(2)}) async-start(bf16[16,64,1152]{2,1,0:T(8,128)(2,1)} %pad_maximum_fusion.2), calls=%async_computation | async-start | bytes 4718592 | tf_op jit(solution)/shard_map/all_to_all | solution.py:573
  53.6 218.2 %all-gather.3.cloned.1.call-start = ((), (), s32[]{:S(2)}) async-start(), calls=%async_computation.6 | async-start | bytes 4456448 | tf_op jit(solution)/shard_map/all_gather | solution.py:774
  55.9 51.0 %collective-permute-start.6 = (bf16[192,2048]{1,0:T(8,128)(2,1)S(1)}, bf16[192,2048]{1,0:T(8,128)(2,1)S(1)}, u32[]{:S(2)}, u32[]{:S(2)}) collective-permute-start(bf16[192,2048]{1,0:T(8,128)(2,1)S(1)} %get-tuple-element.271), channel_id=1, source_target_pairs={{0,4},{2,6},{4,0},{6,2},{8,12},{10,14},{12,8},{14,10},{16,20},{18,... | collective-permute-start | bytes 2359304 | tf_op jit(solution)/shard_map/ppermute | solution.py:565
  57.9 49.2 %collective-permute-start.4 = (bf16[192,2048]{1,0:T(8,128)(2,1)S(1)}, bf16[192,2048]{1,0:T(8,128)(2,1)S(1)}, u32[]{:S(2)}, u32[]{:S(2)}) collective-permute-start(bf16[192,2048]{1,0:T(8,128)(2,1)S(1)} %get-tuple-element.271), channel_id=1, source_target_pairs={{0,2},{2,0},{4,6},{6,4},{8,10},{10,8},{12,14},{14,12},{16,18},{18,... | collective-permute-start | bytes 2359304 | tf_op jit(solution)/shard_map/ppermute | solution.py:565
  59.3 43.8 %collective-permute-start.5 = (bf16[64,2048]{1,0:T(8,128)(2,1)S(1)}, bf16[64,2048]{1,0:T(8,128)(2,1)S(1)}, u32[]{:S(2)}, u32[]{:S(2)}) collective-permute-start(bf16[64,2048]{1,0:T(8,128)(2,1)S(1)} %get-tuple-element.191), channel_id=1, source_target_pairs={{0,4},{2,6},{4,0},{6,2},{8,12},{10,14},{12,8},{14,10},{16,20},{18,... | collective-permute-start | bytes 786440 | tf_op jit(solution)/shard_map/ppermute | solution.py:565
  59.9 44.8 %collective-permute-start.3 = (bf16[64,2048]{1,0:T(8,128)(2,1)S(1)}, bf16[64,2048]{1,0:T(8,128)(2,1)S(1)}, u32[]{:S(2)}, u32[]{:S(2)}) collective-permute-start(bf16[64,2048]{1,0:T(8,128)(2,1)S(1)} %get-tuple-element.191), channel_id=1, source_target_pairs={{0,2},{2,0},{4,6},{6,4},{8,10},{10,8},{12,14},{14,12},{16,18},{18,... | collective-permute-start | bytes 786440 | tf_op jit(solution)/shard_map/ppermute | solution.py:565
  142.2 129.5 %all-to-all-start.1 = ((bf16[16,528,128]{2,1,0:T(8,128)(2,1)}), bf16[16,528,128]{2,1,0:T(8,128)(2,1)}, u32[]{:S(2)}, u32[]{:S(2)}) async-start(bf16[16,528,128]{2,1,0:T(8,128)(2,1)} %pad_maximum_fusion.3), calls=%async_computation.1 | async-start | bytes 4325376 | tf_op jit(solution)/shard_map/all_to_all | solution.py:573
  193.8 25.1 %collective-permute-start.21 = (bf16[96,2048]{1,0:T(8,128)(2,1)S(1)}, bf16[96,2048]{1,0:T(8,128)(2,1)S(1)}, u32[]{:S(2)}, u32[]{:S(2)}) collective-permute-start(bf16[96,2048]{1,0:T(8,128)(2,1)S(1)} %get-tuple-element.231), channel_id=1, source_target_pairs={{0,2},{2,0},{4,6},{6,4},{8,10},{10,8},{12,14},{14,12},{16,18},{18,... | collective-permute-start | bytes 1179656 | tf_op jit(solution)/shard_map/ppermute | solution.py:565
  197.4 24.1 %collective-permute-start.17 = (bf16[32,2048]{1,0:T(8,128)(2,1)S(1)}, bf16[32,2048]{1,0:T(8,128)(2,1)S(1)}, u32[]{:S(2)}, u32[]{:S(2)}) collective-permute-start(bf16[32,2048]{1,0:T(8,128)(2,1)S(1)} %get-tuple-element.225), channel_id=1, source_target_pairs={{0,2},{2,0},{4,6},{6,4},{8,10},{10,8},{12,14},{14,12},{16,18},{18,... | collective-permute-start | bytes 393224 | tf_op jit(solution)/shard_map/ppermute | solution.py:565
  198.0 23.5 %collective-permute-start.15 = (bf16[32,2048]{1,0:T(8,128)(2,1)S(1)}, bf16[32,2048]{1,0:T(8,128)(2,1)S(1)}, u32[]{:S(2)}, u32[]{:S(2)}) collective-permute-start(bf16[32,2048]{1,0:T(8,128)(2,1)S(1)} %get-tuple-element.226), channel_id=1, source_target_pairs={{0,4},{2,6},{4,0},{6,2},{8,12},{10,14},{12,8},{14,10},{16,20},{18,... | collective-permute-start | bytes 393224 | tf_op jit(solution)/shard_map/ppermute | solution.py:565
  222.3 28.4 %collective-permute-start.18 = (bf16[64,2048]{1,0:T(8,128)(2,1)}, bf16[64,2048]{1,0:T(8,128)(2,1)S(1)}, u32[]{:S(2)}, u32[]{:S(2)}) collective-permute-start(bf16[64,2048]{1,0:T(8,128)(2,1)} %pad_maximum_fusion.15), channel_id=1, source_target_pairs={{0,4},{2,6},{4,0},{6,2},{8,12},{10,14},{12,8},{14,10},{16,20},{18,... | collective-permute-start | bytes 786440 | tf_op jit(solution)/shard_map/ppermute | solution.py:565
  222.9 27.8 %collective-permute-start.16 = (bf16[64,2048]{1,0:T(8,128)(2,1)S(1)}, bf16[64,2048]{1,0:T(8,128)(2,1)S(1)}, u32[]{:S(2)}, u32[]{:S(2)}) collective-permute-start(bf16[64,2048]{1,0:T(8,128)(2,1)S(1)} %pad_maximum_fusion.14), channel_id=1, source_target_pairs={{0,2},{2,0},{4,6},{6,4},{8,10},{10,8},{12,14},{14,12},{16,18},{18,... | collective-permute-start | bytes 786440 | tf_op jit(solution)/shard_map/ppermute | solution.py:565
  272.7 26.7 %collective-permute-start.28 = (bf16[64,2048]{1,0:T(8,128)(2,1)S(1)}, bf16[64,2048]{1,0:T(8,128)(2,1)S(1)}, u32[]{:S(2)}, u32[]{:S(2)}) collective-permute-start(bf16[64,2048]{1,0:T(8,128)(2,1)S(1)} %get-tuple-element.184), channel_id=1, source_target_pairs={{0,24},{2,26},{4,28},{6,30},{8,0},{10,2},{12,4},{14,6},{16,8},{18,... | collective-permute-start | bytes 786440 | tf_op jit(solution)/shard_map/ppermute | solution.py:565
  275.3 24.1 %collective-permute-start.27 = (bf16[64,2048]{1,0:T(8,128)(2,1)S(1)}, bf16[64,2048]{1,0:T(8,128)(2,1)S(1)}, u32[]{:S(2)}, u32[]{:S(2)}) collective-permute-start(bf16[64,2048]{1,0:T(8,128)(2,1)S(1)} %get-tuple-element.184), channel_id=1, source_target_pairs={{0,16},{2,18},{4,20},{6,22},{8,24},{10,26},{12,28},{14,30},{16,0},... | collective-permute-start | bytes 786440 | tf_op jit(solution)/shard_map/ppermute | solution.py:565
  275.3 24.1 %collective-permute-start.26 = (bf16[64,2048]{1,0:T(8,128)(2,1)S(1)}, bf16[64,2048]{1,0:T(8,128)(2,1)S(1)}, u32[]{:S(2)}, u32[]{:S(2)}) collective-permute-start(bf16[64,2048]{1,0:T(8,128)(2,1)S(1)} %get-tuple-element.184), channel_id=1, source_target_pairs={{0,8},{2,10},{4,12},{6,14},{8,16},{10,18},{12,20},{14,22},{16,24},... | collective-permute-start | bytes 786440 | tf_op jit(solution)/shard_map/ppermute | solution.py:565
  299.9 27.5 %collective-permute-start.34 = (bf16[192,2048]{1,0:T(8,128)(2,1)S(1)}, bf16[192,2048]{1,0:T(8,128)(2,1)S(1)}, u32[]{:S(2)}, u32[]{:S(2)}) collective-permute-start(bf16[192,2048]{1,0:T(8,128)(2,1)S(1)} %get-tuple-element.265), channel_id=1, source_target_pairs={{0,4},{2,6},{4,0},{6,2},{8,12},{10,14},{12,8},{14,10},{16,20},{18,... | collective-permute-start | bytes 2359304 | tf_op jit(solution)/shard_map/ppermute | solution.py:565
  300.0 28.2 %collective-permute-start.32 = (bf16[192,2048]{1,0:T(8,128)(2,1)S(1)}, bf16[192,2048]{1,0:T(8,128)(2,1)S(1)}, u32[]{:S(2)}, u32[]{:S(2)}) collective-permute-start(bf16[192,2048]{1,0:T(8,128)(2,1)S(1)} %get-tuple-element.265), channel_id=1, source_target_pairs={{0,2},{2,0},{4,6},{6,4},{8,10},{10,8},{12,14},{14,12},{16,18},{18,... | collective-permute-start | bytes 2359304 | tf_op jit(solution)/shard_map/ppermute | solution.py:565
  300.6 24.9 %collective-permute-start.33 = (bf16[64,2048]{1,0:T(8,128)(2,1)S(1)}, bf16[64,2048]{1,0:T(8,128)(2,1)S(1)}, u32[]{:S(2)}, u32[]{:S(2)}) collective-permute-start(bf16[64,2048]{1,0:T(8,128)(2,1)S(1)} %get-tuple-element.184), channel_id=1, source_target_pairs={{0,4},{2,6},{4,0},{6,2},{8,12},{10,14},{12,8},{14,10},{16,20},{18,... | collective-permute-start | bytes 786440 | tf_op jit(solution)/shard_map/ppermute | solution.py:565
  302.6 23.6 %collective-permute-start.31 = (bf16[64,2048]{1,0:T(8,128)(2,1)S(1)}, bf16[64,2048]{1,0:T(8,128)(2,1)S(1)}, u32[]{:S(2)}, u32[]{:S(2)}) collective-permute-start(bf16[64,2048]{1,0:T(8,128)(2,1)S(1)} %get-tuple-element.184), channel_id=1, source_target_pairs={{0,2},{2,0},{4,6},{6,4},{8,10},{10,8},{12,14},{14,12},{16,18},{18,... | collective-permute-start | bytes 786440 | tf_op jit(solution)/shard_map/ppermute | solution.py:565
  365.3 23.8 %collective-permute-start.42 = (bf16[64,2048]{1,0:T(8,128)(2,1)S(1)}, bf16[64,2048]{1,0:T(8,128)(2,1)S(1)}, u32[]{:S(2)}, u32[]{:S(2)}) collective-permute-start(bf16[64,2048]{1,0:T(8,128)(2,1)S(1)} %pad_maximum_fusion.17), channel_id=1, source_target_pairs={{0,4},{2,6},{4,0},{6,2},{8,12},{10,14},{12,8},{14,10},{16,20},{18,... | collective-permute-start | bytes 786440 | tf_op jit(solution)/shard_map/ppermute | solution.py:565
  430.0 23.4 %collective-permute-start.56 = (bf16[192,2048]{1,0:T(8,128)(2,1)}, bf16[192,2048]{1,0:T(8,128)(2,1)S(1)}, u32[]{:S(2)}, u32[]{:S(2)}) collective-permute-start(bf16[192,2048]{1,0:T(8,128)(2,1)} %constant_dynamic-update-slice_fusion.30), channel_id=1, source_target_pairs={{0,4},{2,6},{4,0},{6,2},{8,12},{10,14},{12,8},{14,10},{16,20},{18,... | collective-permute-start | bytes 2359304 | tf_op jit(solution)/shard_map/ppermute | solution.py:565
  437.4 30.6 %collective-permute-start.63 = (bf16[528,2048]{1,0:T(8,128)(2,1)}, bf16[528,2048]{1,0:T(8,128)(2,1)}, u32[]{:S(2)}, u32[]{:S(2)}) collective-permute-start(bf16[528,2048]{1,0:T(8,128)(2,1)} %pad_maximum_fusion.4), channel_id=1, source_target_pairs={{0,1},{1,0},{2,3},{3,2},{4,5},{5,4},{6,7},{7,6},{8,9},{9,8},{10,11... | collective-permute-start | bytes 6488072 | tf_op jit(solution)/shard_map/ppermute | solution.py:569
  478.0 75.9 %all-to-all-start.2 = ((bf16[16,656,128]{2,1,0:T(8,128)(2,1)}), bf16[16,656,128]{2,1,0:T(8,128)(2,1)}, u32[]{:S(2)}, u32[]{:S(2)}) async-start(bf16[16,656,128]{2,1,0:T(8,128)(2,1)} %pad_maximum_fusion.1), calls=%async_computation.3 | async-start | bytes 5373952 | tf_op jit(solution)/shard_map/all_to_all | solution.py:573
  486.8 171.8 %reduce-scatter.2.cloned.1.call-start = ((), (), s32[]{:S(2)}) async-start(), calls=%async_computation.5 | async-start | bytes 4456448 | tf_op jit(solution)/shard_map/reduce_scatter | solution.py:838
  564.2 114.8 %all-to-all-start.3 = ((bf16[16,64,896]{2,1,0:T(8,128)(2,1)}), bf16[16,64,896]{2,1,0:T(8,128)(2,1)S(1)}, u32[]{:S(2)}, u32[]{:S(2)}) async-start(bf16[16,64,896]{2,1,0:T(8,128)(2,1)} %add_convert_fusion.1), calls=%async_computation.4 | async-start | bytes 3670016 | tf_op jit(solution)/shard_map/all_to_all | solution.py:573
  594.6 37.0 %collective-permute-start.79 = (bf16[8,64,256]{2,1,0:T(8,128)(2,1)}, bf16[8,64,256]{2,1,0:T(8,128)(2,1)S(1)}, u32[]{:S(2)}, u32[]{:S(2)}) collective-permute-start(bf16[8,64,256]{2,1,0:T(8,128)(2,1)} %constant_dynamic-slice_fusion), channel_id=1, source_target_pairs={{0,1},{1,0},{2,3},{3,2},{4,5},{5,4},{6,7},{7,6},{8,9},{9,8},{10,11... | collective-permute-start | bytes 786440 | tf_op jit(solution)/shard_map/ppermute | solution.py:569
  607.3 41.0 %collective-permute-start.71 = (bf16[96,2048]{1,0:T(8,128)(2,1)}, bf16[96,2048]{1,0:T(8,128)(2,1)}, u32[]{:S(2)}, u32[]{:S(2)}) collective-permute-start(bf16[96,2048]{1,0:T(8,128)(2,1)} %get-tuple-element.199), channel_id=1, source_target_pairs={{0,2},{2,0},{4,6},{6,4},{8,10},{10,8},{12,14},{14,12},{16,18},{18,... | collective-permute-start | bytes 1179656 | tf_op jit(solution)/shard_map/ppermute | solution.py:565
  607.8 40.5 %collective-permute-start.69 = (bf16[96,2048]{1,0:T(8,128)(2,1)}, bf16[96,2048]{1,0:T(8,128)(2,1)}, u32[]{:S(2)}, u32[]{:S(2)}) collective-permute-start(bf16[96,2048]{1,0:T(8,128)(2,1)} %get-tuple-element.200), channel_id=1, source_target_pairs={{0,4},{2,6},{4,0},{6,2},{8,12},{10,14},{12,8},{14,10},{16,20},{18,... | collective-permute-start | bytes 1179656 | tf_op jit(solution)/shard_map/ppermute | solution.py:565
  627.8 28.3 %collective-permute-start.68 = (bf16[64,2048]{1,0:T(8,128)(2,1)}, bf16[64,2048]{1,0:T(8,128)(2,1)}, u32[]{:S(2)}, u32[]{:S(2)}) collective-permute-start(bf16[64,2048]{1,0:T(8,128)(2,1)} %pad_maximum_fusion.19), channel_id=1, source_target_pairs={{0,4},{2,6},{4,0},{6,2},{8,12},{10,14},{12,8},{14,10},{16,20},{18,... | collective-permute-start | bytes 786440 | tf_op jit(solution)/shard_map/ppermute | solution.py:565
  628.9 27.2 %collective-permute-start.66 = (bf16[64,2048]{1,0:T(8,128)(2,1)}, bf16[64,2048]{1,0:T(8,128)(2,1)}, u32[]{:S(2)}, u32[]{:S(2)}) collective-permute-start(bf16[64,2048]{1,0:T(8,128)(2,1)} %pad_maximum_fusion.18), channel_id=1, source_target_pairs={{0,2},{2,0},{4,6},{6,4},{8,10},{10,8},{12,14},{14,12},{16,18},{18,... | collective-permute-start | bytes 786440 | tf_op jit(solution)/shard_map/ppermute | solution.py:565
  685.3 23.7 %collective-permute-start.74 = (bf16[64,2048]{1,0:T(8,128)(2,1)}, bf16[64,2048]{1,0:T(8,128)(2,1)}, u32[]{:S(2)}, u32[]{:S(2)}) collective-permute-start(bf16[64,2048]{1,0:T(8,128)(2,1)} %get-tuple-element.256), channel_id=1, source_target_pairs={{0,16},{2,18},{4,20},{6,22},{8,24},{10,26},{12,28},{14,30},{16,0},... | collective-permute-start | bytes 786440 | tf_op jit(solution)/shard_map/ppermute | solution.py:565
  690.9 24.3 %collective-permute-start.77 = (bf16[8,64,896]{2,1,0:T(8,128)(2,1)}, bf16[8,64,896]{2,1,0:T(8,128)(2,1)S(1)}, u32[]{:S(2)}, u32[]{:S(2)}) collective-permute-start(bf16[8,64,896]{2,1,0:T(8,128)(2,1)} %constant_dynamic-slice_fusion.2), channel_id=1, source_target_pairs={{0,1},{1,0},{2,3},{3,2},{4,5},{5,4},{6,7},{7,6},{8,9},{9,8},{10,11... | collective-permute-start | bytes 2752520 | tf_op jit(solution)/shard_map/ppermute | solution.py:569
  (100 other events, 1209.5 us)
Sparse Core Ops, SparseCore 0:
  119.6 115.8 all-gather.2
  491.3 167.3 reduce-scatter.1

commit v3 on v2

--- a/solution.py
+++ b/solution.py
@@ -16,7 +16,7 @@
 PACK = LOGIT + 128
 MIXED = 2 * KEY_SIZE + DV
 SCALE = KEY_SIZE**-0.5
-UNROLL = 4
+UNROLL = 16
 
 
 def mm(a, b, dims=((1,), (0,))):
@@ -109,6 +109,13 @@
     head_gain,
     gated_own,
     gated_other,
+    mixer_to,
+    mixed_to,
+    inverse_to,
+    state_to,
+    fresh_to,
+    carry_to,
+    read_to,
     mixer_out,
     mixed_out,
     inverse_out,
@@ -122,11 +129,31 @@
     add_part,
     pre,
     gated,
+    marks,
 ):
     blocks = decay_grid.shape[0]
     half = pre_own.shape[0]
-    pre[:half] = pre_own[...]
-    pre[half:] = pre_other[...]
+    loads = [
+        pltpu.make_async_copy(pre_own, pre.at[:half], marks.at[0]),
+        pltpu.make_async_copy(pre_other, pre.at[half:], marks.at[1]),
+    ]
+    prepared = [
+        pltpu.make_async_copy(mixed_out, mixed_to, marks.at[2]),
+        pltpu.make_async_copy(inverse_out, inverse_to, marks.at[3]),
+        pltpu.make_async_copy(carry_out, carry_to, marks.at[4]),
+        pltpu.make_async_copy(read_out, read_to, marks.at[5]),
+    ]
+    chained = [pltpu.make_async_copy(state_out, state_to, marks.at[6])]
+    finished = [
+        pltpu.make_async_copy(gated.at[:half], gated_own, marks.at[7]),
+        pltpu.make_async_copy(gated.at[half:], gated_other, marks.at[8]),
+        pltpu.make_async_copy(mixer_out, mixer_to, marks.at[9]),
+        pltpu.make_async_copy(fresh_out, fresh_to, marks.at[10]),
+    ]
+    for copy in loads:
+        copy.start()
+    for copy in loads:
+        copy.wait()
     strict, levels, eye = block_masks()
     key_eye = (
         lax.broadcasted_iota(jnp.int32, (KEY_SIZE, KEY_SIZE), 0)
@@ -178,12 +205,16 @@
         return 0
 
     lax.fori_loop(0, blocks // UNROLL, prepare, 0)
+    for copy in prepared:
+        copy.start()
 
     def chain(b, state):
         state_out[b] = state.astype(BF16)
         return mm_both(carry_out[b], state) + add_part[b]
 
     lax.fori_loop(0, blocks, chain, jnp.zeros((KEY_SIZE, DV), F32))
+    for copy in chained:
+        copy.start()
 
     def finish(group, _):
         for lane in range(UNROLL):
@@ -202,8 +233,10 @@
         return 0
 
     lax.fori_loop(0, blocks // UNROLL, finish, 0)
-    gated_own[...] = gated[:half]
-    gated_other[...] = gated[half:]
+    for copy in finished:
+        copy.start()
+    for copy in prepared + chained + finished:
+        copy.wait()
 
 
 def backward_kernel(
@@ -216,6 +249,17 @@
     cols,
     taps,
     head_gain,
+    mixer_from,
+    mixed_from,
+    inverse_from,
+    state_from,
+    fresh_from,
+    carry_from,
+    read_from,
+    d_pre_own,
+    d_pre_other,
+    grad_taps,
+    grad_gain,
     mixer_out,
     mixed_in,
     inverse_in,
@@ -223,24 +267,48 @@
     fresh_in,
     carry_in,
     read_in,
-    d_pre_own,
-    d_pre_other,
-    grad_taps,
-    grad_gain,
     d_out,
     pull_part,
     end_state,
     d_mixed,
     d_gated,
     pre,
-    d_pre,
+    d_main,
+    d_gating,
+    d_logits,
+    marks,
 ):
     blocks = decay_grid.shape[0]
     half = pre_own.shape[0]
-    pre[:half] = pre_own[...]
-    pre[half:] = pre_other[...]
-    d_gated[:half] = d_gated_own[...]
-    d_gated[half:] = d_gated_other[...]
+    first_loads = [
+        pltpu.make_async_copy(pre_own, pre.at[:half], marks.at[0]),
+        pltpu.make_async_copy(pre_other, pre.at[half:], marks.at[1]),
+        pltpu.make_async_copy(d_gated_own, d_gated.at[:half], marks.at[2]),
+        pltpu.make_async_copy(d_gated_other, d_gated.at[half:], marks.at[3]),
+        pltpu.make_async_copy(mixer_from, mixer_out, marks.at[4]),
+        pltpu.make_async_copy(read_from, read_in, marks.at[5]),
+    ]
+    chain_loads = [pltpu.make_async_copy(carry_from, carry_in, marks.at[6])]
+    late_loads = [
+        pltpu.make_async_copy(mixed_from, mixed_in, marks.at[7]),
+        pltpu.make_async_copy(inverse_from, inverse_in, marks.at[8]),
+        pltpu.make_async_copy(state_from, state_in, marks.at[9]),
+        pltpu.make_async_copy(fresh_from, fresh_in, marks.at[10]),
+    ]
+
+    def stores(source, columns, mark):
+        return [
+            pltpu.make_async_copy(source.at[:half], d_pre_own.at[:, columns], marks.at[mark]),
+            pltpu.make_async_copy(source.at[half:], d_pre_other.at[:, columns], marks.at[mark + 1]),
+        ]
+
+    gating_stores = stores(d_gating, slice(MIXED, LOGIT), 11)
+    logit_stores = stores(d_logits, slice(LOGIT, PACK), 13)
+    main_stores = stores(d_main, slice(0, MIXED), 15)
+    for copy in first_loads + chain_loads + late_loads:
+        copy.start()
+    for copy in first_loads:
+        copy.wait()
     strict, _, _ = block_masks()
     lane_index = lax.broadcasted_iota(jnp.int32, (BLOCK, PACK - LOGIT), 1)
     grad_taps[...] = jnp.zeros_like(grad_taps)
@@ -264,7 +332,7 @@
             along = jnp.mean(pulled * normed, axis=-1, keepdims=True)
             low = (scale * (pulled - normed * along)).astype(BF16)
             grad_gain[...] += row_sums(grad * normed * act)
-            d_pre[there, MIXED:LOGIT] = (
+            d_gating[there, :] = (
                 weighted * normed * (sig * (1.0 + gate * (1.0 - sig)))
             ).astype(BF16)
             d_out[here, :] = low
@@ -272,6 +340,10 @@
         return 0
 
     lax.fori_loop(0, blocks // UNROLL, prepare, 0)
+    for copy in gating_stores:
+        copy.start()
+    for copy in chain_loads:
+        copy.wait()
 
     def chain(step, state):
         b = blocks - 1 - step
@@ -279,6 +351,8 @@
         return mm_both(carry_in[b], state, TN) + pull_part[b]
 
     lax.fori_loop(0, blocks, chain, jnp.zeros((KEY_SIZE, DV), F32))
+    for copy in late_loads:
+        copy.wait()
 
     def finish(group, _):
         for lane in range(UNROLL):
@@ -323,10 +397,12 @@
                 d_key - key_unit * jnp.sum(key_unit * d_key, axis=-1, keepdims=True)
             ) * (key_scale * slope[:, KEY_SIZE : 2 * KEY_SIZE])
             d_mixed[here, 2 * KEY_SIZE :] = d_right_low.astype(F32) * slope[:, 2 * KEY_SIZE :]
-            d_pre[there, LOGIT:] = jnp.where(lane_index == 0, d_logit, 0.0).astype(BF16)
+            d_logits[there, :] = jnp.where(lane_index == 0, d_logit, 0.0).astype(BF16)
         return 0
 
     lax.fori_loop(0, blocks // UNROLL, finish, 0)
+    for copy in logit_stores:
+        copy.start()
 
     def unmix(group, _):
         for lane in range(UNROLL):
@@ -342,17 +418,21 @@
                 moved = pltpu.roll(kept, BLOCK + 8 - lag, 0)[:BLOCK]
                 total = total + taps[lag : lag + 1] * moved
                 grad_taps[lag] += row_sums(current * moved)
-            d_pre[there, :MIXED] = total.astype(BF16)
+            d_main[there, :] = total.astype(BF16)
         return 0
 
     lax.fori_loop(0, blocks // UNROLL, unmix, 0)
-    d_pre_own[...] = d_pre[:half]
-    d_pre_other[...] = d_pre[half:]
+    for copy in main_stores:
+        copy.start()
+    for copy in gating_stores + logit_stores + main_stores:
+        copy.wait()
 
 
 VMEM_SPEC = pl.BlockSpec(memory_space=pltpu.VMEM)
 SMEM_SPEC = pl.BlockSpec(memory_space=pltpu.SMEM)
-KERNEL_COST = pl.CostEstimate(flops=30_000_000_000, bytes_accessed=100_000_000, transcendentals=0)
+ANY_SPEC = pl.BlockSpec(memory_space=pl.ANY)
+FORWARD_COST = pl.CostEstimate(flops=30_000_000_000, bytes_accessed=100_000_000, transcendentals=0)
+BACKWARD_COST = pl.CostEstimate(flops=1_000_000, bytes_accessed=1_000, transcendentals=0)
 
 
 def mixer_forward(place, pre_own, pre_other, decay_grid, cols, rows, taps, head_gain):
@@ -372,18 +452,26 @@
             shape((blocks, KEY_SIZE, KEY_SIZE), F32),
             shape((tokens, KEY_SIZE), BF16),
         ),
-        in_specs=[SMEM_SPEC] + [VMEM_SPEC] * 7,
-        out_specs=[VMEM_SPEC] * 9,
+        in_specs=[SMEM_SPEC] + [ANY_SPEC] * 2 + [VMEM_SPEC] * 5,
+        out_specs=[ANY_SPEC] * 9,
         scratch_shapes=[
+            pltpu.VMEM((tokens, DV), F32),
+            pltpu.VMEM((tokens, MIXED), F32),
+            pltpu.VMEM((tokens, BLOCK), F32),
+            pltpu.VMEM((blocks, KEY_SIZE, DV), BF16),
+            pltpu.VMEM((tokens, DV), BF16),
+            pltpu.VMEM((blocks, KEY_SIZE, KEY_SIZE), F32),
+            pltpu.VMEM((tokens, KEY_SIZE), BF16),
             pltpu.VMEM((blocks, 2 * BLOCK, KEY_SIZE), BF16),
             pltpu.VMEM((tokens, DV), F32),
             pltpu.VMEM((tokens, DV), F32),
             pltpu.VMEM((blocks, KEY_SIZE, DV), F32),
             pltpu.VMEM((tokens, PACK), BF16),
             pltpu.VMEM((tokens, DV), BF16),
+            pltpu.SemaphoreType.DMA((11,)),
         ],
         compiler_params=pltpu.CompilerParams(vmem_limit_bytes=52 * 1024 * 1024),
-        cost_estimate=KERNEL_COST,
+        cost_estimate=FORWARD_COST,
         name="mixer_forward",
     )(place, pre_own, pre_other, decay_grid, cols, rows, taps, head_gain)
 
@@ -400,19 +488,29 @@
             shape((CONV, 8, MIXED), F32),
             shape((8, DV), F32),
         ),
-        in_specs=[SMEM_SPEC] + [VMEM_SPEC] * 15,
-        out_specs=[VMEM_SPEC] * 4,
+        in_specs=[SMEM_SPEC] + [ANY_SPEC] * 4 + [VMEM_SPEC] * 4 + [ANY_SPEC] * 7,
+        out_specs=[ANY_SPEC] * 2 + [VMEM_SPEC] * 2,
         scratch_shapes=[
+            pltpu.VMEM((tokens, DV), F32),
+            pltpu.VMEM((tokens, MIXED), F32),
+            pltpu.VMEM((tokens, BLOCK), F32),
+            pltpu.VMEM((blocks, KEY_SIZE, DV), BF16),
+            pltpu.VMEM((tokens, DV), BF16),
+            pltpu.VMEM((blocks, KEY_SIZE, KEY_SIZE), F32),
+            pltpu.VMEM((tokens, KEY_SIZE), BF16),
             pltpu.VMEM((tokens, DV), BF16),
             pltpu.VMEM((blocks, KEY_SIZE, DV), F32),
             pltpu.VMEM((blocks, KEY_SIZE, DV), BF16),
             pltpu.VMEM((tokens + 8, MIXED), F32),
             pltpu.VMEM((tokens, DV), BF16),
             pltpu.VMEM((tokens, PACK), BF16),
-            pltpu.VMEM((tokens, PACK), BF16),
+            pltpu.VMEM((tokens, MIXED), BF16),
+            pltpu.VMEM((tokens, DV), BF16),
+            pltpu.VMEM((tokens, PACK - LOGIT), BF16),
+            pltpu.SemaphoreType.DMA((17,)),
         ],
         compiler_params=pltpu.CompilerParams(vmem_limit_bytes=52 * 1024 * 1024),
-        cost_estimate=KERNEL_COST,
+        cost_estimate=BACKWARD_COST,
         name="mixer_backward",
     )(place, *d_gated, *pre, decay_grid, cols, taps, head_gain, *kept)
 
@@ -544,6 +642,31 @@
     )(core, gain, w_query, w_key, w_value, w_gating, w_beta, w_output, rates, starts)
 
 
+def join_kernel(*refs):
+    *pieces, out = refs
+    start = 0
+    for piece in pieces:
+        out[start : start + piece.shape[0]] = piece[...]
+        start += piece.shape[0]
+
+
+def joined_rows(pieces):
+    rows, width = sum(piece.shape[0] for piece in pieces), pieces[0].shape[1]
+    steps = 2
+
+    def block(size):
+        return pl.BlockSpec((size, width // steps), lambda step: (0, step))
+
+    return pl.pallas_call(
+        join_kernel,
+        out_shape=jax.ShapeDtypeStruct((rows, width), pieces[0].dtype),
+        grid=(steps,),
+        in_specs=[block(piece.shape[0]) for piece in pieces],
+        out_specs=block(rows),
+        name="joined_rows",
+    )(*pieces)
+
+
 CHIPS = 16
 CORES = 2
 BOTH = ("seq", "head")
@@ -593,53 +716,40 @@
 
 
 def gather_near(levels):
-    blocks = [levels[0], stacked(levels[1:])]
-    return [(block, send(block, along_x), send(block, along_y)) for block in blocks]
+    block = stacked(levels)
+    return block, send(block, along_x), send(block, along_y)
 
 
 def gather_far(near):
-    own, others = [
-        (
-            [block],
-            [from_x],
-            [from_y],
-            [
-                send(from_y[: block.shape[0] // 2], along_x),
-                send(from_x[block.shape[0] // 2 :], along_y),
-            ],
-        )
-        for block, from_x, from_y in near
+    _, from_x, from_y = near
+    half = from_x.shape[0] // 2
+    return near + (send(from_y[:half], along_x), send(from_x[half:], along_y))
+
+
+def gather_rows(block):
+    return stacked(gather_far(gather_near(gather_levels(block))))
+
+
+def scatter_far(parts):
+    rows = parts.shape[0] // 8
+    return parts, send(parts[6 * rows : 7 * rows], along_x), send(parts[7 * rows :], along_y)
+
+
+def scatter_near(begun):
+    parts, low, high = begun
+    rows = parts.shape[0] // 8
+    for_x = stacked([parts[2 * rows : 3 * rows], total_of(parts[3 * rows : 4 * rows], high).astype(BF16)])
+    for_y = stacked([total_of(parts[4 * rows : 5 * rows], low).astype(BF16), parts[5 * rows : 6 * rows]])
+    return parts[: 2 * rows], send(for_x, along_x), send(for_y, along_y)
+
+
+def scatter_levels(near):
+    own, from_x, from_y = near
+    total = total_of(own, from_x, from_y)
+    rows = total.shape[0] // 4
+    return [total[:rows]] + [
+        send(total[j * rows : (j + 1) * rows].astype(BF16), along_z(-j)) for j in (1, 2, 3)
     ]
-    return stacked([piece for pair in zip(own, others) for part in pair for piece in part])
-
-
-def scatter_begin(parts):
-    rows = parts.shape[0] // CHIPS
-    groups = []
-    for first, last in ((0, 1), (1, 4)):
-        own, for_x, for_y, far = [
-            parts[(4 * plane + first) * rows : (4 * plane + last) * rows] for plane in range(4)
-        ]
-        half = far.shape[0] // 2
-        groups.append(
-            (own, for_x, for_y, send(far[:half], along_x), send(far[half:], along_y))
-        )
-    return groups
-
-
-def scatter_near(groups):
-    totals = []
-    for own, for_x, for_y, low, high in groups:
-        half = own.shape[0] // 2
-        for_y = stacked([total_of(for_y[:half], low).astype(BF16), for_y[half:]])
-        for_x = stacked([for_x[:half], total_of(for_x[half:], high).astype(BF16)])
-        totals.append(total_of(own, send(for_x, along_x), send(for_y, along_y)))
-    return totals[0], totals[1].astype(BF16)
-
-
-def scatter_levels(own, away):
-    rows = own.shape[0]
-    return [own] + [send(away[(j - 1) * rows : j * rows], along_z(-j)) for j in (1, 2, 3)]
 
 
 def nn(a, b):
@@ -721,8 +831,9 @@
     in_payload = in_order(in_kept, swap_cores(in_given), 0)
     one_levels = gather_levels(normed_one.astype(BF16))
     in_mine = exchange(after(in_payload, one_levels))
-    normed_all = gather_far(gather_near(one_levels))
-    in_mine = after(in_mine, normed_all)
+    one_near = gather_near(one_levels)
+    in_mine = after(in_mine, one_near)
+    normed_all = stacked(gather_far(one_near))
     weights_all = joined_by_core(in_mine)
     weights_in, weights_out = weights_all[:, :PACK], weights_all[:, PACK:]
 
@@ -768,20 +879,18 @@
         ],
         axis=1,
     )
-    feed = after(feed, normed_all, weights_in, cols)
+    feed = after(feed, in_mine)
     feed_mine = exchange(feed)
-    cot_own = own_rows(cotangent)
-    cot_gathered = lax.all_gather(cot_own, "seq", axis=0, tiled=False)
     gated_own, gated_other, *kept = mixer_forward(place, *pre, decay_grid, cols, rows, taps, gain_head)
     mixed_parts = nt(gated_own, weights_out).astype(BF16)
-    mixed_sums = scatter_begin(mixed_parts)
-
-    mixed_sums = scatter_near(mixed_sums)
-    feed_mine, normed_late, cot_all = after((feed_mine, normed_all, cot_gathered), mixed_sums)
-    relative = jnp.arange(CHIPS)
-    order = 4 * ((chip // 4 - relative % 4) % 4) + ((chip % 4) ^ (relative // 4))
-    cot_all = cot_all.at[order].get(mode="promise_in_bounds").reshape(own_count, width)
+    mixed = scatter_far(mixed_parts)
+
+    cot_own = own_rows(cotangent)
+    mixed, cot, feed_mine = after((mixed, cot_own, feed_mine))
+    mixed, cot = scatter_near(mixed), gather_levels(cot)
     feed_other = swap_cores(feed_mine)
+    mixed, cot, normed_late = after((mixed, cot, normed_all))
+    mixed, cot = scatter_levels(mixed), gather_near(cot)
 
     def unit_rows(position):
         return stacked(
@@ -797,13 +906,19 @@
     cut_given = lax.dynamic_index_in_dim(cut, 1 - core, 2, False).reshape(own_count, width // CORES)
     cut_other = swap_cores(cut_given)
 
-    d_hidden = nt(cot_all, down_rows).astype(BF16)
-    middle = inputs_own + total_of(*scatter_levels(*mixed_sums))
+    mixed, cot = after((mixed, cot))
+    middle = inputs_own + total_of(*mixed)
     scale_two = lax.rsqrt(jnp.mean(middle * middle, axis=-1, keepdims=True) + EPSILON)
     normed_mid = middle * scale_two
-    levels = gather_levels(normed_mid.astype(BF16))
-    levels[1:] = after(levels[1:], gate_rows, up_rows, d_hidden, cut_mine, cut_other)
-    mid_all = gather_far(gather_near(levels))
+    mid, cot = gather_levels(normed_mid.astype(BF16)), gather_far(cot)
+    mid, cot, gate_rows, up_rows, down_rows, cut_mine, cut_other = after(
+        (mid, cot, gate_rows, up_rows, down_rows, cut_mine, cut_other)
+    )
+    mid = gather_near(mid)
+    cot_all = stacked(cot)
+    d_hidden = nt(cot_all, down_rows).astype(BF16)
+    mid, d_hidden = after((mid, d_hidden))
+    mid_all = stacked(gather_far(mid))
 
     gate_lin = nt(mid_all, gate_rows)
     up_lin = nt(mid_all, up_rows)
@@ -813,29 +928,29 @@
     hidden = (act * up_lin).astype(BF16)
     d_gate = (d_hidden * up_lin * (sig * (1.0 + gate_lin * (1.0 - sig)))).astype(BF16)
     d_up = (d_hidden * act).astype(BF16)
-    e_sums = scatter_near(scatter_begin((nn(d_gate, gate_rows) + nn(d_up, up_rows)).astype(BF16)))
-
-    feed_parts = after(nn(hidden, down_rows).astype(BF16), e_sums)
-    e_two = total_of(*scatter_levels(*e_sums))
-    d_middle = cot_own.astype(F32) + scale_two * (
-        e_two - normed_mid * jnp.mean(e_two * normed_mid, axis=-1, keepdims=True)
-    )
-    levels = gather_levels(d_middle.astype(BF16))
+    e_mid = scatter_far((nn(d_gate, gate_rows) + nn(d_up, up_rows)).astype(BF16))
+    feed_parts = nn(after(hidden, e_mid[0]), down_rows).astype(BF16)
+    e_mid, feed_parts = after((e_mid, feed_parts))
+    e_mid = scatter_near(e_mid)
 
     parts = [tn(d_gate, mid_all), tn(d_up, mid_all), tn(hidden, cot_all)]
     keep_part = stacked([part[:units] for part in parts])
     give_part = stacked([part[units:] for part in parts]).astype(BF16)
+    e_mid, feed_out, keep_part, give_part = after((e_mid, feed_parts, keep_part, give_part))
+    e_mid, feed_out = scatter_levels(e_mid), scatter_far(feed_out)
+    e_mid, feed_out = after((e_mid, feed_out))
+    e_two = total_of(*e_mid)
+    d_middle = cot_own.astype(F32) + scale_two * (
+        e_two - normed_mid * jnp.mean(e_two * normed_mid, axis=-1, keepdims=True)
+    )
+    d_mid, feed_out = gather_levels(d_middle.astype(BF16)), scatter_near(feed_out)
     feed_grad = (keep_part + swap_cores(give_part).astype(F32)).astype(BF16)
     feed_grad = feed_grad.reshape(3 * units, CHIPS, row_count).transpose(1, 0, 2)
     feed_grad = jnp.pad(feed_grad, ((0, 0), (0, half_count * DV // row_count), (0, 0)))
-    levels[1:] = after(levels[1:], feed_grad)
-    seats = jnp.arange(CHIPS)
-    seat = 4 * ((seats % 4) ^ (chip % 4)) + (chip // 4 - seats // 4) % 4
-    feed_parts = feed_parts.reshape(CHIPS, half_rows, width)
-    feed_parts = feed_parts.at[seat].get(mode="promise_in_bounds").reshape(own_count, width)
-    near = after(gather_near(levels), feed_parts)
-    d_mid_all = gather_far(near)
-    feed_out = lax.psum_scatter(after(feed_parts, d_mid_all), "seq", scatter_dimension=0, tiled=True)
+    d_mid, feed_out, feed_grad = after((d_mid, feed_out, feed_grad))
+    d_mid, feed_out = gather_near(d_mid), scatter_levels(feed_out)
+    d_mid, feed_out = after((d_mid, feed_out))
+    d_mid_all = stacked(gather_far(d_mid))
 
     d_gated_own = nn(d_mid_all, weights_out).astype(BF16)
     d_gated = (d_gated_own, swap_cores(d_gated_own))
@@ -852,8 +967,6 @@
         place, d_gated, pre, decay_grid, cols, taps, gain_head, kept
     )
 
-    d_pre_own, d_pre_other, feed_back = after((d_pre_own, d_pre_other, feed_back))
-
 
     small = jnp.concatenate([jnp.sum(grad_taps, axis=1).reshape(-1), jnp.sum(grad_gain, axis=0)])
     small = small.reshape(-1, 64)
@@ -861,10 +974,11 @@
     grad_in = tn(cut_mine, d_pre_own) + tn(cut_other, d_pre_other)
     small = jnp.pad(small, ((0, half_count - small_rows), (PACK - 64, 0)))
     grad_in = (grad_in.reshape(CHIPS, half_count, PACK) + small).astype(BF16)
+    grad_in, feed_back = after((grad_in, feed_back))
     e_parts = nt(after(d_pre_own, grad_in), weights_in).astype(BF16)
     grad_in = exchange(grad_in)
-    e_sums = scatter_near(scatter_begin(e_parts))
-    e_sums, grad_in = after((e_sums, grad_in))
+    e_sums = scatter_near(scatter_far(e_parts))
+    e_sums, grad_in, feed_back = after((e_sums, grad_in, feed_back))
     small = grad_in[:, :small_rows, PACK - 64 :].astype(F32).reshape(CHIPS, -1)
     taps_all = lax.dynamic_slice_in_dim(small[:, : CONV * MIXED], core * head_count, head_count, 0)
     taps_all = taps_all.reshape(head_count, CONV, MIXED).transpose(1, 0, 2)
@@ -875,13 +989,9 @@
         return in_order(mine, swap_cores(given), 1)
 
     grad_in = heads_here(grad_in)
-    block_out_own = (middle + feed_out.astype(F32)).astype(BF16)
+    block_out_own = (middle + total_of(*feed_out)).astype(BF16)
     block_out = in_order(block_out_own, swap_cores(block_out_own), 0)
-    e_one = total_of(*scatter_levels(*e_sums))
-    grad_own = d_middle + scale_one * (
-        e_one - normed_one * jnp.mean(e_one * normed_one, axis=-1, keepdims=True)
-    )
-    grad_inputs = in_order(grad_own, swap_cores(grad_own), 0)
+    e_levels = scatter_levels(e_sums)
 
     grad_out = heads_here(feed_back[:, 3 * units :].reshape(CHIPS, half_count, DV))
     grad_output = grad_out.astype(F32).transpose(0, 2, 1).reshape(head_count * DV, row_count)
@@ -897,9 +1007,7 @@
     gain_parts = jnp.stack([mixer_gain_part, feed_gain_part])
     gain_totals = gain_parts + swap_cores(gain_parts)
 
-    return (
-        block_out,
-        grad_inputs,
+    others = (
         gain_totals[0],
         raw_query,
         raw_key,
@@ -916,6 +1024,13 @@
         raw_up * gain_two,
         grad_down,
     )
+    e_levels, block_out, others = after((e_levels, block_out, others))
+    e_one = total_of(*e_levels)
+    grad_own = d_middle + scale_one * (
+        e_one - normed_one * jnp.mean(e_one * normed_one, axis=-1, keepdims=True)
+    )
+    grad_inputs = in_order(grad_own, swap_cores(grad_own), 0)
+    return (block_out, grad_inputs) + others
 
 
 EXACT_PRECISION = lax.Precision.HIGHEST

time: 738 us -> 664 us (0.90)
  waiting for transfers between devices: 293 us -> 272 us
  Pallas kernels: 92.1 us -> 75.7 us
  between operations: 16.1 us -> 2.6 us
  local copies, waits for them, and re-layouts: 91.8 us -> 78.4 us
    all_to_all x4, waiting for transfers between devices: 15.2 us -> 0.01 us  [exchange(): lax.all_to_all(pieces, 'seq', split_axis=0, concat_axis=0, tiled=True)]
    pallas_call x1, Pallas kernels: 42.9 us -> 32.4 us  [mixer_forward(): pl.pallas_call(forward_kernel, out_shape=(shape((half, DV), BF16), shape(...]
    gather x2 -> x0, local copies, waits for them, and re-layouts: 10.1 us -> none  [the longest x1 5.06 us: head_plan(): cot_all.at[order].get(mode='promise_in_bounds').reshape(own_count, width)]
    all_to_all x4, starting transfers between devices: 49.3 us -> 40.1 us  [exchange(): lax.all_to_all(pieces, 'seq', split_axis=0, concat_axis=0, tiled=True)]
    ppermute x66 -> x56, waiting for transfers between devices: 275 us -> 266 us  [send(): lax.ppermute(value, 'seq', [(index, target(index)) for index in range(CHI...]
    ppermute x66 -> x56, starting transfers between devices: 81.9 us -> 88.5 us  [send(): lax.ppermute(value, 'seq', [(index, target(index)) for index in range(CHI...]
    unnamed x131 -> x163, local copies, waits for them, and re-layouts: 43 us -> 39.4 us
  transfers between devices with their start and end apart: 86 -> 74, of which waited for: 39 -> 36; matrix products, arithmetic and copies ran while one was open for 21% -> 18% of each run, Pallas kernels for 12% -> 11%
where the time goes in v3:
time: 664 us; the launch traced here: 651 us
  waiting for transfers between devices  272 us (41%)
  starting transfers between devices  130 us (20%)
  local copies, waits for them, and re-layouts  78.4 us (12%)
  Pallas kernels  75.7 us (11%)
  other arithmetic  46.5 us (7%)
  matrix products  45.5 us (7%)
    ppermute x56, waiting for transfers between devices, send(): lax.ppermute(value, 'seq', [(index, target(index)) for index in range(CHI...  266 us
    ppermute x56, starting transfers between devices, send(): lax.ppermute(value, 'seq', [(index, target(index)) for index in range(CHI...  88.5 us
    dot_general x16, matrix products, mm(): return lax.dot_general(a, b, (dims, ((), ())), preferred_element_type=F32)  45.5 us
    all_to_all x4, starting transfers between devices, exchange(): lax.all_to_all(pieces, 'seq', split_axis=0, concat_axis=0, tiled=True)  40.1 us
    pallas_call x1, Pallas kernels, mixer_backward(): pl.pallas_call(backward_kernel, out_shape=(shape((half, PACK), BF16), sha...  39.7 us
    unnamed x163, local copies, waits for them, and re-layouts  39.4 us
    pallas_call x1, Pallas kernels, mixer_forward(): pl.pallas_call(forward_kernel, out_shape=(shape((half, DV), BF16), shape(...  32.4 us
  transfers between devices with their start and end apart: 74, of which 36 were waited for; matrix products, arithmetic and copies ran while one was open for 18% of the time, Pallas kernels for 11%

profile of v3, /device:TPU:0, one launch (start us, length us, event | category | flops | bytes accessed | tf_op | source)
XLA Modules:
  0.0 650.9 jit_solution(13288066568906257229)
XLA Ops:
  11.6 4.6 collective-permute-start.2
  23.2 16.1 %collective-permute-done.1 = bf16[64,2048]{1,0:T(8,128)(2,1)S(1)} collective-permute-done((bf16[64,2048]{1,0:T(8,128)(2,1)}, bf16[64,2048]{1,0:T(8,128)(2,1)S(1)}, u32[]{:S(2)}, u32[]{:S(2)}) %collective-permute-start.1) | collective-permute-done | bytes 262176 | tf_op jit(solution)/shard_map/ppermute | solution.py:688
  39.4 6.1 all-to-all-start
  55.0 40.1 %collective-permute-done.4 = bf16[256,2048]{1,0:T(8,128)(2,1)} collective-permute-done((bf16[256,2048]{1,0:T(8,128)(2,1)}, bf16[256,2048]{1,0:T(8,128)(2,1)}, u32[]{:S(2)}, u32[]{:S(2)}) %collective-permute-start.4) | collective-permute-done | bytes 1048608 | tf_op jit(solution)/shard_map/ppermute | solution.py:688
  107.2 8.0 %collective-permute-done.5 = bf16[128,2048]{1,0:T(8,128)(2,1)S(1)} collective-permute-done((bf16[128,2048]{1,0:T(8,128)(2,1)S(1)}, bf16[128,2048]{1,0:T(8,128)(2,1)S(1)}, u32[]{:S(2)}, u32[]{:S(2)}) %collective-permute-start.5) | collective-permute-done | bytes 524320 | tf_op jit(solution)/shard_map/ppermute | solution.py:688
  119.7 5.7 fusion.pre_own
  125.4 8.5 %all-to-all-start.1 = ((bf16[16,528,128]{2,1,0:T(8,128)(2,1)}), bf16[16,528,128]{2,1,0:T(8,128)(2,1)}, u32[]{:S(2)}, u32[]{:S(2)}) async-start(bf16[16,528,128]{2,1,0:T(8,128)(2,1)} %pad_maximum_fusion.3), calls=%async_computation.1 | async-start | bytes 4325376 | tf_op jit(solution)/shard_map/all_to_all | solution.py:696
  137.2 32.4 %mixer_forward.1 = (bf16[1024,256]{1,0:T(8,128)(2,1)S(1)}, bf16[1024,256]{1,0:T(8,128)(2,1)}, f32[2048,256]{1,0:T(8,128)}, f32[2048,512]{1,0:T(8,128)}, f32[2048...) custom-call(s32[32]{0:T(128)S(1)} %fusion.32.place, ...), custom_call_target="tpu_custom_call" | custom-call | flops 30000001024 | bytes 100000000 | tf_op jit(solution)/shard_map/mixer_forward/pallas_call | solution.py:442
  178.5 11.0 %collective-permute-done.12 = bf16[128,2048]{1,0:T(8,128)(2,1)S(1)} collective-permute-done((bf16[128,2048]{1,0:T(8,128)(2,1)}, bf16[128,2048]{1,0:T(8,128)(2,1)S(1)}, u32[]{:S(2)}, u32[]{:S(2)}) %collective-permute-start.12) | collective-permute-done | bytes 524320 | tf_op jit(solution)/shard_map/ppermute | solution.py:688
  198.1 5.0 collective-permute-start.17
  205.3 4.6 collective-permute-done.17
  209.9 17.4 %collective-permute-done.16 = bf16[64,2048]{1,0:T(8,128)(2,1)} collective-permute-done((bf16[64,2048]{1,0:T(8,128)(2,1)S(1)}, bf16[64,2048]{1,0:T(8,128)(2,1)}, u32[]{:S(2)}, u32[]{:S(2)}) %collective-permute-start.16) | collective-permute-done | bytes 262176 | tf_op jit(solution)/shard_map/ppermute | solution.py:688
  240.7 7.1 %collective-permute-done.20 = bf16[64,2048]{1,0:T(8,128)(2,1)S(1)} collective-permute-done((bf16[64,2048]{1,0:T(8,128)(2,1)S(1)}, bf16[64,2048]{1,0:T(8,128)(2,1)S(1)}, u32[]{:S(2)}, u32[]{:S(2)}) %collective-permute-start.20) | collective-permute-done | bytes 262176 | tf_op jit(solution)/shard_map/ppermute | solution.py:688
  249.6 6.4 copy.122
  263.4 11.4 %collective-permute-start.25 = (bf16[64,2048]{1,0:T(8,128)(2,1)S(1)}, bf16[64,2048]{1,0:T(8,128)(2,1)S(1)}, u32[]{:S(2)}, u32[]{:S(2)}) collective-permute-start(bf16[64,2048]{1,0:T(8,128)(2,1)S(1)} %multiply_convert_fusion.1), channel_id=1, source_target_pairs={{0,24},{2,26},{4,28},{6,30},{8,0},{10,2},{12,4},{14,6},{16,8},{18,... | collective-permute-start | bytes 786440 | tf_op jit(solution)/shard_map/ppermute | solution.py:688
  282.6 14.6 %collective-permute-done.24 = bf16[64,2048]{1,0:T(8,128)(2,1)S(1)} collective-permute-done((bf16[64,2048]{1,0:T(8,128)(2,1)S(1)}, bf16[64,2048]{1,0:T(8,128)(2,1)S(1)}, u32[]{:S(2)}, u32[]{:S(2)}) %collective-permute-start.24) | collective-permute-done | bytes 262176 | tf_op jit(solution)/shard_map/ppermute | solution.py:688
  304.4 18.0 %collective-permute-done.31 = bf16[256,2048]{1,0:T(8,128)(2,1)S(1)} collective-permute-done((bf16[256,2048]{1,0:T(8,128)(2,1)S(1)}, bf16[256,2048]{1,0:T(8,128)(2,1)S(1)}, u32[]{:S(2)}, u32[]{:S(2)}) %collective-permute-start.31) | collective-permute-done | bytes 1048608 | tf_op jit(solution)/shard_map/ppermute | solution.py:688
  325.3 10.0 %collective-permute-done.32 = bf16[128,2048]{1,0:T(8,128)(2,1)S(1)} collective-permute-done((bf16[128,2048]{1,0:T(8,128)(2,1)S(1)}, bf16[128,2048]{1,0:T(8,128)(2,1)S(1)}, u32[]{:S(2)}, u32[]{:S(2)}) %collective-permute-start.32) | collective-permute-done | bytes 524320 | tf_op jit(solution)/shard_map/ppermute | solution.py:688
  366.8 15.5 %collective-permute-done.36 = bf16[256,2048]{1,0:T(8,128)(2,1)S(1)} collective-permute-done((bf16[256,2048]{1,0:T(8,128)(2,1)S(1)}, bf16[256,2048]{1,0:T(8,128)(2,1)S(1)}, u32[]{:S(2)}, u32[]{:S(2)}) %collective-permute-start.36) | collective-permute-done | bytes 1048608 | tf_op jit(solution)/shard_map/ppermute | solution.py:688
  396.2 7.4 %collective-permute-done.39 = bf16[64,2048]{1,0:T(8,128)(2,1)S(1)} collective-permute-done((bf16[64,2048]{1,0:T(8,128)(2,1)S(1)}, bf16[64,2048]{1,0:T(8,128)(2,1)S(1)}, u32[]{:S(2)}, u32[]{:S(2)}) %collective-permute-start.39) | collective-permute-done | bytes 262176 | tf_op jit(solution)/shard_map/ppermute | solution.py:688
  407.6 4.9 collective-permute-start.45
  419.2 12.8 %collective-permute-done.44 = bf16[64,2048]{1,0:T(8,128)(2,1)S(1)} collective-permute-done((bf16[64,2048]{1,0:T(8,128)(2,1)S(1)}, bf16[64,2048]{1,0:T(8,128)(2,1)S(1)}, u32[]{:S(2)}, u32[]{:S(2)}) %collective-permute-start.44) | collective-permute-done | bytes 262176 | tf_op jit(solution)/shard_map/ppermute | solution.py:688
  446.1 8.7 %collective-permute-done.52 = bf16[64,2048]{1,0:T(8,128)(2,1)S(1)} collective-permute-done((bf16[64,2048]{1,0:T(8,128)(2,1)S(1)}, bf16[64,2048]{1,0:T(8,128)(2,1)S(1)}, u32[]{:S(2)}, u32[]{:S(2)}) %collective-permute-start.52) | collective-permute-done | bytes 262176 | tf_op jit(solution)/shard_map/ppermute | solution.py:688
  457.5 7.7 %collective-permute-done.54 = bf16[128,2048]{1,0:T(8,128)(2,1)S(1)} collective-permute-done((bf16[128,2048]{1,0:T(8,128)(2,1)S(1)}, bf16[128,2048]{1,0:T(8,128)(2,1)S(1)}, u32[]{:S(2)}, u32[]{:S(2)}) %collective-permute-start.54) | collective-permute-done | bytes 524320 | tf_op jit(solution)/shard_map/ppermute | solution.py:688
  470.7 13.4 %all-to-all-start.2 = ((bf16[16,656,128]{2,1,0:T(8,128)(2,1)}), bf16[16,656,128]{2,1,0:T(8,128)(2,1)}, u32[]{:S(2)}, u32[]{:S(2)}) async-start(bf16[16,656,128]{2,1,0:T(8,128)(2,1)} %constant_dynamic-update-slice_fusion.35), calls=%async_computation.2 | async-start | bytes 5373952 | tf_op jit(solution)/shard_map/all_to_all | solution.py:696
  489.8 39.7 %mixer_backward.1 = (bf16[1024,896]{1,0:T(8,128)(2,1)}, bf16[1024,896]{1,0:T(8,128)(2,1)}, f32[4,8,512]{2,1,0:T(8,128)S(1)}, f32[8,256]{1,0:T(8,128)S(1)}) custom-call(s32[32]{0:T(128)S(1)} %fusion.32.place, bf16[1024,256]{1,0:T(8,128)(2,1)S(1)} %convolution_convert_fusion.5.d_gated_own, bf16[1024,256]{1,0:T(8,128)(2,1)S(1)} %collective-permute-done.56.d_gated_other, ...), custom_call_target="tpu_custom_call" | custom-call | flops 1000000 | bytes 1000 | tf_op jit(solution)/shard_map/mixer_backward/pallas_call | solution.py:483
  529.7 4.6 fusion.65
  538.3 12.2 %all-to-all-start.3 = ((bf16[16,64,896]{2,1,0:T(8,128)(2,1)}), bf16[16,64,896]{2,1,0:T(8,128)(2,1)S(1)}, u32[]{:S(2)}, u32[]{:S(2)}) async-start(bf16[16,64,896]{2,1,0:T(8,128)(2,1)} %add_convert_fusion.2), calls=%async_computation.3 | async-start | bytes 3670016 | tf_op jit(solution)/shard_map/all_to_all | solution.py:696
  550.5 7.1 %convolution_convert_fusion.2 = bf16[1024,2048]{1,0:T(8,128)(2,1)S(1)} fusion(bf16[1024,896]{1,0:T(8,128)(2,1)} %get-tuple-element.224, bf16[2048,1152]{1,0:T(8,128)(2,1)} %bitcast.152), kind=kOutput, calls=%fused_computation.7 | convolution fusion | flops 3760193536 | bytes 9699328 | tf_op jit(solution)/shard_map/dot_general | solution.py:23
  561.2 19.1 %collective-permute-done.60 = bf16[128,2048]{1,0:T(8,128)(2,1)S(1)} collective-permute-done((bf16[128,2048]{1,0:T(8,128)(2,1)S(1)}, bf16[128,2048]{1,0:T(8,128)(2,1)S(1)}, u32[]{:S(2)}, u32[]{:S(2)}) %collective-permute-start.60) | collective-permute-done | bytes 524320 | tf_op jit(solution)/shard_map/ppermute | solution.py:688
  590.2 19.4 %collective-permute-done.59 = bf16[256,2048]{1,0:T(8,128)(2,1)} collective-permute-done((bf16[256,2048]{1,0:T(8,128)(2,1)S(1)}, bf16[256,2048]{1,0:T(8,128)(2,1)}, u32[]{:S(2)}, u32[]{:S(2)}) %collective-permute-start.59) | collective-permute-done | bytes 1048608 | tf_op jit(solution)/shard_map/ppermute | solution.py:688
  619.2 4.5 collective-permute-start.63
  (461 shorter events, 244.3 us)
Async XLA Ops:
  16.2 23.2 %collective-permute-start.1 = (bf16[64,2048]{1,0:T(8,128)(2,1)}, bf16[64,2048]{1,0:T(8,128)(2,1)S(1)}, u32[]{:S(2)}, u32[]{:S(2)}) collective-permute-start(bf16[64,2048]{1,0:T(8,128)(2,1)} %get-tuple-element.344), channel_id=1, source_target_pairs={{0,16},{2,18},{4,20},{6,22},{8,24},{10,26},{12,28},{14,30},{16,0},... | collective-permute-start | bytes 786440 | tf_op jit(solution)/shard_map/ppermute | solution.py:688
  16.2 23.2 %collective-permute-start = (bf16[64,2048]{1,0:T(8,128)(2,1)}, bf16[64,2048]{1,0:T(8,128)(2,1)S(1)}, u32[]{:S(2)}, u32[]{:S(2)}) collective-permute-start(bf16[64,2048]{1,0:T(8,128)(2,1)} %get-tuple-element.344), channel_id=1, source_target_pairs={{0,8},{2,10},{4,12},{6,14},{8,16},{10,18},{12,20},{14,22},{16,24},... | collective-permute-start | bytes 786440 | tf_op jit(solution)/shard_map/ppermute | solution.py:688
  39.4 55.8 %all-to-all-start = ((bf16[16,64,1152]{2,1,0:T(8,128)(2,1)}), bf16[16,64,1152]{2,1,0:T(8,128)(2,1)S(1)}, u32[]{:S(2)}, u32[]{:S(2)}) async-start(bf16[16,64,1152]{2,1,0:T(8,128)(2,1)} %pad_maximum_fusion.2), calls=%async_computation | async-start | bytes 4718592 | tf_op jit(solution)/shard_map/all_to_all | solution.py:696
  47.5 47.6 %collective-permute-start.4 = (bf16[256,2048]{1,0:T(8,128)(2,1)}, bf16[256,2048]{1,0:T(8,128)(2,1)}, u32[]{:S(2)}, u32[]{:S(2)}) collective-permute-start(bf16[256,2048]{1,0:T(8,128)(2,1)} %pad_maximum_fusion.9), channel_id=1, source_target_pairs={{0,4},{2,6},{4,0},{6,2},{8,12},{10,14},{12,8},{14,10},{16,20},{18,... | collective-permute-start | bytes 3145736 | tf_op jit(solution)/shard_map/ppermute | solution.py:688
  49.4 45.7 %collective-permute-start.3 = (bf16[256,2048]{1,0:T(8,128)(2,1)}, bf16[256,2048]{1,0:T(8,128)(2,1)}, u32[]{:S(2)}, u32[]{:S(2)}) collective-permute-start(bf16[256,2048]{1,0:T(8,128)(2,1)} %pad_maximum_fusion.9), channel_id=1, source_target_pairs={{0,2},{2,0},{4,6},{6,4},{8,10},{10,8},{12,14},{14,12},{16,18},{18,... | collective-permute-start | bytes 3145736 | tf_op jit(solution)/shard_map/ppermute | solution.py:688
  50.9 74.5 %collective-permute-start.10 = (bf16[8,4,512]{2,1,0:T(4,128)(2,1)S(1)}, bf16[8,4,512]{2,1,0:T(4,128)(2,1)S(1)}, u32[]{:S(2)}, u32[]{:S(2)}) collective-permute-start(bf16[8,4,512]{2,1,0:T(4,128)(2,1)S(1)} %maximum_bitcast_fusion), channel_id=1, source_target_pairs={{0,1},{1,0},{2,3},{3,2},{4,5},{5,4},{6,7},{7,6},{8,9},{9,8},{10,11... | collective-permute-start | bytes 98312 | tf_op jit(solution)/shard_map/ppermute | solution.py:692
  95.1 22.5 %collective-permute-start.8 = (bf16[16,64,1152]{2,1,0:T(8,128)(2,1)S(1)}, bf16[16,64,1152]{2,1,0:T(8,128)(2,1)S(1)}, u32[]{:S(2)}, u32[]{:S(2)}) collective-permute-start(bf16[16,64,1152]{2,1,0:T(8,128)(2,1)S(1)} %all-to-all-done), channel_id=1, source_target_pairs={{0,1},{1,0},{2,3},{3,2},{4,5},{5,4},{6,7},{7,6},{8,9},{9,8},{10,11... | collective-permute-start | bytes 7077896 | tf_op jit(solution)/shard_map/ppermute | solution.py:692
  125.4 53.1 %all-to-all-start.1 = ((bf16[16,528,128]{2,1,0:T(8,128)(2,1)}), bf16[16,528,128]{2,1,0:T(8,128)(2,1)}, u32[]{:S(2)}, u32[]{:S(2)}) async-start(bf16[16,528,128]{2,1,0:T(8,128)(2,1)} %pad_maximum_fusion.3), calls=%async_computation.1 | async-start | bytes 4325376 | tf_op jit(solution)/shard_map/all_to_all | solution.py:696
  193.8 33.4 %collective-permute-start.13 = (bf16[256,2048]{1,0:T(8,128)(2,1)S(1)}, bf16[256,2048]{1,0:T(8,128)(2,1)}, u32[]{:S(2)}, u32[]{:S(2)}) collective-permute-start(bf16[256,2048]{1,0:T(8,128)(2,1)S(1)} %pad_maximum_fusion.10), channel_id=1, source_target_pairs={{0,2},{2,0},{4,6},{6,4},{8,10},{10,8},{12,14},{14,12},{16,18},{18,... | collective-permute-start | bytes 3145736 | tf_op jit(solution)/shard_map/ppermute | solution.py:688
  196.1 31.2 %collective-permute-start.14 = (bf16[256,2048]{1,0:T(8,128)(2,1)}, bf16[256,2048]{1,0:T(8,128)(2,1)}, u32[]{:S(2)}, u32[]{:S(2)}) collective-permute-start(bf16[256,2048]{1,0:T(8,128)(2,1)} %pad_maximum_fusion.11), channel_id=1, source_target_pairs={{0,4},{2,6},{4,0},{6,2},{8,12},{10,14},{12,8},{14,10},{16,20},{18,... | collective-permute-start | bytes 3145736 | tf_op jit(solution)/shard_map/ppermute | solution.py:688
  203.1 24.1 %collective-permute-start.16 = (bf16[64,2048]{1,0:T(8,128)(2,1)S(1)}, bf16[64,2048]{1,0:T(8,128)(2,1)}, u32[]{:S(2)}, u32[]{:S(2)}) collective-permute-start(bf16[64,2048]{1,0:T(8,128)(2,1)S(1)} %constant_dynamic-slice_fusion.5), channel_id=1, source_target_pairs={{0,16},{2,18},{4,20},{6,22},{8,24},{10,26},{12,28},{14,30},{16,0},... | collective-permute-start | bytes 786440 | tf_op jit(solution)/shard_map/ppermute | solution.py:688
  205.3 22.0 %collective-permute-start.15 = (bf16[64,2048]{1,0:T(8,128)(2,1)S(1)}, bf16[64,2048]{1,0:T(8,128)(2,1)}, u32[]{:S(2)}, u32[]{:S(2)}) collective-permute-start(bf16[64,2048]{1,0:T(8,128)(2,1)S(1)} %constant_dynamic-slice_fusion.5), channel_id=1, source_target_pairs={{0,8},{2,10},{4,12},{6,14},{8,16},{10,18},{12,20},{14,22},{16,24},... | collective-permute-start | bytes 786440 | tf_op jit(solution)/shard_map/ppermute | solution.py:688
  209.9 67.9 %collective-permute-start.28 = (bf16[16,528,128]{2,1,0:T(8,128)(2,1)}, bf16[16,528,128]{2,1,0:T(8,128)(2,1)}, u32[]{:S(2)}, u32[]{:S(2)}) collective-permute-start(bf16[16,528,128]{2,1,0:T(8,128)(2,1)} %all-to-all-done.1), channel_id=1, source_target_pairs={{0,1},{1,0},{2,3},{3,2},{4,5},{5,4},{6,7},{7,6},{8,9},{9,8},{10,11... | collective-permute-start | bytes 6488072 | tf_op jit(solution)/shard_map/ppermute | solution.py:692
  233.0 28.9 %collective-permute-start.22 = (bf16[256,2048]{1,0:T(8,128)(2,1)}, bf16[256,2048]{1,0:T(8,128)(2,1)}, u32[]{:S(2)}, u32[]{:S(2)}) collective-permute-start(bf16[256,2048]{1,0:T(8,128)(2,1)} %constant_dynamic-update-slice_fusion.8), channel_id=1, source_target_pairs={{0,4},{2,6},{4,0},{6,2},{8,12},{10,14},{12,8},{14,10},{16,20},{18,... | collective-permute-start | bytes 3145736 | tf_op jit(solution)/shard_map/ppermute | solution.py:688
  233.3 28.6 %collective-permute-start.21 = (bf16[256,2048]{1,0:T(8,128)(2,1)}, bf16[256,2048]{1,0:T(8,128)(2,1)}, u32[]{:S(2)}, u32[]{:S(2)}) collective-permute-start(bf16[256,2048]{1,0:T(8,128)(2,1)} %constant_dynamic-update-slice_fusion.8), channel_id=1, source_target_pairs={{0,2},{2,0},{4,6},{6,4},{8,10},{10,8},{12,14},{14,12},{16,18},{18,... | collective-permute-start | bytes 3145736 | tf_op jit(solution)/shard_map/ppermute | solution.py:688
  238.6 21.6 %collective-permute-start.19 = (bf16[64,2048]{1,0:T(8,128)(2,1)S(1)}, bf16[64,2048]{1,0:T(8,128)(2,1)}, u32[]{:S(2)}, u32[]{:S(2)}) collective-permute-start(bf16[64,2048]{1,0:T(8,128)(2,1)S(1)} %get-tuple-element.403), channel_id=1, source_target_pairs={{0,16},{2,18},{4,20},{6,22},{8,24},{10,26},{12,28},{14,30},{16,0},... | collective-permute-start | bytes 786440 | tf_op jit(solution)/shard_map/ppermute | solution.py:688
  260.2 36.9 %collective-permute-start.29 = (bf16[1024,1024]{0,1:T(8,128)(2,1)S(1)}, bf16[1024,1024]{0,1:T(8,128)(2,1)S(1)}, u32[]{:S(2)}, u32[]{:S(2)}) collective-permute-start(bf16[1024,1024]{0,1:T(8,128)(2,1)S(1)} %bitcast.157), channel_id=1, source_target_pairs={{0,1},{1,0},{2,3},{3,2},{4,5},{5,4},{6,7},{7,6},{8,9},{9,8},{10,11... | collective-permute-start | bytes 6291464 | tf_op jit(solution)/shard_map/ppermute | solution.py:692
  274.8 22.4 %collective-permute-start.24 = (bf16[64,2048]{1,0:T(8,128)(2,1)S(1)}, bf16[64,2048]{1,0:T(8,128)(2,1)S(1)}, u32[]{:S(2)}, u32[]{:S(2)}) collective-permute-start(bf16[64,2048]{1,0:T(8,128)(2,1)S(1)} %multiply_convert_fusion.1), channel_id=1, source_target_pairs={{0,16},{2,18},{4,20},{6,22},{8,24},{10,26},{12,28},{14,30},{16,0},... | collective-permute-start | bytes 786440 | tf_op jit(solution)/shard_map/ppermute | solution.py:688
  297.3 25.0 %collective-permute-start.31 = (bf16[256,2048]{1,0:T(8,128)(2,1)S(1)}, bf16[256,2048]{1,0:T(8,128)(2,1)S(1)}, u32[]{:S(2)}, u32[]{:S(2)}) collective-permute-start(bf16[256,2048]{1,0:T(8,128)(2,1)S(1)} %constant_dynamic-update-slice_fusion.12), channel_id=1, source_target_pairs={{0,4},{2,6},{4,0},{6,2},{8,12},{10,14},{12,8},{14,10},{16,20},{18,... | collective-permute-start | bytes 3145736 | tf_op jit(solution)/shard_map/ppermute | solution.py:688
  297.7 24.7 %collective-permute-start.30 = (bf16[256,2048]{1,0:T(8,128)(2,1)S(1)}, bf16[256,2048]{1,0:T(8,128)(2,1)S(1)}, u32[]{:S(2)}, u32[]{:S(2)}) collective-permute-start(bf16[256,2048]{1,0:T(8,128)(2,1)S(1)} %constant_dynamic-update-slice_fusion.12), channel_id=1, source_target_pairs={{0,2},{2,0},{4,6},{6,4},{8,10},{10,8},{12,14},{14,12},{16,18},{18,... | collective-permute-start | bytes 3145736 | tf_op jit(solution)/shard_map/ppermute | solution.py:688
  360.5 21.9 %collective-permute-start.36 = (bf16[256,2048]{1,0:T(8,128)(2,1)S(1)}, bf16[256,2048]{1,0:T(8,128)(2,1)S(1)}, u32[]{:S(2)}, u32[]{:S(2)}) collective-permute-start(bf16[256,2048]{1,0:T(8,128)(2,1)S(1)} %pad_maximum_fusion.12), channel_id=1, source_target_pairs={{0,2},{2,0},{4,6},{6,4},{8,10},{10,8},{12,14},{14,12},{16,18},{18,... | collective-permute-start | bytes 3145736 | tf_op jit(solution)/shard_map/ppermute | solution.py:688
  361.8 23.2 %collective-permute-start.37 = (bf16[256,2048]{1,0:T(8,128)(2,1)S(1)}, bf16[256,2048]{1,0:T(8,128)(2,1)S(1)}, u32[]{:S(2)}, u32[]{:S(2)}) collective-permute-start(bf16[256,2048]{1,0:T(8,128)(2,1)S(1)} %pad_maximum_fusion.13), channel_id=1, source_target_pairs={{0,4},{2,6},{4,0},{6,2},{8,12},{10,14},{12,8},{14,10},{16,20},{18,... | collective-permute-start | bytes 3145736 | tf_op jit(solution)/shard_map/ppermute | solution.py:688
  404.2 27.8 %collective-permute-start.46 = (bf16[256,2048]{1,0:T(8,128)(2,1)S(1)}, bf16[256,2048]{1,0:T(8,128)(2,1)S(1)}, u32[]{:S(2)}, u32[]{:S(2)}) collective-permute-start(bf16[256,2048]{1,0:T(8,128)(2,1)S(1)} %pad_maximum_fusion.14), channel_id=1, source_target_pairs={{0,2},{2,0},{4,6},{6,4},{8,10},{10,8},{12,14},{14,12},{16,18},{18,... | collective-permute-start | bytes 3145736 | tf_op jit(solution)/shard_map/ppermute | solution.py:688
  405.6 26.5 %collective-permute-start.47 = (bf16[256,2048]{1,0:T(8,128)(2,1)S(1)}, bf16[256,2048]{1,0:T(8,128)(2,1)S(1)}, u32[]{:S(2)}, u32[]{:S(2)}) collective-permute-start(bf16[256,2048]{1,0:T(8,128)(2,1)S(1)} %pad_maximum_fusion.15), channel_id=1, source_target_pairs={{0,4},{2,6},{4,0},{6,2},{8,12},{10,14},{12,8},{14,10},{16,20},{18,... | collective-permute-start | bytes 3145736 | tf_op jit(solution)/shard_map/ppermute | solution.py:688
  432.2 22.6 %collective-permute-start.50 = (bf16[256,2048]{1,0:T(8,128)(2,1)S(1)}, bf16[256,2048]{1,0:T(8,128)(2,1)S(1)}, u32[]{:S(2)}, u32[]{:S(2)}) collective-permute-start(bf16[256,2048]{1,0:T(8,128)(2,1)S(1)} %constant_dynamic-update-slice_fusion.26), channel_id=1, source_target_pairs={{0,4},{2,6},{4,0},{6,2},{8,12},{10,14},{12,8},{14,10},{16,20},{18,... | collective-permute-start | bytes 3145736 | tf_op jit(solution)/shard_map/ppermute | solution.py:688
  433.4 21.4 %collective-permute-start.49 = (bf16[256,2048]{1,0:T(8,128)(2,1)S(1)}, bf16[256,2048]{1,0:T(8,128)(2,1)S(1)}, u32[]{:S(2)}, u32[]{:S(2)}) collective-permute-start(bf16[256,2048]{1,0:T(8,128)(2,1)S(1)} %constant_dynamic-update-slice_fusion.26), channel_id=1, source_target_pairs={{0,2},{2,0},{4,6},{6,4},{8,10},{10,8},{12,14},{14,12},{16,18},{18,... | collective-permute-start | bytes 3145736 | tf_op jit(solution)/shard_map/ppermute | solution.py:688
  470.7 67.7 %all-to-all-start.2 = ((bf16[16,656,128]{2,1,0:T(8,128)(2,1)}), bf16[16,656,128]{2,1,0:T(8,128)(2,1)}, u32[]{:S(2)}, u32[]{:S(2)}) async-start(bf16[16,656,128]{2,1,0:T(8,128)(2,1)} %constant_dynamic-update-slice_fusion.35), calls=%async_computation.2 | async-start | bytes 5373952 | tf_op jit(solution)/shard_map/all_to_all | solution.py:696
  538.3 71.6 %all-to-all-start.3 = ((bf16[16,64,896]{2,1,0:T(8,128)(2,1)}), bf16[16,64,896]{2,1,0:T(8,128)(2,1)S(1)}, u32[]{:S(2)}, u32[]{:S(2)}) async-start(bf16[16,64,896]{2,1,0:T(8,128)(2,1)} %add_convert_fusion.2), calls=%async_computation.3 | async-start | bytes 3670016 | tf_op jit(solution)/shard_map/all_to_all | solution.py:696
  557.8 22.5 %collective-permute-start.60 = (bf16[128,2048]{1,0:T(8,128)(2,1)S(1)}, bf16[128,2048]{1,0:T(8,128)(2,1)S(1)}, u32[]{:S(2)}, u32[]{:S(2)}) collective-permute-start(bf16[128,2048]{1,0:T(8,128)(2,1)S(1)} %get-tuple-element.352), channel_id=1, source_target_pairs={{0,2},{2,0},{4,6},{6,4},{8,10},{10,8},{12,14},{14,12},{16,18},{18,... | collective-permute-start | bytes 1572872 | tf_op jit(solution)/shard_map/ppermute | solution.py:688
  580.9 28.7 %collective-permute-start.59 = (bf16[256,2048]{1,0:T(8,128)(2,1)S(1)}, bf16[256,2048]{1,0:T(8,128)(2,1)}, u32[]{:S(2)}, u32[]{:S(2)}) collective-permute-start(bf16[256,2048]{1,0:T(8,128)(2,1)S(1)} %pad_maximum_fusion.16), channel_id=1, source_target_pairs={{0,2},{2,0},{4,6},{6,4},{8,10},{10,8},{12,14},{14,12},{16,18},{18,... | collective-permute-start | bytes 3145736 | tf_op jit(solution)/shard_map/ppermute | solution.py:688
  583.6 26.2 %collective-permute-start.61 = (bf16[256,2048]{1,0:T(8,128)(2,1)}, bf16[256,2048]{1,0:T(8,128)(2,1)}, u32[]{:S(2)}, u32[]{:S(2)}) collective-permute-start(bf16[256,2048]{1,0:T(8,128)(2,1)} %pad_maximum_fusion.17), channel_id=1, source_target_pairs={{0,4},{2,6},{4,0},{6,2},{8,12},{10,14},{12,8},{14,10},{16,20},{18,... | collective-permute-start | bytes 3145736 | tf_op jit(solution)/shard_map/ppermute | solution.py:688
  619.2 21.2 %collective-permute-start.63 = (bf16[64,2048]{1,0:T(8,128)(2,1)}, bf16[64,2048]{1,0:T(8,128)(2,1)}, u32[]{:S(2)}, u32[]{:S(2)}) collective-permute-start(bf16[64,2048]{1,0:T(8,128)(2,1)} %get-tuple-element.394), channel_id=1, source_target_pairs={{0,16},{2,18},{4,20},{6,22},{8,24},{10,26},{12,28},{14,30},{16,0},... | collective-permute-start | bytes 786440 | tf_op jit(solution)/shard_map/ppermute | solution.py:688
  (109 other events, 1087.3 us)

commit v4 on v3

--- a/solution.py
+++ b/solution.py
@@ -432,7 +432,7 @@
 SMEM_SPEC = pl.BlockSpec(memory_space=pltpu.SMEM)
 ANY_SPEC = pl.BlockSpec(memory_space=pl.ANY)
 FORWARD_COST = pl.CostEstimate(flops=30_000_000_000, bytes_accessed=100_000_000, transcendentals=0)
-BACKWARD_COST = pl.CostEstimate(flops=1_000_000, bytes_accessed=1_000, transcendentals=0)
+SMALL_COST = pl.CostEstimate(flops=1_000_000, bytes_accessed=1_000, transcendentals=0)
 
 
 def mixer_forward(place, pre_own, pre_other, decay_grid, cols, rows, taps, head_gain):
@@ -510,7 +510,7 @@
             pltpu.SemaphoreType.DMA((17,)),
         ],
         compiler_params=pltpu.CompilerParams(vmem_limit_bytes=52 * 1024 * 1024),
-        cost_estimate=BACKWARD_COST,
+        cost_estimate=SMALL_COST,
         name="mixer_backward",
     )(place, *d_gated, *pre, decay_grid, cols, taps, head_gain, *kept)
 
@@ -581,14 +581,25 @@
         in_specs=[VMEM_SPEC] * 7,
         out_specs=[VMEM_SPEC] * 6,
         compiler_params=pltpu.CompilerParams(vmem_limit_bytes=32 * 1024 * 1024),
+        cost_estimate=SMALL_COST,
         name="unpack_heads",
     )(grads, gain, *weights)
     return query, key, value, gating, beta, gain_part[:, 0]
 
 
 def pack_kernel(
-    core, gain, w_query, w_key, w_value, w_gating, w_beta, w_output, rates, starts, kept, given
+    core, gain, w_beta, rates, starts, *refs
 ):
+    sources, (kept, given), copies, marks = refs[:5], refs[5:7], refs[7:12], refs[12]
+    loads = [
+        pltpu.make_async_copy(source, copy, marks.at[index])
+        for index, (source, copy) in enumerate(zip(sources, copies))
+    ]
+    for load in loads:
+        load.start()
+    for load in loads:
+        load.wait()
+    w_query, w_key, w_value, w_gating, w_output = copies
     heads = kept.shape[0]
     half = kept.shape[1]
     first = core[0] == 0
@@ -631,15 +642,18 @@
 def pack_heads(core, gain, w_query, w_key, w_value, w_gating, w_beta, w_output, rates, starts):
     rows = gain.shape[0]
     heads = w_query.shape[1] // KEY_SIZE
+    wide = (w_query, w_key, w_value, w_gating, w_output)
     shape = jax.ShapeDtypeStruct((heads, rows // 2, PACK + DV), BF16)
     return pl.pallas_call(
         pack_kernel,
         out_shape=(shape, shape),
-        in_specs=[SMEM_SPEC] + [VMEM_SPEC] * 9,
+        in_specs=[SMEM_SPEC] + [VMEM_SPEC] * 4 + [ANY_SPEC] * 5,
         out_specs=[VMEM_SPEC] * 2,
-        compiler_params=pltpu.CompilerParams(vmem_limit_bytes=32 * 1024 * 1024),
+        scratch_shapes=[pltpu.VMEM(w.shape, BF16) for w in wide] + [pltpu.SemaphoreType.DMA((5,))],
+        compiler_params=pltpu.CompilerParams(vmem_limit_bytes=58 * 1024 * 1024),
+        cost_estimate=SMALL_COST,
         name="pack_heads",
-    )(core, gain, w_query, w_key, w_value, w_gating, w_beta, w_output, rates, starts)
+    )(core, gain, w_beta, rates, starts, *wide)
 
 
 def join_kernel(*refs):
@@ -715,41 +729,44 @@
     return [block] + [send(block, along_z(steps)) for steps in (1, 2, 3)]
 
 
-def gather_near(levels):
-    block = stacked(levels)
+def send_near(block):
     return block, send(block, along_x), send(block, along_y)
 
 
-def gather_far(near):
+def far_halves(near):
     _, from_x, from_y = near
     half = from_x.shape[0] // 2
-    return near + (send(from_y[:half], along_x), send(from_x[half:], along_y))
-
-
-def gather_rows(block):
-    return stacked(gather_far(gather_near(gather_levels(block))))
-
-
-def scatter_far(parts):
+    return from_y[:half], from_x[half:]
+
+
+def send_far(halves):
+    return send(halves[0], along_x), send(halves[1], along_y)
+
+
+def far_parts(parts):
     rows = parts.shape[0] // 8
-    return parts, send(parts[6 * rows : 7 * rows], along_x), send(parts[7 * rows :], along_y)
-
-
-def scatter_near(begun):
-    parts, low, high = begun
+    return parts[6 * rows : 7 * rows], parts[7 * rows :]
+
+
+def near_parts(parts, low, high):
     rows = parts.shape[0] // 8
     for_x = stacked([parts[2 * rows : 3 * rows], total_of(parts[3 * rows : 4 * rows], high).astype(BF16)])
     for_y = stacked([total_of(parts[4 * rows : 5 * rows], low).astype(BF16), parts[5 * rows : 6 * rows]])
-    return parts[: 2 * rows], send(for_x, along_x), send(for_y, along_y)
-
-
-def scatter_levels(near):
-    own, from_x, from_y = near
-    total = total_of(own, from_x, from_y)
+    return for_x, for_y
+
+
+def send_parts(parts):
+    return send(parts[0], along_x), send(parts[1], along_y)
+
+
+def level_parts(parts, from_x, from_y):
+    total = total_of(parts[: parts.shape[0] // 4], from_x, from_y)
     rows = total.shape[0] // 4
-    return [total[:rows]] + [
-        send(total[j * rows : (j + 1) * rows].astype(BF16), along_z(-j)) for j in (1, 2, 3)
-    ]
+    return [total[:rows]] + [total[j * rows : (j + 1) * rows].astype(BF16) for j in (1, 2, 3)]
+
+
+def send_levels(levels):
+    return levels[:1] + [send(level, along_z(-j)) for j, level in zip((1, 2, 3), levels[1:])]
 
 
 def nn(a, b):
@@ -831,9 +848,9 @@
     in_payload = in_order(in_kept, swap_cores(in_given), 0)
     one_levels = gather_levels(normed_one.astype(BF16))
     in_mine = exchange(after(in_payload, one_levels))
-    one_near = gather_near(one_levels)
+    one_near = send_near(stacked(one_levels))
     in_mine = after(in_mine, one_near)
-    normed_all = stacked(gather_far(one_near))
+    normed_all = stacked(one_near + send_far(far_halves(one_near)))
     weights_all = joined_by_core(in_mine)
     weights_in, weights_out = weights_all[:, :PACK], weights_all[:, PACK:]
 
@@ -883,14 +900,24 @@
     feed_mine = exchange(feed)
     gated_own, gated_other, *kept = mixer_forward(place, *pre, decay_grid, cols, rows, taps, gain_head)
     mixed_parts = nt(gated_own, weights_out).astype(BF16)
-    mixed = scatter_far(mixed_parts)
+    far = send_far(far_parts(mixed_parts))
 
     cot_own = own_rows(cotangent)
-    mixed, cot, feed_mine = after((mixed, cot_own, feed_mine))
-    mixed, cot = scatter_near(mixed), gather_levels(cot)
+    far, feed_mine = after((far, feed_mine))
+    near = near_parts(mixed_parts, *far)
+    near, cot = send_parts(near), gather_levels(after(cot_own, near))
     feed_other = swap_cores(feed_mine)
-    mixed, cot, normed_late = after((mixed, cot, normed_all))
-    mixed, cot = scatter_levels(mixed), gather_near(cot)
+    near, cot = after((near, cot))
+    levels = level_parts(mixed_parts, *near)
+    levels, cot = send_levels(levels), send_near(stacked(after(cot, levels)))
+
+    levels, cot = after((levels, cot))
+    middle = inputs_own + total_of(*levels)
+    scale_two = lax.rsqrt(jnp.mean(middle * middle, axis=-1, keepdims=True) + EPSILON)
+    normed_mid = middle * scale_two
+    mid = normed_mid.astype(BF16)
+    mid_sent, cot_far = gather_levels(mid), send_far(far_halves(after(cot, mid)))
+    feed_mine, feed_other = after((feed_mine, feed_other), mid)
 
     def unit_rows(position):
         return stacked(
@@ -901,24 +928,18 @@
         )
 
     gate_rows, up_rows, down_rows = unit_rows(0), unit_rows(1), unit_rows(2)
-    cut = normed_late.reshape(own_count, CHIPS, CORES, half_count)
+    mid = mid_sent
+    mid, cot_far, gate_rows, up_rows, down_rows = after((mid, cot_far, gate_rows, up_rows, down_rows))
+    mid = stacked(mid)
+    cot_all = stacked(after(cot, mid) + cot_far)
+    cut = after(normed_all, mid).reshape(own_count, CHIPS, CORES, half_count)
     cut_mine = lax.dynamic_index_in_dim(cut, core, 2, False).reshape(own_count, width // CORES)
     cut_given = lax.dynamic_index_in_dim(cut, 1 - core, 2, False).reshape(own_count, width // CORES)
+    mid = send_near(mid)
+    d_hidden = nt(cot_all, down_rows).astype(BF16)
+    mid, d_hidden, cut_mine, cut_given = after((mid, d_hidden, cut_mine, cut_given))
     cut_other = swap_cores(cut_given)
-
-    mixed, cot = after((mixed, cot))
-    middle = inputs_own + total_of(*mixed)
-    scale_two = lax.rsqrt(jnp.mean(middle * middle, axis=-1, keepdims=True) + EPSILON)
-    normed_mid = middle * scale_two
-    mid, cot = gather_levels(normed_mid.astype(BF16)), gather_far(cot)
-    mid, cot, gate_rows, up_rows, down_rows, cut_mine, cut_other = after(
-        (mid, cot, gate_rows, up_rows, down_rows, cut_mine, cut_other)
-    )
-    mid = gather_near(mid)
-    cot_all = stacked(cot)
-    d_hidden = nt(cot_all, down_rows).astype(BF16)
-    mid, d_hidden = after((mid, d_hidden))
-    mid_all = stacked(gather_far(mid))
+    mid_all = stacked(mid + send_far(far_halves(mid)))
 
     gate_lin = nt(mid_all, gate_rows)
     up_lin = nt(mid_all, up_rows)
@@ -928,29 +949,34 @@
     hidden = (act * up_lin).astype(BF16)
     d_gate = (d_hidden * up_lin * (sig * (1.0 + gate_lin * (1.0 - sig)))).astype(BF16)
     d_up = (d_hidden * act).astype(BF16)
-    e_mid = scatter_far((nn(d_gate, gate_rows) + nn(d_up, up_rows)).astype(BF16))
-    feed_parts = nn(after(hidden, e_mid[0]), down_rows).astype(BF16)
-    e_mid, feed_parts = after((e_mid, feed_parts))
-    e_mid = scatter_near(e_mid)
+    e_parts = (nn(d_gate, gate_rows) + nn(d_up, up_rows)).astype(BF16)
+    far = send_far(far_parts(e_parts))
+    feed_parts = nn(after(hidden, e_parts), down_rows).astype(BF16)
+    far, feed_parts = after((far, feed_parts))
+    near = send_parts(near_parts(e_parts, *far))
 
     parts = [tn(d_gate, mid_all), tn(d_up, mid_all), tn(hidden, cot_all)]
     keep_part = stacked([part[:units] for part in parts])
     give_part = stacked([part[units:] for part in parts]).astype(BF16)
-    e_mid, feed_out, keep_part, give_part = after((e_mid, feed_parts, keep_part, give_part))
-    e_mid, feed_out = scatter_levels(e_mid), scatter_far(feed_out)
-    e_mid, feed_out = after((e_mid, feed_out))
-    e_two = total_of(*e_mid)
+    near, feed_parts, keep_part, give_part = after((near, feed_parts, keep_part, give_part))
+    levels = level_parts(e_parts, *near)
+    levels, feed_far = send_levels(levels), send_far(far_parts(after(feed_parts, levels)))
+    levels, feed_far = after((levels, feed_far))
+    e_two = total_of(*levels)
     d_middle = cot_own.astype(F32) + scale_two * (
         e_two - normed_mid * jnp.mean(e_two * normed_mid, axis=-1, keepdims=True)
     )
-    d_mid, feed_out = gather_levels(d_middle.astype(BF16)), scatter_near(feed_out)
+    d_mid = d_middle.astype(BF16)
+    d_mid, feed_near = gather_levels(d_mid), send_parts(near_parts(feed_parts, *after(feed_far, d_mid)))
     feed_grad = (keep_part + swap_cores(give_part).astype(F32)).astype(BF16)
     feed_grad = feed_grad.reshape(3 * units, CHIPS, row_count).transpose(1, 0, 2)
     feed_grad = jnp.pad(feed_grad, ((0, 0), (0, half_count * DV // row_count), (0, 0)))
-    d_mid, feed_out, feed_grad = after((d_mid, feed_out, feed_grad))
-    d_mid, feed_out = gather_near(d_mid), scatter_levels(feed_out)
-    d_mid, feed_out = after((d_mid, feed_out))
-    d_mid_all = stacked(gather_far(d_mid))
+    d_mid, feed_near, feed_grad = after((d_mid, feed_near, feed_grad))
+    d_mid = stacked(d_mid)
+    feed_levels = level_parts(feed_parts, *after(feed_near, d_mid))
+    d_mid, feed_levels = send_near(d_mid), send_levels(feed_levels)
+    d_mid, feed_levels = after((d_mid, feed_levels))
+    d_mid_all = stacked(d_mid + send_far(far_halves(d_mid)))
 
     d_gated_own = nn(d_mid_all, weights_out).astype(BF16)
     d_gated = (d_gated_own, swap_cores(d_gated_own))
@@ -977,8 +1003,11 @@
     grad_in, feed_back = after((grad_in, feed_back))
     e_parts = nt(after(d_pre_own, grad_in), weights_in).astype(BF16)
     grad_in = exchange(grad_in)
-    e_sums = scatter_near(scatter_far(e_parts))
-    e_sums, grad_in, feed_back = after((e_sums, grad_in, feed_back))
+    near = send_parts(near_parts(e_parts, *send_far(far_parts(e_parts))))
+    near, grad_in = after((near, grad_in))
+    levels = level_parts(e_parts, *near)
+    grad_in, feed_back = after((grad_in, feed_back), levels)
+    e_levels = send_levels(levels)
     small = grad_in[:, :small_rows, PACK - 64 :].astype(F32).reshape(CHIPS, -1)
     taps_all = lax.dynamic_slice_in_dim(small[:, : CONV * MIXED], core * head_count, head_count, 0)
     taps_all = taps_all.reshape(head_count, CONV, MIXED).transpose(1, 0, 2)
@@ -989,10 +1018,8 @@
         return in_order(mine, swap_cores(given), 1)
 
     grad_in = heads_here(grad_in)
-    block_out_own = (middle + total_of(*feed_out)).astype(BF16)
+    block_out_own = (middle + total_of(*feed_levels)).astype(BF16)
     block_out = in_order(block_out_own, swap_cores(block_out_own), 0)
-    e_levels = scatter_levels(e_sums)
-
     grad_out = heads_here(feed_back[:, 3 * units :].reshape(CHIPS, half_count, DV))
     grad_output = grad_out.astype(F32).transpose(0, 2, 1).reshape(head_count * DV, row_count)
     feed_back = feed_back[:, : 3 * units].astype(F32)

time: 664 us -> 646 us (0.973)
  waiting for transfers between devices: 272 us -> 261 us
    ppermute x56, waiting for transfers between devices: 266 us -> 256 us  [send(): lax.ppermute(value, 'seq', [(index, target(index)) for index in range(CHI...]
    unnamed x163 -> x164, local copies, waits for them, and re-layouts: 39.4 us -> 36.3 us
  transfers between devices with their start and end apart: 74 -> 74, of which waited for: 36 -> 35; matrix products, arithmetic and copies ran while one was open for 18% -> 19% of each run, Pallas kernels for 11% -> 12%
where the time goes in v4:
time: 646 us; the launch traced here: 639 us
  waiting for transfers between devices  261 us (40%)
  starting transfers between devices  127 us (20%)
  Pallas kernels  79.7 us (12%)
  local copies, waits for them, and re-layouts  73.6 us (11%)
  other arithmetic  48.6 us (8%)
  matrix products  45.9 us (7%)
    ppermute x56, waiting for transfers between devices, send(): lax.ppermute(value, 'seq', [(index, target(index)) for index in range(CHI...  256 us
    ppermute x56, starting transfers between devices, send(): lax.ppermute(value, 'seq', [(index, target(index)) for index in range(CHI...  88.6 us
    dot_general x16, matrix products, mm(): return lax.dot_general(a, b, (dims, ((), ())), preferred_element_type=F32)  45.9 us
    pallas_call x1, Pallas kernels, mixer_backward(): pl.pallas_call(backward_kernel, out_shape=(shape((half, PACK), BF16), sha...  39.5 us
    unnamed x164, local copies, waits for them, and re-layouts  36.3 us
    all_to_all x4, starting transfers between devices, exchange(): lax.all_to_all(pieces, 'seq', split_axis=0, concat_axis=0, tiled=True)  36.2 us
    pallas_call x1, Pallas kernels, mixer_forward(): pl.pallas_call(forward_kernel, out_shape=(shape((half, DV), BF16), shape(...  32.8 us
  transfers between devices with their start and end apart: 74, of which 35 were waited for; matrix products, arithmetic and copies ran while one was open for 19% of the time, Pallas kernels for 12%

profile of v4, /device:TPU:0, one launch (start us, length us, event | category | flops | bytes accessed | tf_op | source)
XLA Modules:
  0.0 638.8 jit_solution(11955007571146179895)
XLA Ops:
  4.7 5.2 pack_heads.1
  11.4 4.6 collective-permute-start.2
  22.7 16.2 %collective-permute-done.1 = bf16[64,2048]{1,0:T(8,128)(2,1)S(1)} collective-permute-done((bf16[64,2048]{1,0:T(8,128)(2,1)S(1)}, bf16[64,2048]{1,0:T(8,128)(2,1)S(1)}, u32[]{:S(2)}, u32[]{:S(2)}) %collective-permute-start.1) | collective-permute-done | bytes 262176 | tf_op jit(solution)/shard_map/ppermute | solution.py:702
  38.9 6.1 all-to-all-start
  54.6 40.1 %collective-permute-done.4 = bf16[256,2048]{1,0:T(8,128)(2,1)} collective-permute-done((bf16[256,2048]{1,0:T(8,128)(2,1)}, bf16[256,2048]{1,0:T(8,128)(2,1)}, u32[]{:S(2)}, u32[]{:S(2)}) %collective-permute-start.4) | collective-permute-done | bytes 1048608 | tf_op jit(solution)/shard_map/ppermute | solution.py:702
  106.8 8.0 %collective-permute-done.5 = bf16[128,2048]{1,0:T(8,128)(2,1)S(1)} collective-permute-done((bf16[128,2048]{1,0:T(8,128)(2,1)S(1)}, bf16[128,2048]{1,0:T(8,128)(2,1)S(1)}, u32[]{:S(2)}, u32[]{:S(2)}) %collective-permute-start.5) | collective-permute-done | bytes 524320 | tf_op jit(solution)/shard_map/ppermute | solution.py:702
  119.3 5.7 fusion.pre_own
  125.0 8.6 %all-to-all-start.1 = ((bf16[16,528,128]{2,1,0:T(8,128)(2,1)}), bf16[16,528,128]{2,1,0:T(8,128)(2,1)}, u32[]{:S(2)}, u32[]{:S(2)}) async-start(bf16[16,528,128]{2,1,0:T(8,128)(2,1)} %pad_maximum_fusion.3), calls=%async_computation.1 | async-start | bytes 4325376 | tf_op jit(solution)/shard_map/all_to_all | solution.py:710
  136.9 32.8 %mixer_forward.1 = (bf16[1024,256]{1,0:T(8,128)(2,1)S(1)}, bf16[1024,256]{1,0:T(8,128)(2,1)}, f32[2048,256]{1,0:T(8,128)}, f32[2048,512]{1,0:T(8,128)}, f32[2048...) custom-call(s32[32]{0:T(128)S(1)} %fusion.32.place, ...), custom_call_target="tpu_custom_call" | custom-call | flops 30000001024 | bytes 100000000 | tf_op jit(solution)/shard_map/mixer_forward/pallas_call | solution.py:442
  178.6 10.8 %collective-permute-done.12 = bf16[128,2048]{1,0:T(8,128)(2,1)S(1)} collective-permute-done((bf16[128,2048]{1,0:T(8,128)(2,1)}, bf16[128,2048]{1,0:T(8,128)(2,1)S(1)}, u32[]{:S(2)}, u32[]{:S(2)}) %collective-permute-start.12) | collective-permute-done | bytes 524320 | tf_op jit(solution)/shard_map/ppermute | solution.py:702
  195.9 5.1 collective-permute-start.17
  207.7 17.6 %collective-permute-done.16 = bf16[64,2048]{1,0:T(8,128)(2,1)S(1)} collective-permute-done((bf16[64,2048]{1,0:T(8,128)(2,1)S(1)}, bf16[64,2048]{1,0:T(8,128)(2,1)S(1)}, u32[]{:S(2)}, u32[]{:S(2)}) %collective-permute-start.16) | collective-permute-done | bytes 262176 | tf_op jit(solution)/shard_map/ppermute | solution.py:702
  235.0 9.1 %collective-permute-done.20 = bf16[64,2048]{1,0:T(8,128)(2,1)S(1)} collective-permute-done((bf16[64,2048]{1,0:T(8,128)(2,1)S(1)}, bf16[64,2048]{1,0:T(8,128)(2,1)S(1)}, u32[]{:S(2)}, u32[]{:S(2)}) %collective-permute-start.20) | collective-permute-done | bytes 262176 | tf_op jit(solution)/shard_map/ppermute | solution.py:702
  244.1 8.2 %collective-permute-done.19 = bf16[64,2048]{1,0:T(8,128)(2,1)S(1)} collective-permute-done((bf16[64,2048]{1,0:T(8,128)(2,1)}, bf16[64,2048]{1,0:T(8,128)(2,1)S(1)}, u32[]{:S(2)}, u32[]{:S(2)}) %collective-permute-start.19) | collective-permute-done | bytes 262176 | tf_op jit(solution)/shard_map/ppermute | solution.py:702
  252.3 5.6 collective-permute-done.18
  275.1 7.9 %collective-permute-done.24 = bf16[64,2048]{1,0:T(8,128)(2,1)S(1)} collective-permute-done((bf16[64,2048]{1,0:T(8,128)(2,1)S(1)}, bf16[64,2048]{1,0:T(8,128)(2,1)S(1)}, u32[]{:S(2)}, u32[]{:S(2)}) %collective-permute-start.24) | collective-permute-done | bytes 262176 | tf_op jit(solution)/shard_map/ppermute | solution.py:702
  287.2 6.6 %copy.122 = bf16[1024,2048]{0,1:T(8,128)(2,1)} copy(bf16[1024,2048]{1,0:T(8,128)(2,1)} %copy-done.17) | data formatting | bytes 8388608 | tf_op jit(solution)/shard_map/optimization_barrier | solution.py:714
  302.1 5.6 collective-permute-done.30
  353.3 16.1 %collective-permute-done.35 = bf16[256,2048]{1,0:T(8,128)(2,1)S(1)} collective-permute-done((bf16[256,2048]{1,0:T(8,128)(2,1)S(1)}, bf16[256,2048]{1,0:T(8,128)(2,1)S(1)}, u32[]{:S(2)}, u32[]{:S(2)}) %collective-permute-start.35) | collective-permute-done | bytes 1048608 | tf_op jit(solution)/shard_map/ppermute | solution.py:702
  371.3 4.7 collective-permute-start.39
  382.1 6.4 %collective-permute-done.38 = bf16[64,2048]{1,0:T(8,128)(2,1)S(1)} collective-permute-done((bf16[64,2048]{1,0:T(8,128)(2,1)S(1)}, bf16[64,2048]{1,0:T(8,128)(2,1)S(1)}, u32[]{:S(2)}, u32[]{:S(2)}) %collective-permute-start.38) | collective-permute-done | bytes 262176 | tf_op jit(solution)/shard_map/ppermute | solution.py:702
  392.9 7.9 %collective-permute-start.44 = (bf16[64,2048]{1,0:T(8,128)(2,1)S(1)}, bf16[64,2048]{1,0:T(8,128)(2,1)S(1)}, u32[]{:S(2)}, u32[]{:S(2)}) collective-permute-start(bf16[64,2048]{1,0:T(8,128)(2,1)S(1)} %get-tuple-element.212), channel_id=1, source_target_pairs={{0,24},{2,26},{4,28},{6,30},{8,0},{10,2},{12,4},{14,6},{16,8},{18,... | collective-permute-start | bytes 786440 | tf_op jit(solution)/shard_map/ppermute | solution.py:702
  407.6 13.1 %collective-permute-done.43 = bf16[64,2048]{1,0:T(8,128)(2,1)S(1)} collective-permute-done((bf16[64,2048]{1,0:T(8,128)(2,1)S(1)}, bf16[64,2048]{1,0:T(8,128)(2,1)S(1)}, u32[]{:S(2)}, u32[]{:S(2)}) %collective-permute-start.43) | collective-permute-done | bytes 262176 | tf_op jit(solution)/shard_map/ppermute | solution.py:702
  434.2 8.4 %collective-permute-done.51 = bf16[64,2048]{1,0:T(8,128)(2,1)S(1)} collective-permute-done((bf16[64,2048]{1,0:T(8,128)(2,1)S(1)}, bf16[64,2048]{1,0:T(8,128)(2,1)S(1)}, u32[]{:S(2)}, u32[]{:S(2)}) %collective-permute-start.51) | collective-permute-done | bytes 262176 | tf_op jit(solution)/shard_map/ppermute | solution.py:702
  446.4 9.0 %collective-permute-done.53 = bf16[128,2048]{1,0:T(8,128)(2,1)S(1)} collective-permute-done((bf16[128,2048]{1,0:T(8,128)(2,1)S(1)}, bf16[128,2048]{1,0:T(8,128)(2,1)S(1)}, u32[]{:S(2)}, u32[]{:S(2)}) %collective-permute-start.53) | collective-permute-done | bytes 524320 | tf_op jit(solution)/shard_map/ppermute | solution.py:702
  462.1 9.5 %all-to-all-start.2 = ((bf16[16,656,128]{2,1,0:T(8,128)(2,1)}), bf16[16,656,128]{2,1,0:T(8,128)(2,1)}, u32[]{:S(2)}, u32[]{:S(2)}) async-start(bf16[16,656,128]{2,1,0:T(8,128)(2,1)} %constant_dynamic-update-slice_fusion.35), calls=%async_computation.2 | async-start | bytes 5373952 | tf_op jit(solution)/shard_map/all_to_all | solution.py:710
  477.5 39.5 %mixer_backward.1 = (bf16[1024,896]{1,0:T(8,128)(2,1)}, bf16[1024,896]{1,0:T(8,128)(2,1)}, f32[4,8,512]{2,1,0:T(8,128)S(1)}, f32[8,256]{1,0:T(8,128)S(1)}) custom-call(s32[32]{0:T(128)S(1)} %fusion.32.place, bf16[1024,256]{1,0:T(8,128)(2,1)S(1)} %convolution_convert_fusion.5.d_gated_own, bf16[1024,256]{1,0:T(8,128)(2,1)S(1)} %collective-permute-done.55.d_gated_other, ...), custom_call_target="tpu_custom_call" | custom-call | flops 1000000 | bytes 1000 | tf_op jit(solution)/shard_map/mixer_backward/pallas_call | solution.py:483
  517.3 4.6 fusion.63
  525.9 12.1 %all-to-all-start.3 = ((bf16[16,64,896]{2,1,0:T(8,128)(2,1)}), bf16[16,64,896]{2,1,0:T(8,128)(2,1)S(1)}, u32[]{:S(2)}, u32[]{:S(2)}) async-start(bf16[16,64,896]{2,1,0:T(8,128)(2,1)} %add_convert_fusion.2), calls=%async_computation.3 | async-start | bytes 3670016 | tf_op jit(solution)/shard_map/all_to_all | solution.py:710
  538.0 7.1 %convolution_convert_fusion.2 = bf16[1024,2048]{1,0:T(8,128)(2,1)S(1)} fusion(bf16[1024,896]{1,0:T(8,128)(2,1)} %get-tuple-element.238, bf16[2048,1152]{1,0:T(8,128)(2,1)} %bitcast.157), kind=kOutput, calls=%fused_computation.7 | convolution fusion | flops 3760193536 | bytes 9699328 | tf_op jit(solution)/shard_map/dot_general | solution.py:23
  548.8 19.1 %collective-permute-done.60 = bf16[128,2048]{1,0:T(8,128)(2,1)S(1)} collective-permute-done((bf16[128,2048]{1,0:T(8,128)(2,1)S(1)}, bf16[128,2048]{1,0:T(8,128)(2,1)S(1)}, u32[]{:S(2)}, u32[]{:S(2)}) %collective-permute-start.60) | collective-permute-done | bytes 524320 | tf_op jit(solution)/shard_map/ppermute | solution.py:702
  576.6 21.2 %collective-permute-done.59 = bf16[256,2048]{1,0:T(8,128)(2,1)} collective-permute-done((bf16[256,2048]{1,0:T(8,128)(2,1)}, bf16[256,2048]{1,0:T(8,128)(2,1)}, u32[]{:S(2)}, u32[]{:S(2)}) %collective-permute-start.59) | collective-permute-done | bytes 1048608 | tf_op jit(solution)/shard_map/ppermute | solution.py:702
  (455 shorter events, 253.8 us)
Async XLA Ops:
  16.0 23.0 %collective-permute-start.1 = (bf16[64,2048]{1,0:T(8,128)(2,1)S(1)}, bf16[64,2048]{1,0:T(8,128)(2,1)S(1)}, u32[]{:S(2)}, u32[]{:S(2)}) collective-permute-start(bf16[64,2048]{1,0:T(8,128)(2,1)S(1)} %get-tuple-element.358), channel_id=1, source_target_pairs={{0,16},{2,18},{4,20},{6,22},{8,24},{10,26},{12,28},{14,30},{16,0},... | collective-permute-start | bytes 786440 | tf_op jit(solution)/shard_map/ppermute | solution.py:702
  16.0 23.0 %collective-permute-start = (bf16[64,2048]{1,0:T(8,128)(2,1)S(1)}, bf16[64,2048]{1,0:T(8,128)(2,1)S(1)}, u32[]{:S(2)}, u32[]{:S(2)}) collective-permute-start(bf16[64,2048]{1,0:T(8,128)(2,1)S(1)} %get-tuple-element.358), channel_id=1, source_target_pairs={{0,8},{2,10},{4,12},{6,14},{8,16},{10,18},{12,20},{14,22},{16,24},... | collective-permute-start | bytes 786440 | tf_op jit(solution)/shard_map/ppermute | solution.py:702
  38.9 55.8 %all-to-all-start = ((bf16[16,64,1152]{2,1,0:T(8,128)(2,1)}), bf16[16,64,1152]{2,1,0:T(8,128)(2,1)S(1)}, u32[]{:S(2)}, u32[]{:S(2)}) async-start(bf16[16,64,1152]{2,1,0:T(8,128)(2,1)} %pad_maximum_fusion.2), calls=%async_computation | async-start | bytes 4718592 | tf_op jit(solution)/shard_map/all_to_all | solution.py:710
  47.0 47.6 %collective-permute-start.4 = (bf16[256,2048]{1,0:T(8,128)(2,1)}, bf16[256,2048]{1,0:T(8,128)(2,1)}, u32[]{:S(2)}, u32[]{:S(2)}) collective-permute-start(bf16[256,2048]{1,0:T(8,128)(2,1)} %pad_maximum_fusion.9), channel_id=1, source_target_pairs={{0,4},{2,6},{4,0},{6,2},{8,12},{10,14},{12,8},{14,10},{16,20},{18,... | collective-permute-start | bytes 3145736 | tf_op jit(solution)/shard_map/ppermute | solution.py:702
  49.0 45.7 %collective-permute-start.3 = (bf16[256,2048]{1,0:T(8,128)(2,1)}, bf16[256,2048]{1,0:T(8,128)(2,1)}, u32[]{:S(2)}, u32[]{:S(2)}) collective-permute-start(bf16[256,2048]{1,0:T(8,128)(2,1)} %pad_maximum_fusion.9), channel_id=1, source_target_pairs={{0,2},{2,0},{4,6},{6,4},{8,10},{10,8},{12,14},{14,12},{16,18},{18,... | collective-permute-start | bytes 3145736 | tf_op jit(solution)/shard_map/ppermute | solution.py:702
  50.5 74.5 %collective-permute-start.10 = (bf16[8,4,512]{2,1,0:T(4,128)(2,1)S(1)}, bf16[8,4,512]{2,1,0:T(4,128)(2,1)S(1)}, u32[]{:S(2)}, u32[]{:S(2)}) collective-permute-start(bf16[8,4,512]{2,1,0:T(4,128)(2,1)S(1)} %maximum_bitcast_fusion), channel_id=1, source_target_pairs={{0,1},{1,0},{2,3},{3,2},{4,5},{5,4},{6,7},{7,6},{8,9},{9,8},{10,11... | collective-permute-start | bytes 98312 | tf_op jit(solution)/shard_map/ppermute | solution.py:706
  94.7 22.5 %collective-permute-start.8 = (bf16[16,64,1152]{2,1,0:T(8,128)(2,1)S(1)}, bf16[16,64,1152]{2,1,0:T(8,128)(2,1)S(1)}, u32[]{:S(2)}, u32[]{:S(2)}) collective-permute-start(bf16[16,64,1152]{2,1,0:T(8,128)(2,1)S(1)} %all-to-all-done), channel_id=1, source_target_pairs={{0,1},{1,0},{2,3},{3,2},{4,5},{5,4},{6,7},{7,6},{8,9},{9,8},{10,11... | collective-permute-start | bytes 7077896 | tf_op jit(solution)/shard_map/ppermute | solution.py:706
  125.0 53.6 %all-to-all-start.1 = ((bf16[16,528,128]{2,1,0:T(8,128)(2,1)}), bf16[16,528,128]{2,1,0:T(8,128)(2,1)}, u32[]{:S(2)}, u32[]{:S(2)}) async-start(bf16[16,528,128]{2,1,0:T(8,128)(2,1)} %pad_maximum_fusion.3), calls=%async_computation.1 | async-start | bytes 4325376 | tf_op jit(solution)/shard_map/all_to_all | solution.py:710
  192.6 32.7 %collective-permute-start.13 = (bf16[256,2048]{1,0:T(8,128)(2,1)S(1)}, bf16[256,2048]{1,0:T(8,128)(2,1)S(1)}, u32[]{:S(2)}, u32[]{:S(2)}) collective-permute-start(bf16[256,2048]{1,0:T(8,128)(2,1)S(1)} %pad_maximum_fusion.10), channel_id=1, source_target_pairs={{0,2},{2,0},{4,6},{6,4},{8,10},{10,8},{12,14},{14,12},{16,18},{18,... | collective-permute-start | bytes 3145736 | tf_op jit(solution)/shard_map/ppermute | solution.py:702
  194.1 31.2 %collective-permute-start.14 = (bf16[256,2048]{1,0:T(8,128)(2,1)S(1)}, bf16[256,2048]{1,0:T(8,128)(2,1)S(1)}, u32[]{:S(2)}, u32[]{:S(2)}) collective-permute-start(bf16[256,2048]{1,0:T(8,128)(2,1)S(1)} %pad_maximum_fusion.11), channel_id=1, source_target_pairs={{0,4},{2,6},{4,0},{6,2},{8,12},{10,14},{12,8},{14,10},{16,20},{18,... | collective-permute-start | bytes 3145736 | tf_op jit(solution)/shard_map/ppermute | solution.py:702
  200.9 24.4 %collective-permute-start.16 = (bf16[64,2048]{1,0:T(8,128)(2,1)S(1)}, bf16[64,2048]{1,0:T(8,128)(2,1)S(1)}, u32[]{:S(2)}, u32[]{:S(2)}) collective-permute-start(bf16[64,2048]{1,0:T(8,128)(2,1)S(1)} %constant_dynamic-slice_fusion.5), channel_id=1, source_target_pairs={{0,16},{2,18},{4,20},{6,22},{8,24},{10,26},{12,28},{14,30},{16,0},... | collective-permute-start | bytes 786440 | tf_op jit(solution)/shard_map/ppermute | solution.py:702
  203.3 22.0 %collective-permute-start.15 = (bf16[64,2048]{1,0:T(8,128)(2,1)S(1)}, bf16[64,2048]{1,0:T(8,128)(2,1)S(1)}, u32[]{:S(2)}, u32[]{:S(2)}) collective-permute-start(bf16[64,2048]{1,0:T(8,128)(2,1)S(1)} %constant_dynamic-slice_fusion.5), channel_id=1, source_target_pairs={{0,8},{2,10},{4,12},{6,14},{8,16},{10,18},{12,20},{14,22},{16,24},... | collective-permute-start | bytes 786440 | tf_op jit(solution)/shard_map/ppermute | solution.py:702
  207.7 59.8 %collective-permute-start.28 = (bf16[16,528,128]{2,1,0:T(8,128)(2,1)}, bf16[16,528,128]{2,1,0:T(8,128)(2,1)}, u32[]{:S(2)}, u32[]{:S(2)}) collective-permute-start(bf16[16,528,128]{2,1,0:T(8,128)(2,1)} %all-to-all-done.1), channel_id=1, source_target_pairs={{0,1},{1,0},{2,3},{3,2},{4,5},{5,4},{6,7},{7,6},{8,9},{9,8},{10,11... | collective-permute-start | bytes 6488072 | tf_op jit(solution)/shard_map/ppermute | solution.py:706
  231.5 26.4 %collective-permute-start.22 = (bf16[256,2048]{1,0:T(8,128)(2,1)}, bf16[256,2048]{1,0:T(8,128)(2,1)S(1)}, u32[]{:S(2)}, u32[]{:S(2)}) collective-permute-start(bf16[256,2048]{1,0:T(8,128)(2,1)} %constant_dynamic-update-slice_fusion.8), channel_id=1, source_target_pairs={{0,4},{2,6},{4,0},{6,2},{8,12},{10,14},{12,8},{14,10},{16,20},{18,... | collective-permute-start | bytes 3145736 | tf_op jit(solution)/shard_map/ppermute | solution.py:702
  231.9 26.1 %collective-permute-start.21 = (bf16[256,2048]{1,0:T(8,128)(2,1)}, bf16[256,2048]{1,0:T(8,128)(2,1)}, u32[]{:S(2)}, u32[]{:S(2)}) collective-permute-start(bf16[256,2048]{1,0:T(8,128)(2,1)} %constant_dynamic-update-slice_fusion.8), channel_id=1, source_target_pairs={{0,2},{2,0},{4,6},{6,4},{8,10},{10,8},{12,14},{14,12},{16,18},{18,... | collective-permute-start | bytes 3145736 | tf_op jit(solution)/shard_map/ppermute | solution.py:702
  286.1 21.6 %collective-permute-start.30 = (bf16[256,2048]{1,0:T(8,128)(2,1)}, bf16[256,2048]{1,0:T(8,128)(2,1)}, u32[]{:S(2)}, u32[]{:S(2)}) collective-permute-start(bf16[256,2048]{1,0:T(8,128)(2,1)} %constant_dynamic-update-slice_fusion.12), channel_id=1, source_target_pairs={{0,4},{2,6},{4,0},{6,2},{8,12},{10,14},{12,8},{14,10},{16,20},{18,... | collective-permute-start | bytes 3145736 | tf_op jit(solution)/shard_map/ppermute | solution.py:702
  286.5 21.5 %collective-permute-start.29 = (bf16[256,2048]{1,0:T(8,128)(2,1)}, bf16[256,2048]{1,0:T(8,128)(2,1)}, u32[]{:S(2)}, u32[]{:S(2)}) collective-permute-start(bf16[256,2048]{1,0:T(8,128)(2,1)} %constant_dynamic-update-slice_fusion.12), channel_id=1, source_target_pairs={{0,2},{2,0},{4,6},{6,4},{8,10},{10,8},{12,14},{14,12},{16,18},{18,... | collective-permute-start | bytes 3145736 | tf_op jit(solution)/shard_map/ppermute | solution.py:702
  347.0 22.4 %collective-permute-start.35 = (bf16[256,2048]{1,0:T(8,128)(2,1)S(1)}, bf16[256,2048]{1,0:T(8,128)(2,1)S(1)}, u32[]{:S(2)}, u32[]{:S(2)}) collective-permute-start(bf16[256,2048]{1,0:T(8,128)(2,1)S(1)} %pad_maximum_fusion.12), channel_id=1, source_target_pairs={{0,2},{2,0},{4,6},{6,4},{8,10},{10,8},{12,14},{14,12},{16,18},{18,... | collective-permute-start | bytes 3145736 | tf_op jit(solution)/shard_map/ppermute | solution.py:702
  348.5 20.8 %collective-permute-start.36 = (bf16[256,2048]{1,0:T(8,128)(2,1)S(1)}, bf16[256,2048]{1,0:T(8,128)(2,1)S(1)}, u32[]{:S(2)}, u32[]{:S(2)}) collective-permute-start(bf16[256,2048]{1,0:T(8,128)(2,1)S(1)} %pad_maximum_fusion.13), channel_id=1, source_target_pairs={{0,4},{2,6},{4,0},{6,2},{8,12},{10,14},{12,8},{14,10},{16,20},{18,... | collective-permute-start | bytes 3145736 | tf_op jit(solution)/shard_map/ppermute | solution.py:702
  390.5 30.2 %collective-permute-start.45 = (bf16[256,2048]{1,0:T(8,128)(2,1)S(1)}, bf16[256,2048]{1,0:T(8,128)(2,1)S(1)}, u32[]{:S(2)}, u32[]{:S(2)}) collective-permute-start(bf16[256,2048]{1,0:T(8,128)(2,1)S(1)} %pad_maximum_fusion.14), channel_id=1, source_target_pairs={{0,2},{2,0},{4,6},{6,4},{8,10},{10,8},{12,14},{14,12},{16,18},{18,... | collective-permute-start | bytes 3145736 | tf_op jit(solution)/shard_map/ppermute | solution.py:702
  392.0 28.7 %collective-permute-start.46 = (bf16[256,2048]{1,0:T(8,128)(2,1)S(1)}, bf16[256,2048]{1,0:T(8,128)(2,1)S(1)}, u32[]{:S(2)}, u32[]{:S(2)}) collective-permute-start(bf16[256,2048]{1,0:T(8,128)(2,1)S(1)} %pad_maximum_fusion.15), channel_id=1, source_target_pairs={{0,4},{2,6},{4,0},{6,2},{8,12},{10,14},{12,8},{14,10},{16,20},{18,... | collective-permute-start | bytes 3145736 | tf_op jit(solution)/shard_map/ppermute | solution.py:702
  420.8 22.7 %collective-permute-start.49 = (bf16[256,2048]{1,0:T(8,128)(2,1)S(1)}, bf16[256,2048]{1,0:T(8,128)(2,1)S(1)}, u32[]{:S(2)}, u32[]{:S(2)}) collective-permute-start(bf16[256,2048]{1,0:T(8,128)(2,1)S(1)} %constant_dynamic-update-slice_fusion.26), channel_id=1, source_target_pairs={{0,4},{2,6},{4,0},{6,2},{8,12},{10,14},{12,8},{14,10},{16,20},{18,... | collective-permute-start | bytes 3145736 | tf_op jit(solution)/shard_map/ppermute | solution.py:702
  421.9 22.5 %collective-permute-start.48 = (bf16[256,2048]{1,0:T(8,128)(2,1)S(1)}, bf16[256,2048]{1,0:T(8,128)(2,1)S(1)}, u32[]{:S(2)}, u32[]{:S(2)}) collective-permute-start(bf16[256,2048]{1,0:T(8,128)(2,1)S(1)} %constant_dynamic-update-slice_fusion.26), channel_id=1, source_target_pairs={{0,2},{2,0},{4,6},{6,4},{8,10},{10,8},{12,14},{14,12},{16,18},{18,... | collective-permute-start | bytes 3145736 | tf_op jit(solution)/shard_map/ppermute | solution.py:702
  462.1 63.8 %all-to-all-start.2 = ((bf16[16,656,128]{2,1,0:T(8,128)(2,1)}), bf16[16,656,128]{2,1,0:T(8,128)(2,1)}, u32[]{:S(2)}, u32[]{:S(2)}) async-start(bf16[16,656,128]{2,1,0:T(8,128)(2,1)} %constant_dynamic-update-slice_fusion.35), calls=%async_computation.2 | async-start | bytes 5373952 | tf_op jit(solution)/shard_map/all_to_all | solution.py:710
  471.6 45.7 %collective-permute-start.56 = (bf16[1024,1024]{0,1:T(8,128)(2,1)S(1)}, bf16[1024,1024]{0,1:T(8,128)(2,1)}, u32[]{:S(2)}, u32[]{:S(2)}) collective-permute-start(bf16[1024,1024]{0,1:T(8,128)(2,1)S(1)} %bitcast.168), channel_id=1, source_target_pairs={{0,1},{1,0},{2,3},{3,2},{4,5},{5,4},{6,7},{7,6},{8,9},{9,8},{10,11... | collective-permute-start | bytes 6291464 | tf_op jit(solution)/shard_map/ppermute | solution.py:706
  525.9 71.9 %all-to-all-start.3 = ((bf16[16,64,896]{2,1,0:T(8,128)(2,1)}), bf16[16,64,896]{2,1,0:T(8,128)(2,1)S(1)}, u32[]{:S(2)}, u32[]{:S(2)}) async-start(bf16[16,64,896]{2,1,0:T(8,128)(2,1)} %add_convert_fusion.2), calls=%async_computation.3 | async-start | bytes 3670016 | tf_op jit(solution)/shard_map/all_to_all | solution.py:710
  545.3 22.5 %collective-permute-start.60 = (bf16[128,2048]{1,0:T(8,128)(2,1)S(1)}, bf16[128,2048]{1,0:T(8,128)(2,1)S(1)}, u32[]{:S(2)}, u32[]{:S(2)}) collective-permute-start(bf16[128,2048]{1,0:T(8,128)(2,1)S(1)} %get-tuple-element.366), channel_id=1, source_target_pairs={{0,2},{2,0},{4,6},{6,4},{8,10},{10,8},{12,14},{14,12},{16,18},{18,... | collective-permute-start | bytes 1572872 | tf_op jit(solution)/shard_map/ppermute | solution.py:702
  569.4 28.4 %collective-permute-start.59 = (bf16[256,2048]{1,0:T(8,128)(2,1)}, bf16[256,2048]{1,0:T(8,128)(2,1)}, u32[]{:S(2)}, u32[]{:S(2)}) collective-permute-start(bf16[256,2048]{1,0:T(8,128)(2,1)} %pad_maximum_fusion.16), channel_id=1, source_target_pairs={{0,2},{2,0},{4,6},{6,4},{8,10},{10,8},{12,14},{14,12},{16,18},{18,... | collective-permute-start | bytes 3145736 | tf_op jit(solution)/shard_map/ppermute | solution.py:702
  572.0 25.7 %collective-permute-start.61 = (bf16[256,2048]{1,0:T(8,128)(2,1)}, bf16[256,2048]{1,0:T(8,128)(2,1)}, u32[]{:S(2)}, u32[]{:S(2)}) collective-permute-start(bf16[256,2048]{1,0:T(8,128)(2,1)} %pad_maximum_fusion.17), channel_id=1, source_target_pairs={{0,4},{2,6},{4,0},{6,2},{8,12},{10,14},{12,8},{14,10},{16,20},{18,... | collective-permute-start | bytes 3145736 | tf_op jit(solution)/shard_map/ppermute | solution.py:702
  601.1 26.9 %collective-permute-start.64 = (bf16[64,2048]{1,0:T(8,128)(2,1)}, bf16[64,2048]{1,0:T(8,128)(2,1)}, u32[]{:S(2)}, u32[]{:S(2)}) collective-permute-start(bf16[64,2048]{1,0:T(8,128)(2,1)} %get-tuple-element.407), channel_id=1, source_target_pairs={{0,8},{2,10},{4,12},{6,14},{8,16},{10,18},{12,20},{14,22},{16,24},... | collective-permute-start | bytes 786440 | tf_op jit(solution)/shard_map/ppermute | solution.py:702
  602.1 25.9 %collective-permute-start.63 = (bf16[64,2048]{1,0:T(8,128)(2,1)}, bf16[64,2048]{1,0:T(8,128)(2,1)}, u32[]{:S(2)}, u32[]{:S(2)}) collective-permute-start(bf16[64,2048]{1,0:T(8,128)(2,1)} %get-tuple-element.408), channel_id=1, source_target_pairs={{0,16},{2,18},{4,20},{6,22},{8,24},{10,26},{12,28},{14,30},{16,0},... | collective-permute-start | bytes 786440 | tf_op jit(solution)/shard_map/ppermute | solution.py:702
  606.6 21.4 %collective-permute-start.62 = (bf16[64,2048]{1,0:T(8,128)(2,1)}, bf16[64,2048]{1,0:T(8,128)(2,1)}, u32[]{:S(2)}, u32[]{:S(2)}) collective-permute-start(bf16[64,2048]{1,0:T(8,128)(2,1)} %get-tuple-element.409), channel_id=1, source_target_pairs={{0,24},{2,26},{4,28},{6,30},{8,0},{10,2},{12,4},{14,6},{16,8},{18,... | collective-permute-start | bytes 786440 | tf_op jit(solution)/shard_map/ppermute | solution.py:702
  (106 other events, 1005.3 us)

commit v5 on v4

--- a/solution.py
+++ b/solution.py
@@ -155,11 +155,6 @@
     for copy in loads:
         copy.wait()
     strict, levels, eye = block_masks()
-    key_eye = (
-        lax.broadcasted_iota(jnp.int32, (KEY_SIZE, KEY_SIZE), 0)
-        == lax.broadcasted_iota(jnp.int32, (KEY_SIZE, KEY_SIZE), 1)
-    ).astype(F32)
-
     def prepare(group, _):
         work = []
         for lane in range(UNROLL):
@@ -199,8 +194,7 @@
             read_out[here, :] = read.astype(BF16)
             both_maps[b, :BLOCK] = read.astype(BF16)
             both_maps[b, BLOCK:] = fresh_keys.astype(BF16)
-            carry_end = carry[BLOCK - 1 : BLOCK]
-            carry_out[b] = carry_end * key_eye - mm_right(key, tail * fresh_keys, TN)
+            carry_out[b] = mm_right(key, tail * fresh_keys, TN).astype(BF16)
             add_part[b] = mm_right(key, tail * fresh_values, TN)
         return 0
 
@@ -209,10 +203,12 @@
         copy.start()
 
     def chain(b, state):
-        state_out[b] = state.astype(BF16)
-        return mm_both(carry_out[b], state) + add_part[b]
-
-    lax.fori_loop(0, blocks, chain, jnp.zeros((KEY_SIZE, DV), F32))
+        low = state.astype(BF16)
+        state_out[b] = low
+        carry = cols[pl.ds(pl.multiple_of(b * BLOCK + BLOCK - 8, 8), 8), 0:1][7:]
+        return carry * state + (add_part[b] - mm(carry_out[b], low))
+
+    lax.fori_loop(0, blocks, chain, jnp.zeros((KEY_SIZE, DV), F32), unroll=8)
     for copy in chained:
         copy.start()
 
@@ -347,10 +343,12 @@
 
     def chain(step, state):
         b = blocks - 1 - step
-        end_state[b] = state.astype(BF16)
-        return mm_both(carry_in[b], state, TN) + pull_part[b]
-
-    lax.fori_loop(0, blocks, chain, jnp.zeros((KEY_SIZE, DV), F32))
+        low = state.astype(BF16)
+        end_state[b] = low
+        carry = cols[pl.ds(pl.multiple_of(b * BLOCK + BLOCK - 8, 8), 8), 0:1][7:]
+        return carry * state + (pull_part[b] - mm(carry_in[b], low, TN))
+
+    lax.fori_loop(0, blocks, chain, jnp.zeros((KEY_SIZE, DV), F32), unroll=8)
     for copy in late_loads:
         copy.wait()
 
@@ -449,7 +447,7 @@
             shape((tokens, BLOCK), F32),
             shape((blocks, KEY_SIZE, DV), BF16),
             shape((tokens, DV), BF16),
-            shape((blocks, KEY_SIZE, KEY_SIZE), F32),
+            shape((blocks, KEY_SIZE, KEY_SIZE), BF16),
             shape((tokens, KEY_SIZE), BF16),
         ),
         in_specs=[SMEM_SPEC] + [ANY_SPEC] * 2 + [VMEM_SPEC] * 5,
@@ -460,7 +458,7 @@
             pltpu.VMEM((tokens, BLOCK), F32),
             pltpu.VMEM((blocks, KEY_SIZE, DV), BF16),
             pltpu.VMEM((tokens, DV), BF16),
-            pltpu.VMEM((blocks, KEY_SIZE, KEY_SIZE), F32),
+            pltpu.VMEM((blocks, KEY_SIZE, KEY_SIZE), BF16),
             pltpu.VMEM((tokens, KEY_SIZE), BF16),
             pltpu.VMEM((blocks, 2 * BLOCK, KEY_SIZE), BF16),
             pltpu.VMEM((tokens, DV), F32),
@@ -496,7 +494,7 @@
             pltpu.VMEM((tokens, BLOCK), F32),
             pltpu.VMEM((blocks, KEY_SIZE, DV), BF16),
             pltpu.VMEM((tokens, DV), BF16),
-            pltpu.VMEM((blocks, KEY_SIZE, KEY_SIZE), F32),
+            pltpu.VMEM((blocks, KEY_SIZE, KEY_SIZE), BF16),
             pltpu.VMEM((tokens, KEY_SIZE), BF16),
             pltpu.VMEM((tokens, DV), BF16),
             pltpu.VMEM((blocks, KEY_SIZE, DV), F32),
@@ -741,6 +739,14 @@
 
 def send_far(halves):
     return send(halves[0], along_x), send(halves[1], along_y)
+
+
+def by_planes(own, others):
+    return stacked([piece for pair in zip(own, others) for part in pair for piece in part])
+
+
+def four_blocks(near, far):
+    return [near[0]], [near[1]], [near[2]], list(far)
 
 
 def far_parts(parts):
@@ -847,10 +853,14 @@
     )
     in_payload = in_order(in_kept, swap_cores(in_given), 0)
     one_levels = gather_levels(normed_one.astype(BF16))
+    one_own = send_near(one_levels[0])
+    one_own, one_levels = after((one_own, one_levels))
     in_mine = exchange(after(in_payload, one_levels))
-    one_near = send_near(stacked(one_levels))
-    in_mine = after(in_mine, one_near)
-    normed_all = stacked(one_near + send_far(far_halves(one_near)))
+    one_near, one_own_far = send_near(stacked(one_levels[1:])), send_far(far_halves(one_own))
+    one_near, one_own_far, in_mine = after((one_near, one_own_far, in_mine))
+    normed_all = by_planes(
+        four_blocks(one_own, one_own_far), four_blocks(one_near, send_far(far_halves(one_near)))
+    )
     weights_all = joined_by_core(in_mine)
     weights_in, weights_out = weights_all[:, :PACK], weights_all[:, PACK:]
 
@@ -916,7 +926,7 @@
     scale_two = lax.rsqrt(jnp.mean(middle * middle, axis=-1, keepdims=True) + EPSILON)
     normed_mid = middle * scale_two
     mid = normed_mid.astype(BF16)
-    mid_sent, cot_far = gather_levels(mid), send_far(far_halves(after(cot, mid)))
+    mid_sent, mid_own, cot_far = gather_levels(mid), send_near(mid), send_far(far_halves(after(cot, mid)))
     feed_mine, feed_other = after((feed_mine, feed_other), mid)
 
     def unit_rows(position):
@@ -929,17 +939,15 @@
 
     gate_rows, up_rows, down_rows = unit_rows(0), unit_rows(1), unit_rows(2)
     mid = mid_sent
-    mid, cot_far, gate_rows, up_rows, down_rows = after((mid, cot_far, gate_rows, up_rows, down_rows))
-    mid = stacked(mid)
+    mid, mid_own, cot_far, gate_rows, up_rows, down_rows = after(
+        (mid, mid_own, cot_far, gate_rows, up_rows, down_rows)
+    )
+    mid = stacked(mid[1:])
     cot_all = stacked(after(cot, mid) + cot_far)
-    cut = after(normed_all, mid).reshape(own_count, CHIPS, CORES, half_count)
-    cut_mine = lax.dynamic_index_in_dim(cut, core, 2, False).reshape(own_count, width // CORES)
-    cut_given = lax.dynamic_index_in_dim(cut, 1 - core, 2, False).reshape(own_count, width // CORES)
-    mid = send_near(mid)
+    mid, mid_own_far = send_near(mid), send_far(far_halves(mid_own))
     d_hidden = nt(cot_all, down_rows).astype(BF16)
-    mid, d_hidden, cut_mine, cut_given = after((mid, d_hidden, cut_mine, cut_given))
-    cut_other = swap_cores(cut_given)
-    mid_all = stacked(mid + send_far(far_halves(mid)))
+    mid, mid_own_far, d_hidden = after((mid, mid_own_far, d_hidden))
+    mid_all = by_planes(four_blocks(mid_own, mid_own_far), four_blocks(mid, send_far(far_halves(mid))))
 
     gate_lin = nt(mid_all, gate_rows)
     up_lin = nt(mid_all, up_rows)
@@ -958,7 +966,13 @@
     parts = [tn(d_gate, mid_all), tn(d_up, mid_all), tn(hidden, cot_all)]
     keep_part = stacked([part[:units] for part in parts])
     give_part = stacked([part[units:] for part in parts]).astype(BF16)
-    near, feed_parts, keep_part, give_part = after((near, feed_parts, keep_part, give_part))
+    cut = after(normed_all, e_parts).reshape(own_count, CHIPS, CORES, half_count)
+    cut_mine = lax.dynamic_index_in_dim(cut, core, 2, False).reshape(own_count, width // CORES)
+    cut_given = lax.dynamic_index_in_dim(cut, 1 - core, 2, False).reshape(own_count, width // CORES)
+    near, feed_parts, keep_part, give_part, cut_mine, cut_given = after(
+        (near, feed_parts, keep_part, give_part, cut_mine, cut_given)
+    )
+    cut_other = swap_cores(cut_given)
     levels = level_parts(e_parts, *near)
     levels, feed_far = send_levels(levels), send_far(far_parts(after(feed_parts, levels)))
     levels, feed_far = after((levels, feed_far))

time: 646 us -> 642 us (level)
  starting transfers between devices: 127 us -> 137 us
  waiting for transfers between devices: 261 us -> 252 us
    ppermute x56 -> x64, starting transfers between devices: 88.6 us -> 103 us  [send(): lax.ppermute(value, 'seq', [(index, target(index)) for index in range(CHI...]
    ppermute x56 -> x64, waiting for transfers between devices: 256 us -> 245 us  [send(): lax.ppermute(value, 'seq', [(index, target(index)) for index in range(CHI...]
    unnamed x164 -> x179, local copies, waits for them, and re-layouts: 36.3 us -> 28.8 us
  transfers between devices with their start and end apart: 74 -> 82, of which waited for: 35 -> 38; matrix products, arithmetic and copies ran while one was open for 19% -> 19% of each run, Pallas kernels for 12% -> 11%
where the time goes in v5:
time: 642 us; the launch traced here: 634 us
  waiting for transfers between devices  252 us (39%)
  starting transfers between devices  137 us (21%)
  Pallas kernels  74.9 us (12%)
  local copies, waits for them, and re-layouts  68.4 us (11%)
  other arithmetic  50.8 us (8%)
  matrix products  47.9 us (7%)
    ppermute x64, waiting for transfers between devices, send(): lax.ppermute(value, 'seq', [(index, target(index)) for index in range(CHI...  245 us
    ppermute x64, starting transfers between devices, send(): lax.ppermute(value, 'seq', [(index, target(index)) for index in range(CHI...  103 us
    dot_general x16, matrix products, mm(): return lax.dot_general(a, b, (dims, ((), ())), preferred_element_type=F32)  47.9 us
    pallas_call x1, Pallas kernels, mixer_backward(): pl.pallas_call(backward_kernel, out_shape=(shape((half, PACK), BF16), sha...  36.9 us
    all_to_all x4, starting transfers between devices, exchange(): lax.all_to_all(pieces, 'seq', split_axis=0, concat_axis=0, tiled=True)  30.8 us
    pallas_call x1, Pallas kernels, mixer_forward(): pl.pallas_call(forward_kernel, out_shape=(shape((half, DV), BF16), shape(...  30.6 us
    unnamed x179, local copies, waits for them, and re-layouts  28.8 us
  transfers between devices with their start and end apart: 82, of which 38 were waited for; matrix products, arithmetic and copies ran while one was open for 19% of the time, Pallas kernels for 11%

profile of v5, /device:TPU:0, one launch (start us, length us, event | category | flops | bytes accessed | tf_op | source)
XLA Modules:
  0.0 634.1 jit_solution(13273580395317088765)
XLA Ops:
  4.7 5.2 pack_heads.1
  10.6 4.7 collective-permute-start.4
  23.5 14.7 %collective-permute-done.3 = bf16[64,2048]{1,0:T(8,128)(2,1)S(1)} collective-permute-done((bf16[64,2048]{1,0:T(8,128)(2,1)S(1)}, bf16[64,2048]{1,0:T(8,128)(2,1)S(1)}, u32[]{:S(2)}, u32[]{:S(2)}) %collective-permute-start.3) | collective-permute-done | bytes 262176 | tf_op jit(solution)/shard_map/ppermute | solution.py:700
  41.9 6.1 all-to-all-start
  62.6 31.5 %collective-permute-done.8 = bf16[32,2048]{1,0:T(8,128)(2,1)S(1)} collective-permute-done((bf16[32,2048]{1,0:T(8,128)(2,1)S(1)}, bf16[32,2048]{1,0:T(8,128)(2,1)S(1)}, u32[]{:S(2)}, u32[]{:S(2)}) %collective-permute-start.8) | collective-permute-done | bytes 131104 | tf_op jit(solution)/shard_map/ppermute | solution.py:700
  106.1 7.9 %collective-permute-done.10 = bf16[96,2048]{1,0:T(8,128)(2,1)S(1)} collective-permute-done((bf16[96,2048]{1,0:T(8,128)(2,1)S(1)}, bf16[96,2048]{1,0:T(8,128)(2,1)S(1)}, u32[]{:S(2)}, u32[]{:S(2)}) %collective-permute-start.10) | collective-permute-done | bytes 393248 | tf_op jit(solution)/shard_map/ppermute | solution.py:700
  120.0 5.6 fusion.pre_own
  125.7 6.1 all-to-all-start.1
  135.2 30.6 %mixer_forward.1 = (bf16[1024,256]{1,0:T(8,128)(2,1)S(1)}, bf16[1024,256]{1,0:T(8,128)(2,1)}, f32[2048,256]{1,0:T(8,128)}, f32[2048,512]{1,0:T(8,128)}, f32[2048...) custom-call(s32[32]{0:T(128)S(1)} %fusion.32.place, ...), custom_call_target="tpu_custom_call" | custom-call | flops 30000001024 | bytes 100000000 | tf_op jit(solution)/shard_map/mixer_forward/pallas_call | solution.py:440
  176.1 11.1 %collective-permute-done.16 = bf16[128,2048]{1,0:T(8,128)(2,1)S(1)} collective-permute-done((bf16[128,2048]{1,0:T(8,128)(2,1)}, bf16[128,2048]{1,0:T(8,128)(2,1)S(1)}, u32[]{:S(2)}, u32[]{:S(2)}) %collective-permute-start.16) | collective-permute-done | bytes 524320 | tf_op jit(solution)/shard_map/ppermute | solution.py:700
  194.1 4.8 collective-permute-start.21
  199.6 6.1 collective-permute-done.21
  205.7 15.3 %collective-permute-done.20 = bf16[64,2048]{1,0:T(8,128)(2,1)S(1)} collective-permute-done((bf16[64,2048]{1,0:T(8,128)(2,1)S(1)}, bf16[64,2048]{1,0:T(8,128)(2,1)S(1)}, u32[]{:S(2)}, u32[]{:S(2)}) %collective-permute-start.20) | collective-permute-done | bytes 262176 | tf_op jit(solution)/shard_map/ppermute | solution.py:700
  232.1 7.9 %collective-permute-done.24 = bf16[64,2048]{1,0:T(8,128)(2,1)S(1)} collective-permute-done((bf16[64,2048]{1,0:T(8,128)(2,1)S(1)}, bf16[64,2048]{1,0:T(8,128)(2,1)S(1)}, u32[]{:S(2)}, u32[]{:S(2)}) %collective-permute-start.24) | collective-permute-done | bytes 262176 | tf_op jit(solution)/shard_map/ppermute | solution.py:700
  240.0 8.3 %collective-permute-done.23 = bf16[64,2048]{1,0:T(8,128)(2,1)S(1)} collective-permute-done((bf16[64,2048]{1,0:T(8,128)(2,1)}, bf16[64,2048]{1,0:T(8,128)(2,1)S(1)}, u32[]{:S(2)}, u32[]{:S(2)}) %collective-permute-start.23) | collective-permute-done | bytes 262176 | tf_op jit(solution)/shard_map/ppermute | solution.py:700
  248.3 6.6 %collective-permute-done.22 = bf16[64,2048]{1,0:T(8,128)(2,1)} collective-permute-done((bf16[64,2048]{1,0:T(8,128)(2,1)S(1)}, bf16[64,2048]{1,0:T(8,128)(2,1)}, u32[]{:S(2)}, u32[]{:S(2)}) %collective-permute-start.22) | collective-permute-done | bytes 262176 | tf_op jit(solution)/shard_map/ppermute | solution.py:700
  269.4 10.5 %collective-permute-start.27 = (bf16[64,2048]{1,0:T(8,128)(2,1)S(1)}, bf16[64,2048]{1,0:T(8,128)(2,1)S(1)}, u32[]{:S(2)}, u32[]{:S(2)}) collective-permute-start(bf16[64,2048]{1,0:T(8,128)(2,1)S(1)} %multiply_convert_fusion.1), channel_id=1, source_target_pairs={{0,8},{2,10},{4,12},{6,14},{8,16},{10,18},{12,20},{14,22},{16,24},... | collective-permute-start | bytes 786440 | tf_op jit(solution)/shard_map/ppermute | solution.py:700
  280.9 5.2 collective-permute-done.27
  294.9 10.5 %collective-permute-done.38 = bf16[32,2048]{1,0:T(8,128)(2,1)S(1)} collective-permute-done((bf16[32,2048]{1,0:T(8,128)(2,1)S(1)}, bf16[32,2048]{1,0:T(8,128)(2,1)S(1)}, u32[]{:S(2)}, u32[]{:S(2)}) %collective-permute-start.38) | collective-permute-done | bytes 131104 | tf_op jit(solution)/shard_map/ppermute | solution.py:700
  310.5 4.7 collective-permute-done.39
  351.5 6.4 %copy.122 = bf16[1024,2048]{0,1:T(8,128)(2,1)} copy(bf16[1024,2048]{1,0:T(8,128)(2,1)} %copy-done.17) | data formatting | bytes 8388608 | tf_op jit(solution)/shard_map/optimization_barrier | solution.py:712
  357.9 5.0 constant_dynamic-slice_fusion.3
  381.4 4.7 collective-permute-done.46
  391.0 8.2 %collective-permute-start.52 = (bf16[64,2048]{1,0:T(8,128)(2,1)S(1)}, bf16[64,2048]{1,0:T(8,128)(2,1)S(1)}, u32[]{:S(2)}, u32[]{:S(2)}) collective-permute-start(bf16[64,2048]{1,0:T(8,128)(2,1)S(1)} %get-tuple-element.242), channel_id=1, source_target_pairs={{0,24},{2,26},{4,28},{6,30},{8,0},{10,2},{12,4},{14,6},{16,8},{18,... | collective-permute-start | bytes 786440 | tf_op jit(solution)/shard_map/ppermute | solution.py:700
  399.2 5.1 collective-permute-start.51
  407.1 19.2 %collective-permute-done.51 = bf16[64,2048]{1,0:T(8,128)(2,1)S(1)} collective-permute-done((bf16[64,2048]{1,0:T(8,128)(2,1)S(1)}, bf16[64,2048]{1,0:T(8,128)(2,1)S(1)}, u32[]{:S(2)}, u32[]{:S(2)}) %collective-permute-start.51) | collective-permute-done | bytes 262176 | tf_op jit(solution)/shard_map/ppermute | solution.py:700
  447.2 8.2 %collective-permute-done.61 = bf16[128,2048]{1,0:T(8,128)(2,1)S(1)} collective-permute-done((bf16[128,2048]{1,0:T(8,128)(2,1)S(1)}, bf16[128,2048]{1,0:T(8,128)(2,1)S(1)}, u32[]{:S(2)}, u32[]{:S(2)}) %collective-permute-start.61) | collective-permute-done | bytes 524320 | tf_op jit(solution)/shard_map/ppermute | solution.py:700
  471.6 36.9 %mixer_backward.1 = (bf16[1024,896]{1,0:T(8,128)(2,1)}, bf16[1024,896]{1,0:T(8,128)(2,1)}, f32[4,8,512]{2,1,0:T(8,128)S(1)}, f32[8,256]{1,0:T(8,128)S(1)}) custom-call(s32[32]{0:T(128)S(1)} %fusion.32.place, bf16[1024,256]{1,0:T(8,128)(2,1)S(1)} %convolution_convert_fusion.5.d_gated_own, bf16[1024,256]{1,0:T(8,128)(2,1)S(1)} %collective-permute-done.63.d_gated_other, ...), custom_call_target="tpu_custom_call" | custom-call | flops 1000000 | bytes 1000 | tf_op jit(solution)/shard_map/mixer_backward/pallas_call | solution.py:481
  518.9 13.9 %all-to-all-start.3 = ((bf16[16,64,896]{2,1,0:T(8,128)(2,1)}), bf16[16,64,896]{2,1,0:T(8,128)(2,1)S(1)}, u32[]{:S(2)}, u32[]{:S(2)}) async-start(bf16[16,64,896]{2,1,0:T(8,128)(2,1)} %add_convert_fusion.2), calls=%async_computation.3 | async-start | bytes 3670016 | tf_op jit(solution)/shard_map/all_to_all | solution.py:708
  532.9 7.1 %convolution_convert_fusion.2 = bf16[1024,2048]{1,0:T(8,128)(2,1)S(1)} fusion(bf16[1024,896]{1,0:T(8,128)(2,1)} %get-tuple-element.268, bf16[2048,1152]{1,0:T(8,128)(2,1)} %bitcast.157), kind=kOutput, calls=%fused_computation.7 | convolution fusion | flops 3760193536 | bytes 9699328 | tf_op jit(solution)/shard_map/dot_general | solution.py:23
  543.6 19.3 %collective-permute-done.68 = bf16[128,2048]{1,0:T(8,128)(2,1)S(1)} collective-permute-done((bf16[128,2048]{1,0:T(8,128)(2,1)S(1)}, bf16[128,2048]{1,0:T(8,128)(2,1)S(1)}, u32[]{:S(2)}, u32[]{:S(2)}) %collective-permute-start.68) | collective-permute-done | bytes 524320 | tf_op jit(solution)/shard_map/ppermute | solution.py:700
  571.7 21.2 %collective-permute-done.67 = bf16[256,2048]{1,0:T(8,128)(2,1)} collective-permute-done((bf16[256,2048]{1,0:T(8,128)(2,1)}, bf16[256,2048]{1,0:T(8,128)(2,1)}, u32[]{:S(2)}, u32[]{:S(2)}) %collective-permute-start.67) | collective-permute-done | bytes 1048608 | tf_op jit(solution)/shard_map/ppermute | solution.py:700
  (491 shorter events, 272.4 us)
Async XLA Ops:
  9.8 28.5 %collective-permute-start.9 = (bf16[8,64,1152]{2,1,0:T(8,128)(2,1)}, bf16[8,64,1152]{2,1,0:T(8,128)(2,1)S(1)}, u32[]{:S(2)}, u32[]{:S(2)}) collective-permute-start(bf16[8,64,1152]{2,1,0:T(8,128)(2,1)} %get-tuple-element.168), channel_id=1, source_target_pairs={{0,1},{1,0},{2,3},{3,2},{4,5},{5,4},{6,7},{7,6},{8,9},{9,8},{10,11... | collective-permute-start | bytes 3538952 | tf_op jit(solution)/shard_map/ppermute | solution.py:704
  15.3 23.0 %collective-permute-start.3 = (bf16[64,2048]{1,0:T(8,128)(2,1)S(1)}, bf16[64,2048]{1,0:T(8,128)(2,1)S(1)}, u32[]{:S(2)}, u32[]{:S(2)}) collective-permute-start(bf16[64,2048]{1,0:T(8,128)(2,1)S(1)} %fusion.20), channel_id=1, source_target_pairs={{0,16},{2,18},{4,20},{6,22},{8,24},{10,26},{12,28},{14,30},{16,0},... | collective-permute-start | bytes 786440 | tf_op jit(solution)/shard_map/ppermute | solution.py:700
  15.3 23.0 %collective-permute-start.2 = (bf16[64,2048]{1,0:T(8,128)(2,1)S(1)}, bf16[64,2048]{1,0:T(8,128)(2,1)S(1)}, u32[]{:S(2)}, u32[]{:S(2)}) collective-permute-start(bf16[64,2048]{1,0:T(8,128)(2,1)S(1)} %fusion.20), channel_id=1, source_target_pairs={{0,8},{2,10},{4,12},{6,14},{8,16},{10,18},{12,20},{14,22},{16,24},... | collective-permute-start | bytes 786440 | tf_op jit(solution)/shard_map/ppermute | solution.py:700
  16.3 22.0 %collective-permute-start.1 = (bf16[64,2048]{1,0:T(8,128)(2,1)S(1)}, bf16[64,2048]{1,0:T(8,128)(2,1)S(1)}, u32[]{:S(2)}, u32[]{:S(2)}) collective-permute-start(bf16[64,2048]{1,0:T(8,128)(2,1)S(1)} %fusion.20), channel_id=1, source_target_pairs={{0,4},{2,6},{4,0},{6,2},{8,12},{10,14},{12,8},{14,10},{16,20},{18,... | collective-permute-start | bytes 786440 | tf_op jit(solution)/shard_map/ppermute | solution.py:700
  41.9 58.3 %all-to-all-start = ((bf16[16,64,1152]{2,1,0:T(8,128)(2,1)}), bf16[16,64,1152]{2,1,0:T(8,128)(2,1)S(1)}, u32[]{:S(2)}, u32[]{:S(2)}) async-start(bf16[16,64,1152]{2,1,0:T(8,128)(2,1)} %pad_maximum_fusion.2), calls=%async_computation | async-start | bytes 4718592 | tf_op jit(solution)/shard_map/all_to_all | solution.py:708
  48.1 77.6 %collective-permute-start.14 = (bf16[8,4,512]{2,1,0:T(4,128)(2,1)S(1)}, bf16[8,4,512]{2,1,0:T(4,128)(2,1)S(1)}, u32[]{:S(2)}, u32[]{:S(2)}) collective-permute-start(bf16[8,4,512]{2,1,0:T(4,128)(2,1)S(1)} %maximum_bitcast_fusion), channel_id=1, source_target_pairs={{0,1},{1,0},{2,3},{3,2},{4,5},{5,4},{6,7},{7,6},{8,9},{9,8},{10,11... | collective-permute-start | bytes 98312 | tf_op jit(solution)/shard_map/ppermute | solution.py:704
  55.3 43.4 %collective-permute-start.6 = (bf16[192,2048]{1,0:T(8,128)(2,1)S(1)}, bf16[192,2048]{1,0:T(8,128)(2,1)S(1)}, u32[]{:S(2)}, u32[]{:S(2)}) collective-permute-start(bf16[192,2048]{1,0:T(8,128)(2,1)S(1)} %constant_dynamic-update-slice_fusion), channel_id=1, source_target_pairs={{0,4},{2,6},{4,0},{6,2},{8,12},{10,14},{12,8},{14,10},{16,20},{18,... | collective-permute-start | bytes 2359304 | tf_op jit(solution)/shard_map/ppermute | solution.py:700
  57.2 42.9 %collective-permute-start.5 = (bf16[192,2048]{1,0:T(8,128)(2,1)S(1)}, bf16[192,2048]{1,0:T(8,128)(2,1)}, u32[]{:S(2)}, u32[]{:S(2)}) collective-permute-start(bf16[192,2048]{1,0:T(8,128)(2,1)S(1)} %constant_dynamic-update-slice_fusion), channel_id=1, source_target_pairs={{0,2},{2,0},{4,6},{6,4},{8,10},{10,8},{12,14},{14,12},{16,18},{18,... | collective-permute-start | bytes 2359304 | tf_op jit(solution)/shard_map/ppermute | solution.py:700
  60.3 33.8 %collective-permute-start.8 = (bf16[32,2048]{1,0:T(8,128)(2,1)S(1)}, bf16[32,2048]{1,0:T(8,128)(2,1)S(1)}, u32[]{:S(2)}, u32[]{:S(2)}) collective-permute-start(bf16[32,2048]{1,0:T(8,128)(2,1)S(1)} %slice.289), channel_id=1, source_target_pairs={{0,4},{2,6},{4,0},{6,2},{8,12},{10,14},{12,8},{14,10},{16,20},{18,... | collective-permute-start | bytes 393224 | tf_op jit(solution)/shard_map/ppermute | solution.py:700
  60.9 37.8 %collective-permute-start.7 = (bf16[32,2048]{1,0:T(8,128)(2,1)S(1)}, bf16[32,2048]{1,0:T(8,128)(2,1)S(1)}, u32[]{:S(2)}, u32[]{:S(2)}) collective-permute-start(bf16[32,2048]{1,0:T(8,128)(2,1)S(1)} %slice.288), channel_id=1, source_target_pairs={{0,2},{2,0},{4,6},{6,4},{8,10},{10,8},{12,14},{14,12},{16,18},{18,... | collective-permute-start | bytes 393224 | tf_op jit(solution)/shard_map/ppermute | solution.py:700
  125.7 50.4 %all-to-all-start.1 = ((bf16[16,528,128]{2,1,0:T(8,128)(2,1)}), bf16[16,528,128]{2,1,0:T(8,128)(2,1)}, u32[]{:S(2)}, u32[]{:S(2)}) async-start(bf16[16,528,128]{2,1,0:T(8,128)(2,1)} %pad_maximum_fusion.3), calls=%async_computation.1 | async-start | bytes 4325376 | tf_op jit(solution)/shard_map/all_to_all | solution.py:708
  190.3 30.8 %collective-permute-start.17 = (bf16[256,2048]{1,0:T(8,128)(2,1)S(1)}, bf16[256,2048]{1,0:T(8,128)(2,1)S(1)}, u32[]{:S(2)}, u32[]{:S(2)}) collective-permute-start(bf16[256,2048]{1,0:T(8,128)(2,1)S(1)} %pad_maximum_fusion.9), channel_id=1, source_target_pairs={{0,2},{2,0},{4,6},{6,4},{8,10},{10,8},{12,14},{14,12},{16,18},{18,... | collective-permute-start | bytes 3145736 | tf_op jit(solution)/shard_map/ppermute | solution.py:700
  191.0 30.1 %collective-permute-start.18 = (bf16[256,2048]{1,0:T(8,128)(2,1)S(1)}, bf16[256,2048]{1,0:T(8,128)(2,1)S(1)}, u32[]{:S(2)}, u32[]{:S(2)}) collective-permute-start(bf16[256,2048]{1,0:T(8,128)(2,1)S(1)} %pad_maximum_fusion.10), channel_id=1, source_target_pairs={{0,4},{2,6},{4,0},{6,2},{8,12},{10,14},{12,8},{14,10},{16,20},{18,... | collective-permute-start | bytes 3145736 | tf_op jit(solution)/shard_map/ppermute | solution.py:700
  198.9 22.2 %collective-permute-start.20 = (bf16[64,2048]{1,0:T(8,128)(2,1)S(1)}, bf16[64,2048]{1,0:T(8,128)(2,1)S(1)}, u32[]{:S(2)}, u32[]{:S(2)}) collective-permute-start(bf16[64,2048]{1,0:T(8,128)(2,1)S(1)} %constant_dynamic-slice_fusion.5), channel_id=1, source_target_pairs={{0,16},{2,18},{4,20},{6,22},{8,24},{10,26},{12,28},{14,30},{16,0},... | collective-permute-start | bytes 786440 | tf_op jit(solution)/shard_map/ppermute | solution.py:700
  205.7 58.5 %collective-permute-start.34 = (bf16[16,528,128]{2,1,0:T(8,128)(2,1)}, bf16[16,528,128]{2,1,0:T(8,128)(2,1)}, u32[]{:S(2)}, u32[]{:S(2)}) collective-permute-start(bf16[16,528,128]{2,1,0:T(8,128)(2,1)} %all-to-all-done.1), channel_id=1, source_target_pairs={{0,1},{1,0},{2,3},{3,2},{4,5},{5,4},{6,7},{7,6},{8,9},{9,8},{10,11... | collective-permute-start | bytes 6488072 | tf_op jit(solution)/shard_map/ppermute | solution.py:704
  227.3 27.6 %collective-permute-start.26 = (bf16[256,2048]{1,0:T(8,128)(2,1)}, bf16[256,2048]{1,0:T(8,128)(2,1)S(1)}, u32[]{:S(2)}, u32[]{:S(2)}) collective-permute-start(bf16[256,2048]{1,0:T(8,128)(2,1)} %constant_dynamic-update-slice_fusion.13), channel_id=1, source_target_pairs={{0,4},{2,6},{4,0},{6,2},{8,12},{10,14},{12,8},{14,10},{16,20},{18,... | collective-permute-start | bytes 3145736 | tf_op jit(solution)/shard_map/ppermute | solution.py:700
  229.0 25.9 %collective-permute-start.25 = (bf16[256,2048]{1,0:T(8,128)(2,1)}, bf16[256,2048]{1,0:T(8,128)(2,1)}, u32[]{:S(2)}, u32[]{:S(2)}) collective-permute-start(bf16[256,2048]{1,0:T(8,128)(2,1)} %constant_dynamic-update-slice_fusion.13), channel_id=1, source_target_pairs={{0,2},{2,0},{4,6},{6,4},{8,10},{10,8},{12,14},{14,12},{16,18},{18,... | collective-permute-start | bytes 3145736 | tf_op jit(solution)/shard_map/ppermute | solution.py:700
  258.6 22.1 %collective-permute-start.29 = (bf16[64,2048]{1,0:T(8,128)(2,1)S(1)}, bf16[64,2048]{1,0:T(8,128)(2,1)S(1)}, u32[]{:S(2)}, u32[]{:S(2)}) collective-permute-start(bf16[64,2048]{1,0:T(8,128)(2,1)S(1)} %multiply_convert_fusion.1), channel_id=1, source_target_pairs={{0,24},{2,26},{4,28},{6,30},{8,0},{10,2},{12,4},{14,6},{16,8},{18,... | collective-permute-start | bytes 786440 | tf_op jit(solution)/shard_map/ppermute | solution.py:700
  262.5 23.6 %collective-permute-start.33 = (bf16[128,2048]{1,0:T(8,128)(2,1)S(1)}, bf16[128,2048]{1,0:T(8,128)(2,1)S(1)}, u32[]{:S(2)}, u32[]{:S(2)}) collective-permute-start(bf16[128,2048]{1,0:T(8,128)(2,1)S(1)} %slice.314), channel_id=1, source_target_pairs={{0,4},{2,6},{4,0},{6,2},{8,12},{10,14},{12,8},{14,10},{16,20},{18,... | collective-permute-start | bytes 1572872 | tf_op jit(solution)/shard_map/ppermute | solution.py:700
  381.4 22.8 %collective-permute-start.55 = (bf16[528,2048]{1,0:T(8,128)(2,1)S(1)}, bf16[528,2048]{1,0:T(8,128)(2,1)S(1)}, u32[]{:S(2)}, u32[]{:S(2)}) collective-permute-start(bf16[528,2048]{1,0:T(8,128)(2,1)S(1)} %pad_maximum_fusion.4), channel_id=1, source_target_pairs={{0,1},{1,0},{2,3},{3,2},{4,5},{5,4},{6,7},{7,6},{8,9},{9,8},{10,11... | collective-permute-start | bytes 6488072 | tf_op jit(solution)/shard_map/ppermute | solution.py:704
  388.0 38.3 %collective-permute-start.53 = (bf16[256,2048]{1,0:T(8,128)(2,1)S(1)}, bf16[256,2048]{1,0:T(8,128)(2,1)S(1)}, u32[]{:S(2)}, u32[]{:S(2)}) collective-permute-start(bf16[256,2048]{1,0:T(8,128)(2,1)S(1)} %pad_maximum_fusion.13), channel_id=1, source_target_pairs={{0,2},{2,0},{4,6},{6,4},{8,10},{10,8},{12,14},{14,12},{16,18},{18,... | collective-permute-start | bytes 3145736 | tf_op jit(solution)/shard_map/ppermute | solution.py:700
  389.0 37.3 %collective-permute-start.54 = (bf16[256,2048]{1,0:T(8,128)(2,1)S(1)}, bf16[256,2048]{1,0:T(8,128)(2,1)S(1)}, u32[]{:S(2)}, u32[]{:S(2)}) collective-permute-start(bf16[256,2048]{1,0:T(8,128)(2,1)S(1)} %pad_maximum_fusion.14), channel_id=1, source_target_pairs={{0,4},{2,6},{4,0},{6,2},{8,12},{10,14},{12,8},{14,10},{16,20},{18,... | collective-permute-start | bytes 3145736 | tf_op jit(solution)/shard_map/ppermute | solution.py:700
  399.2 27.1 %collective-permute-start.51 = (bf16[64,2048]{1,0:T(8,128)(2,1)S(1)}, bf16[64,2048]{1,0:T(8,128)(2,1)S(1)}, u32[]{:S(2)}, u32[]{:S(2)}) collective-permute-start(bf16[64,2048]{1,0:T(8,128)(2,1)S(1)} %get-tuple-element.242), channel_id=1, source_target_pairs={{0,16},{2,18},{4,20},{6,22},{8,24},{10,26},{12,28},{14,30},{16,0},... | collective-permute-start | bytes 786440 | tf_op jit(solution)/shard_map/ppermute | solution.py:700
  404.2 22.0 %collective-permute-start.50 = (bf16[64,2048]{1,0:T(8,128)(2,1)S(1)}, bf16[64,2048]{1,0:T(8,128)(2,1)S(1)}, u32[]{:S(2)}, u32[]{:S(2)}) collective-permute-start(bf16[64,2048]{1,0:T(8,128)(2,1)S(1)} %get-tuple-element.242), channel_id=1, source_target_pairs={{0,8},{2,10},{4,12},{6,14},{8,16},{10,18},{12,20},{14,22},{16,24},... | collective-permute-start | bytes 786440 | tf_op jit(solution)/shard_map/ppermute | solution.py:700
  461.1 57.9 %all-to-all-start.2 = ((bf16[16,656,128]{2,1,0:T(8,128)(2,1)}), bf16[16,656,128]{2,1,0:T(8,128)(2,1)}, u32[]{:S(2)}, u32[]{:S(2)}) async-start(bf16[16,656,128]{2,1,0:T(8,128)(2,1)} %constant_dynamic-update-slice_fusion.44), calls=%async_computation.2 | async-start | bytes 5373952 | tf_op jit(solution)/shard_map/all_to_all | solution.py:708
  465.7 43.0 %collective-permute-start.64 = (bf16[1024,1024]{0,1:T(8,128)(2,1)S(1)}, bf16[1024,1024]{0,1:T(8,128)(2,1)}, u32[]{:S(2)}, u32[]{:S(2)}) collective-permute-start(bf16[1024,1024]{0,1:T(8,128)(2,1)S(1)} %bitcast.168), channel_id=1, source_target_pairs={{0,1},{1,0},{2,3},{3,2},{4,5},{5,4},{6,7},{7,6},{8,9},{9,8},{10,11... | collective-permute-start | bytes 6291464 | tf_op jit(solution)/shard_map/ppermute | solution.py:704
  518.9 73.9 %all-to-all-start.3 = ((bf16[16,64,896]{2,1,0:T(8,128)(2,1)}), bf16[16,64,896]{2,1,0:T(8,128)(2,1)S(1)}, u32[]{:S(2)}, u32[]{:S(2)}) async-start(bf16[16,64,896]{2,1,0:T(8,128)(2,1)} %add_convert_fusion.2), calls=%async_computation.3 | async-start | bytes 3670016 | tf_op jit(solution)/shard_map/all_to_all | solution.py:708
  540.1 22.8 %collective-permute-start.68 = (bf16[128,2048]{1,0:T(8,128)(2,1)S(1)}, bf16[128,2048]{1,0:T(8,128)(2,1)S(1)}, u32[]{:S(2)}, u32[]{:S(2)}) collective-permute-start(bf16[128,2048]{1,0:T(8,128)(2,1)S(1)} %get-tuple-element.394), channel_id=1, source_target_pairs={{0,2},{2,0},{4,6},{6,4},{8,10},{10,8},{12,14},{14,12},{16,18},{18,... | collective-permute-start | bytes 1572872 | tf_op jit(solution)/shard_map/ppermute | solution.py:700
  564.4 28.4 %collective-permute-start.67 = (bf16[256,2048]{1,0:T(8,128)(2,1)}, bf16[256,2048]{1,0:T(8,128)(2,1)}, u32[]{:S(2)}, u32[]{:S(2)}) collective-permute-start(bf16[256,2048]{1,0:T(8,128)(2,1)} %pad_maximum_fusion.15), channel_id=1, source_target_pairs={{0,2},{2,0},{4,6},{6,4},{8,10},{10,8},{12,14},{14,12},{16,18},{18,... | collective-permute-start | bytes 3145736 | tf_op jit(solution)/shard_map/ppermute | solution.py:700
  567.1 25.7 %collective-permute-start.69 = (bf16[256,2048]{1,0:T(8,128)(2,1)}, bf16[256,2048]{1,0:T(8,128)(2,1)}, u32[]{:S(2)}, u32[]{:S(2)}) collective-permute-start(bf16[256,2048]{1,0:T(8,128)(2,1)} %pad_maximum_fusion.16), channel_id=1, source_target_pairs={{0,4},{2,6},{4,0},{6,2},{8,12},{10,14},{12,8},{14,10},{16,20},{18,... | collective-permute-start | bytes 3145736 | tf_op jit(solution)/shard_map/ppermute | solution.py:700
  596.2 27.0 %collective-permute-start.72 = (bf16[64,2048]{1,0:T(8,128)(2,1)}, bf16[64,2048]{1,0:T(8,128)(2,1)}, u32[]{:S(2)}, u32[]{:S(2)}) collective-permute-start(bf16[64,2048]{1,0:T(8,128)(2,1)} %get-tuple-element.435), channel_id=1, source_target_pairs={{0,8},{2,10},{4,12},{6,14},{8,16},{10,18},{12,20},{14,22},{16,24},... | collective-permute-start | bytes 786440 | tf_op jit(solution)/shard_map/ppermute | solution.py:700
  597.1 26.0 %collective-permute-start.71 = (bf16[64,2048]{1,0:T(8,128)(2,1)}, bf16[64,2048]{1,0:T(8,128)(2,1)}, u32[]{:S(2)}, u32[]{:S(2)}) collective-permute-start(bf16[64,2048]{1,0:T(8,128)(2,1)} %get-tuple-element.436), channel_id=1, source_target_pairs={{0,16},{2,18},{4,20},{6,22},{8,24},{10,26},{12,28},{14,30},{16,0},... | collective-permute-start | bytes 786440 | tf_op jit(solution)/shard_map/ppermute | solution.py:700
  (118 other events, 1114.8 us)

commit v6 on v5

--- a/solution.py
+++ b/solution.py
@@ -1011,13 +1011,16 @@
     small = jnp.concatenate([jnp.sum(grad_taps, axis=1).reshape(-1), jnp.sum(grad_gain, axis=0)])
     small = small.reshape(-1, 64)
     small_rows = small.shape[0]
-    grad_in = tn(cut_mine, d_pre_own) + tn(cut_other, d_pre_other)
+    e_parts = nt(d_pre_own, weights_in).astype(BF16)
+    far = far_parts(e_parts)
+    late_own, late_other = after((d_pre_own, d_pre_other), far)
+    far = send_far(far)
+    grad_in = tn(cut_mine, late_own) + tn(cut_other, late_other)
     small = jnp.pad(small, ((0, half_count - small_rows), (PACK - 64, 0)))
     grad_in = (grad_in.reshape(CHIPS, half_count, PACK) + small).astype(BF16)
-    grad_in, feed_back = after((grad_in, feed_back))
-    e_parts = nt(after(d_pre_own, grad_in), weights_in).astype(BF16)
+    grad_in, feed_back, far = after((grad_in, feed_back, far))
     grad_in = exchange(grad_in)
-    near = send_parts(near_parts(e_parts, *send_far(far_parts(e_parts))))
+    near = send_parts(near_parts(e_parts, *far))
     near, grad_in = after((near, grad_in))
     levels = level_parts(e_parts, *near)
     grad_in, feed_back = after((grad_in, feed_back), levels)

time: 642 us -> 635 us (0.989)
  starting transfers between devices: 137 us -> 119 us
  waiting for transfers between devices: 252 us -> 259 us
    ppermute x64, starting transfers between devices: 103 us -> 85.9 us  [send(): lax.ppermute(value, 'seq', [(index, target(index)) for index in range(CHI...]
    ppermute x64, waiting for transfers between devices: 245 us -> 253 us  [send(): lax.ppermute(value, 'seq', [(index, target(index)) for index in range(CHI...]
    unnamed x179 -> x187, local copies, waits for them, and re-layouts: 28.8 us -> 28.9 us
  transfers between devices with their start and end apart: 82 -> 82, of which waited for: 38 -> 38; matrix products, arithmetic and copies ran while one was open for 19% -> 20% of each run, Pallas kernels for 11% -> 11%
where the time goes in v6:
time: 635 us; the launch traced here: 627 us
  waiting for transfers between devices  259 us (41%)
  starting transfers between devices  119 us (19%)
  Pallas kernels  74.7 us (12%)
  local copies, waits for them, and re-layouts  69.4 us (11%)
  other arithmetic  54.6 us (9%)
  matrix products  47 us (7%)
    ppermute x64, waiting for transfers between devices, send(): lax.ppermute(value, 'seq', [(index, target(index)) for index in range(CHI...  253 us
    ppermute x64, starting transfers between devices, send(): lax.ppermute(value, 'seq', [(index, target(index)) for index in range(CHI...  85.9 us
    dot_general x16, matrix products, mm(): return lax.dot_general(a, b, (dims, ((), ())), preferred_element_type=F32)  47 us
    pallas_call x1, Pallas kernels, mixer_backward(): pl.pallas_call(backward_kernel, out_shape=(shape((half, PACK), BF16), sha...  36.7 us
    pallas_call x1, Pallas kernels, mixer_forward(): pl.pallas_call(forward_kernel, out_shape=(shape((half, DV), BF16), shape(...  30.6 us
    all_to_all x4, starting transfers between devices, exchange(): lax.all_to_all(pieces, 'seq', split_axis=0, concat_axis=0, tiled=True)  30.6 us
    unnamed x187, local copies, waits for them, and re-layouts  28.9 us
  transfers between devices with their start and end apart: 82, of which 38 were waited for; matrix products, arithmetic and copies ran while one was open for 20% of the time, Pallas kernels for 11%

profile of v6, /device:TPU:0, one launch (start us, length us, event | category | flops | bytes accessed | tf_op | source)
XLA Modules:
  0.0 626.8 jit_solution(26124010364224724)
XLA Ops:
  4.7 5.2 pack_heads.1
  23.5 14.7 %collective-permute-done.3 = bf16[64,2048]{1,0:T(8,128)(2,1)S(1)} collective-permute-done((bf16[64,2048]{1,0:T(8,128)(2,1)S(1)}, bf16[64,2048]{1,0:T(8,128)(2,1)S(1)}, u32[]{:S(2)}, u32[]{:S(2)}) %collective-permute-start.3) | collective-permute-done | bytes 262176 | tf_op jit(solution)/shard_map/ppermute | solution.py:700
  42.0 6.1 all-to-all-start
  62.6 31.5 %collective-permute-done.8 = bf16[32,2048]{1,0:T(8,128)(2,1)S(1)} collective-permute-done((bf16[32,2048]{1,0:T(8,128)(2,1)S(1)}, bf16[32,2048]{1,0:T(8,128)(2,1)S(1)}, u32[]{:S(2)}, u32[]{:S(2)}) %collective-permute-start.8) | collective-permute-done | bytes 131104 | tf_op jit(solution)/shard_map/ppermute | solution.py:700
  106.2 7.9 %collective-permute-done.10 = bf16[96,2048]{1,0:T(8,128)(2,1)S(1)} collective-permute-done((bf16[96,2048]{1,0:T(8,128)(2,1)S(1)}, bf16[96,2048]{1,0:T(8,128)(2,1)S(1)}, u32[]{:S(2)}, u32[]{:S(2)}) %collective-permute-start.10) | collective-permute-done | bytes 393248 | tf_op jit(solution)/shard_map/ppermute | solution.py:700
  120.1 5.6 fusion.pre_own
  125.8 6.3 %all-to-all-start.1 = ((bf16[16,528,128]{2,1,0:T(8,128)(2,1)}), bf16[16,528,128]{2,1,0:T(8,128)(2,1)}, u32[]{:S(2)}, u32[]{:S(2)}) async-start(bf16[16,528,128]{2,1,0:T(8,128)(2,1)} %pad_maximum_fusion.3), calls=%async_computation.1 | async-start | bytes 4325376 | tf_op jit(solution)/shard_map/all_to_all | solution.py:708
  135.4 30.6 %mixer_forward.1 = (bf16[1024,256]{1,0:T(8,128)(2,1)S(1)}, bf16[1024,256]{1,0:T(8,128)(2,1)}, f32[2048,256]{1,0:T(8,128)}, f32[2048,512]{1,0:T(8,128)}, f32[2048...) custom-call(s32[32]{0:T(128)S(1)} %fusion.32.place, ...), custom_call_target="tpu_custom_call" | custom-call | flops 30000001024 | bytes 100000000 | tf_op jit(solution)/shard_map/mixer_forward/pallas_call | solution.py:440
  176.4 11.1 %collective-permute-done.16 = bf16[128,2048]{1,0:T(8,128)(2,1)S(1)} collective-permute-done((bf16[128,2048]{1,0:T(8,128)(2,1)}, bf16[128,2048]{1,0:T(8,128)(2,1)S(1)}, u32[]{:S(2)}, u32[]{:S(2)}) %collective-permute-start.16) | collective-permute-done | bytes 524320 | tf_op jit(solution)/shard_map/ppermute | solution.py:700
  194.4 4.9 collective-permute-start.21
  199.9 6.1 collective-permute-done.21
  206.0 15.4 %collective-permute-done.20 = bf16[64,2048]{1,0:T(8,128)(2,1)S(1)} collective-permute-done((bf16[64,2048]{1,0:T(8,128)(2,1)S(1)}, bf16[64,2048]{1,0:T(8,128)(2,1)S(1)}, u32[]{:S(2)}, u32[]{:S(2)}) %collective-permute-start.20) | collective-permute-done | bytes 262176 | tf_op jit(solution)/shard_map/ppermute | solution.py:700
  232.4 7.9 %collective-permute-done.24 = bf16[64,2048]{1,0:T(8,128)(2,1)S(1)} collective-permute-done((bf16[64,2048]{1,0:T(8,128)(2,1)S(1)}, bf16[64,2048]{1,0:T(8,128)(2,1)S(1)}, u32[]{:S(2)}, u32[]{:S(2)}) %collective-permute-start.24) | collective-permute-done | bytes 262176 | tf_op jit(solution)/shard_map/ppermute | solution.py:700
  240.3 8.3 %collective-permute-done.23 = bf16[64,2048]{1,0:T(8,128)(2,1)S(1)} collective-permute-done((bf16[64,2048]{1,0:T(8,128)(2,1)}, bf16[64,2048]{1,0:T(8,128)(2,1)S(1)}, u32[]{:S(2)}, u32[]{:S(2)}) %collective-permute-start.23) | collective-permute-done | bytes 262176 | tf_op jit(solution)/shard_map/ppermute | solution.py:700
  248.6 6.6 %collective-permute-done.22 = bf16[64,2048]{1,0:T(8,128)(2,1)} collective-permute-done((bf16[64,2048]{1,0:T(8,128)(2,1)S(1)}, bf16[64,2048]{1,0:T(8,128)(2,1)}, u32[]{:S(2)}, u32[]{:S(2)}) %collective-permute-start.22) | collective-permute-done | bytes 262176 | tf_op jit(solution)/shard_map/ppermute | solution.py:700
  272.6 11.4 %collective-permute-done.28 = bf16[64,2048]{1,0:T(8,128)(2,1)S(1)} collective-permute-done((bf16[64,2048]{1,0:T(8,128)(2,1)S(1)}, bf16[64,2048]{1,0:T(8,128)(2,1)S(1)}, u32[]{:S(2)}, u32[]{:S(2)}) %collective-permute-start.28) | collective-permute-done | bytes 262176 | tf_op jit(solution)/shard_map/ppermute | solution.py:700
  292.8 12.4 %collective-permute-done.38 = bf16[32,2048]{1,0:T(8,128)(2,1)S(1)} collective-permute-done((bf16[32,2048]{1,0:T(8,128)(2,1)S(1)}, bf16[32,2048]{1,0:T(8,128)(2,1)S(1)}, u32[]{:S(2)}, u32[]{:S(2)}) %collective-permute-start.38) | collective-permute-done | bytes 131104 | tf_op jit(solution)/shard_map/ppermute | solution.py:700
  308.5 6.4 %collective-permute-done.39 = bf16[96,2048]{1,0:T(8,128)(2,1)S(1)} collective-permute-done((bf16[96,2048]{1,0:T(8,128)(2,1)S(1)}, bf16[96,2048]{1,0:T(8,128)(2,1)S(1)}, u32[]{:S(2)}, u32[]{:S(2)}) %collective-permute-start.39) | collective-permute-done | bytes 393248 | tf_op jit(solution)/shard_map/ppermute | solution.py:700
  346.8 6.4 %copy.122 = bf16[1024,2048]{0,1:T(8,128)(2,1)} copy(bf16[1024,2048]{1,0:T(8,128)(2,1)} %copy-done.17) | data formatting | bytes 8388608 | tf_op jit(solution)/shard_map/optimization_barrier | solution.py:712
  353.2 5.0 constant_dynamic-slice_fusion.3
  372.6 5.5 collective-permute-done.47
  378.1 6.4 %collective-permute-done.46 = bf16[64,2048]{1,0:T(8,128)(2,1)S(1)} collective-permute-done((bf16[64,2048]{1,0:T(8,128)(2,1)S(1)}, bf16[64,2048]{1,0:T(8,128)(2,1)S(1)}, u32[]{:S(2)}, u32[]{:S(2)}) %collective-permute-start.46) | collective-permute-done | bytes 262176 | tf_op jit(solution)/shard_map/ppermute | solution.py:700
  388.0 4.8 collective-permute-start.52
  399.7 15.8 %collective-permute-done.51 = bf16[64,2048]{1,0:T(8,128)(2,1)S(1)} collective-permute-done((bf16[64,2048]{1,0:T(8,128)(2,1)S(1)}, bf16[64,2048]{1,0:T(8,128)(2,1)S(1)}, u32[]{:S(2)}, u32[]{:S(2)}) %collective-permute-start.51) | collective-permute-done | bytes 262176 | tf_op jit(solution)/shard_map/ppermute | solution.py:700
  423.2 6.4 %collective-permute-done.60 = bf16[64,2048]{1,0:T(8,128)(2,1)S(1)} collective-permute-done((bf16[64,2048]{1,0:T(8,128)(2,1)S(1)}, bf16[64,2048]{1,0:T(8,128)(2,1)S(1)}, u32[]{:S(2)}, u32[]{:S(2)}) %collective-permute-start.60) | collective-permute-done | bytes 262176 | tf_op jit(solution)/shard_map/ppermute | solution.py:700
  429.6 7.6 %collective-permute-done.59 = bf16[64,2048]{1,0:T(8,128)(2,1)S(1)} collective-permute-done((bf16[64,2048]{1,0:T(8,128)(2,1)S(1)}, bf16[64,2048]{1,0:T(8,128)(2,1)S(1)}, u32[]{:S(2)}, u32[]{:S(2)}) %collective-permute-start.59) | collective-permute-done | bytes 262176 | tf_op jit(solution)/shard_map/ppermute | solution.py:700
  442.3 8.7 %collective-permute-done.61 = bf16[128,2048]{1,0:T(8,128)(2,1)S(1)} collective-permute-done((bf16[128,2048]{1,0:T(8,128)(2,1)S(1)}, bf16[128,2048]{1,0:T(8,128)(2,1)S(1)}, u32[]{:S(2)}, u32[]{:S(2)}) %collective-permute-start.61) | collective-permute-done | bytes 524320 | tf_op jit(solution)/shard_map/ppermute | solution.py:700
  456.4 7.7 %all-to-all-start.2 = ((bf16[16,656,128]{2,1,0:T(8,128)(2,1)}), bf16[16,656,128]{2,1,0:T(8,128)(2,1)}, u32[]{:S(2)}, u32[]{:S(2)}) async-start(bf16[16,656,128]{2,1,0:T(8,128)(2,1)} %constant_dynamic-update-slice_fusion.44), calls=%async_computation.2 | async-start | bytes 5373952 | tf_op jit(solution)/shard_map/all_to_all | solution.py:708
  470.2 36.7 %mixer_backward.1 = (bf16[1024,896]{1,0:T(8,128)(2,1)}, bf16[1024,896]{1,0:T(8,128)(2,1)}, f32[4,8,512]{2,1,0:T(8,128)S(1)}, f32[8,256]{1,0:T(8,128)S(1)}) custom-call(s32[32]{0:T(128)S(1)} %fusion.32.place, bf16[1024,256]{1,0:T(8,128)(2,1)S(1)} %convolution_convert_fusion.5.d_gated_own, bf16[1024,256]{1,0:T(8,128)(2,1)S(1)} %collective-permute-done.63.d_gated_other, ...), custom_call_target="tpu_custom_call" | custom-call | flops 1000000 | bytes 1000 | tf_op jit(solution)/shard_map/mixer_backward/pallas_call | solution.py:481
  506.9 6.5 %convolution_convert_fusion.2 = bf16[1024,2048]{1,0:T(8,128)(2,1)S(1)} fusion(bf16[1024,896]{1,0:T(8,128)(2,1)} %get-tuple-element.266, bf16[2048,1152]{1,0:T(8,128)(2,1)S(1)} %bitcast.159), kind=kOutput, calls=%fused_computation.7 | convolution fusion | flops 3760193536 | bytes 9699328 | tf_op jit(solution)/shard_map/dot_general | solution.py:23
  531.1 10.4 %all-to-all-start.3 = ((bf16[16,64,896]{2,1,0:T(8,128)(2,1)}), bf16[16,64,896]{2,1,0:T(8,128)(2,1)S(1)}, u32[]{:S(2)}, u32[]{:S(2)}) async-start(bf16[16,64,896]{2,1,0:T(8,128)(2,1)} %add_convert_fusion.2), calls=%async_computation.3 | async-start | bytes 3670016 | tf_op jit(solution)/shard_map/all_to_all | solution.py:708
  551.7 34.5 %collective-permute-done.68 = bf16[256,2048]{1,0:T(8,128)(2,1)} collective-permute-done((bf16[256,2048]{1,0:T(8,128)(2,1)}, bf16[256,2048]{1,0:T(8,128)(2,1)}, u32[]{:S(2)}, u32[]{:S(2)}) %collective-permute-start.68) | collective-permute-done | bytes 1048608 | tf_op jit(solution)/shard_map/ppermute | solution.py:700
  (500 shorter events, 262.9 us)
Async XLA Ops:
  9.8 28.5 %collective-permute-start.9 = (bf16[8,64,1152]{2,1,0:T(8,128)(2,1)}, bf16[8,64,1152]{2,1,0:T(8,128)(2,1)S(1)}, u32[]{:S(2)}, u32[]{:S(2)}) collective-permute-start(bf16[8,64,1152]{2,1,0:T(8,128)(2,1)} %get-tuple-element.171), channel_id=1, source_target_pairs={{0,1},{1,0},{2,3},{3,2},{4,5},{5,4},{6,7},{7,6},{8,9},{9,8},{10,11... | collective-permute-start | bytes 3538952 | tf_op jit(solution)/shard_map/ppermute | solution.py:704
  15.3 23.0 %collective-permute-start.3 = (bf16[64,2048]{1,0:T(8,128)(2,1)S(1)}, bf16[64,2048]{1,0:T(8,128)(2,1)S(1)}, u32[]{:S(2)}, u32[]{:S(2)}) collective-permute-start(bf16[64,2048]{1,0:T(8,128)(2,1)S(1)} %fusion.20), channel_id=1, source_target_pairs={{0,16},{2,18},{4,20},{6,22},{8,24},{10,26},{12,28},{14,30},{16,0},... | collective-permute-start | bytes 786440 | tf_op jit(solution)/shard_map/ppermute | solution.py:700
  15.3 23.0 %collective-permute-start.2 = (bf16[64,2048]{1,0:T(8,128)(2,1)S(1)}, bf16[64,2048]{1,0:T(8,128)(2,1)S(1)}, u32[]{:S(2)}, u32[]{:S(2)}) collective-permute-start(bf16[64,2048]{1,0:T(8,128)(2,1)S(1)} %fusion.20), channel_id=1, source_target_pairs={{0,8},{2,10},{4,12},{6,14},{8,16},{10,18},{12,20},{14,22},{16,24},... | collective-permute-start | bytes 786440 | tf_op jit(solution)/shard_map/ppermute | solution.py:700
  16.3 22.0 %collective-permute-start.1 = (bf16[64,2048]{1,0:T(8,128)(2,1)S(1)}, bf16[64,2048]{1,0:T(8,128)(2,1)S(1)}, u32[]{:S(2)}, u32[]{:S(2)}) collective-permute-start(bf16[64,2048]{1,0:T(8,128)(2,1)S(1)} %fusion.20), channel_id=1, source_target_pairs={{0,4},{2,6},{4,0},{6,2},{8,12},{10,14},{12,8},{14,10},{16,20},{18,... | collective-permute-start | bytes 786440 | tf_op jit(solution)/shard_map/ppermute | solution.py:700
  42.0 58.3 %all-to-all-start = ((bf16[16,64,1152]{2,1,0:T(8,128)(2,1)}), bf16[16,64,1152]{2,1,0:T(8,128)(2,1)S(1)}, u32[]{:S(2)}, u32[]{:S(2)}) async-start(bf16[16,64,1152]{2,1,0:T(8,128)(2,1)} %pad_maximum_fusion.2), calls=%async_computation | async-start | bytes 4718592 | tf_op jit(solution)/shard_map/all_to_all | solution.py:708
  48.1 77.6 %collective-permute-start.14 = (bf16[8,4,512]{2,1,0:T(4,128)(2,1)S(1)}, bf16[8,4,512]{2,1,0:T(4,128)(2,1)S(1)}, u32[]{:S(2)}, u32[]{:S(2)}) collective-permute-start(bf16[8,4,512]{2,1,0:T(4,128)(2,1)S(1)} %maximum_bitcast_fusion), channel_id=1, source_target_pairs={{0,1},{1,0},{2,3},{3,2},{4,5},{5,4},{6,7},{7,6},{8,9},{9,8},{10,11... | collective-permute-start | bytes 98312 | tf_op jit(solution)/shard_map/ppermute | solution.py:704
  55.3 43.4 %collective-permute-start.6 = (bf16[192,2048]{1,0:T(8,128)(2,1)S(1)}, bf16[192,2048]{1,0:T(8,128)(2,1)S(1)}, u32[]{:S(2)}, u32[]{:S(2)}) collective-permute-start(bf16[192,2048]{1,0:T(8,128)(2,1)S(1)} %constant_dynamic-update-slice_fusion), channel_id=1, source_target_pairs={{0,4},{2,6},{4,0},{6,2},{8,12},{10,14},{12,8},{14,10},{16,20},{18,... | collective-permute-start | bytes 2359304 | tf_op jit(solution)/shard_map/ppermute | solution.py:700
  57.3 42.9 %collective-permute-start.5 = (bf16[192,2048]{1,0:T(8,128)(2,1)S(1)}, bf16[192,2048]{1,0:T(8,128)(2,1)}, u32[]{:S(2)}, u32[]{:S(2)}) collective-permute-start(bf16[192,2048]{1,0:T(8,128)(2,1)S(1)} %constant_dynamic-update-slice_fusion), channel_id=1, source_target_pairs={{0,2},{2,0},{4,6},{6,4},{8,10},{10,8},{12,14},{14,12},{16,18},{18,... | collective-permute-start | bytes 2359304 | tf_op jit(solution)/shard_map/ppermute | solution.py:700
  60.3 33.8 %collective-permute-start.8 = (bf16[32,2048]{1,0:T(8,128)(2,1)S(1)}, bf16[32,2048]{1,0:T(8,128)(2,1)S(1)}, u32[]{:S(2)}, u32[]{:S(2)}) collective-permute-start(bf16[32,2048]{1,0:T(8,128)(2,1)S(1)} %slice.289), channel_id=1, source_target_pairs={{0,4},{2,6},{4,0},{6,2},{8,12},{10,14},{12,8},{14,10},{16,20},{18,... | collective-permute-start | bytes 393224 | tf_op jit(solution)/shard_map/ppermute | solution.py:700
  61.0 37.8 %collective-permute-start.7 = (bf16[32,2048]{1,0:T(8,128)(2,1)S(1)}, bf16[32,2048]{1,0:T(8,128)(2,1)S(1)}, u32[]{:S(2)}, u32[]{:S(2)}) collective-permute-start(bf16[32,2048]{1,0:T(8,128)(2,1)S(1)} %slice.288), channel_id=1, source_target_pairs={{0,2},{2,0},{4,6},{6,4},{8,10},{10,8},{12,14},{14,12},{16,18},{18,... | collective-permute-start | bytes 393224 | tf_op jit(solution)/shard_map/ppermute | solution.py:700
  125.8 50.6 %all-to-all-start.1 = ((bf16[16,528,128]{2,1,0:T(8,128)(2,1)}), bf16[16,528,128]{2,1,0:T(8,128)(2,1)}, u32[]{:S(2)}, u32[]{:S(2)}) async-start(bf16[16,528,128]{2,1,0:T(8,128)(2,1)} %pad_maximum_fusion.3), calls=%async_computation.1 | async-start | bytes 4325376 | tf_op jit(solution)/shard_map/all_to_all | solution.py:708
  190.5 30.9 %collective-permute-start.17 = (bf16[256,2048]{1,0:T(8,128)(2,1)S(1)}, bf16[256,2048]{1,0:T(8,128)(2,1)S(1)}, u32[]{:S(2)}, u32[]{:S(2)}) collective-permute-start(bf16[256,2048]{1,0:T(8,128)(2,1)S(1)} %pad_maximum_fusion.9), channel_id=1, source_target_pairs={{0,2},{2,0},{4,6},{6,4},{8,10},{10,8},{12,14},{14,12},{16,18},{18,... | collective-permute-start | bytes 3145736 | tf_op jit(solution)/shard_map/ppermute | solution.py:700
  191.3 30.1 %collective-permute-start.18 = (bf16[256,2048]{1,0:T(8,128)(2,1)S(1)}, bf16[256,2048]{1,0:T(8,128)(2,1)S(1)}, u32[]{:S(2)}, u32[]{:S(2)}) collective-permute-start(bf16[256,2048]{1,0:T(8,128)(2,1)S(1)} %pad_maximum_fusion.10), channel_id=1, source_target_pairs={{0,4},{2,6},{4,0},{6,2},{8,12},{10,14},{12,8},{14,10},{16,20},{18,... | collective-permute-start | bytes 3145736 | tf_op jit(solution)/shard_map/ppermute | solution.py:700
  199.2 22.2 %collective-permute-start.20 = (bf16[64,2048]{1,0:T(8,128)(2,1)S(1)}, bf16[64,2048]{1,0:T(8,128)(2,1)S(1)}, u32[]{:S(2)}, u32[]{:S(2)}) collective-permute-start(bf16[64,2048]{1,0:T(8,128)(2,1)S(1)} %constant_dynamic-slice_fusion.5), channel_id=1, source_target_pairs={{0,16},{2,18},{4,20},{6,22},{8,24},{10,26},{12,28},{14,30},{16,0},... | collective-permute-start | bytes 786440 | tf_op jit(solution)/shard_map/ppermute | solution.py:700
  199.9 21.5 %collective-permute-start.19 = (bf16[64,2048]{1,0:T(8,128)(2,1)S(1)}, bf16[64,2048]{1,0:T(8,128)(2,1)S(1)}, u32[]{:S(2)}, u32[]{:S(2)}) collective-permute-start(bf16[64,2048]{1,0:T(8,128)(2,1)S(1)} %constant_dynamic-slice_fusion.5), channel_id=1, source_target_pairs={{0,8},{2,10},{4,12},{6,14},{8,16},{10,18},{12,20},{14,22},{16,24},... | collective-permute-start | bytes 786440 | tf_op jit(solution)/shard_map/ppermute | solution.py:700
  206.0 58.5 %collective-permute-start.34 = (bf16[16,528,128]{2,1,0:T(8,128)(2,1)}, bf16[16,528,128]{2,1,0:T(8,128)(2,1)}, u32[]{:S(2)}, u32[]{:S(2)}) collective-permute-start(bf16[16,528,128]{2,1,0:T(8,128)(2,1)} %all-to-all-done.1), channel_id=1, source_target_pairs={{0,1},{1,0},{2,3},{3,2},{4,5},{5,4},{6,7},{7,6},{8,9},{9,8},{10,11... | collective-permute-start | bytes 6488072 | tf_op jit(solution)/shard_map/ppermute | solution.py:704
  227.6 27.6 %collective-permute-start.26 = (bf16[256,2048]{1,0:T(8,128)(2,1)}, bf16[256,2048]{1,0:T(8,128)(2,1)S(1)}, u32[]{:S(2)}, u32[]{:S(2)}) collective-permute-start(bf16[256,2048]{1,0:T(8,128)(2,1)} %constant_dynamic-update-slice_fusion.13), channel_id=1, source_target_pairs={{0,4},{2,6},{4,0},{6,2},{8,12},{10,14},{12,8},{14,10},{16,20},{18,... | collective-permute-start | bytes 3145736 | tf_op jit(solution)/shard_map/ppermute | solution.py:700
  229.3 25.9 %collective-permute-start.25 = (bf16[256,2048]{1,0:T(8,128)(2,1)}, bf16[256,2048]{1,0:T(8,128)(2,1)}, u32[]{:S(2)}, u32[]{:S(2)}) collective-permute-start(bf16[256,2048]{1,0:T(8,128)(2,1)} %constant_dynamic-update-slice_fusion.13), channel_id=1, source_target_pairs={{0,2},{2,0},{4,6},{6,4},{8,10},{10,8},{12,14},{14,12},{16,18},{18,... | collective-permute-start | bytes 3145736 | tf_op jit(solution)/shard_map/ppermute | solution.py:700
  284.1 22.0 %collective-permute-start.36 = (bf16[192,2048]{1,0:T(8,128)(2,1)S(1)}, bf16[192,2048]{1,0:T(8,128)(2,1)S(1)}, u32[]{:S(2)}, u32[]{:S(2)}) collective-permute-start(bf16[192,2048]{1,0:T(8,128)(2,1)S(1)} %constant_dynamic-update-slice_fusion.17), channel_id=1, source_target_pairs={{0,4},{2,6},{4,0},{6,2},{8,12},{10,14},{12,8},{14,10},{16,20},{18,... | collective-permute-start | bytes 2359304 | tf_op jit(solution)/shard_map/ppermute | solution.py:700
  386.4 29.1 %collective-permute-start.53 = (bf16[256,2048]{1,0:T(8,128)(2,1)S(1)}, bf16[256,2048]{1,0:T(8,128)(2,1)S(1)}, u32[]{:S(2)}, u32[]{:S(2)}) collective-permute-start(bf16[256,2048]{1,0:T(8,128)(2,1)S(1)} %pad_maximum_fusion.13), channel_id=1, source_target_pairs={{0,2},{2,0},{4,6},{6,4},{8,10},{10,8},{12,14},{14,12},{16,18},{18,... | collective-permute-start | bytes 3145736 | tf_op jit(solution)/shard_map/ppermute | solution.py:700
  387.4 28.0 %collective-permute-start.54 = (bf16[256,2048]{1,0:T(8,128)(2,1)S(1)}, bf16[256,2048]{1,0:T(8,128)(2,1)S(1)}, u32[]{:S(2)}, u32[]{:S(2)}) collective-permute-start(bf16[256,2048]{1,0:T(8,128)(2,1)S(1)} %pad_maximum_fusion.14), channel_id=1, source_target_pairs={{0,4},{2,6},{4,0},{6,2},{8,12},{10,14},{12,8},{14,10},{16,20},{18,... | collective-permute-start | bytes 3145736 | tf_op jit(solution)/shard_map/ppermute | solution.py:700
  392.9 22.5 %collective-permute-start.51 = (bf16[64,2048]{1,0:T(8,128)(2,1)S(1)}, bf16[64,2048]{1,0:T(8,128)(2,1)S(1)}, u32[]{:S(2)}, u32[]{:S(2)}) collective-permute-start(bf16[64,2048]{1,0:T(8,128)(2,1)S(1)} %get-tuple-element.245), channel_id=1, source_target_pairs={{0,16},{2,18},{4,20},{6,22},{8,24},{10,26},{12,28},{14,30},{16,0},... | collective-permute-start | bytes 786440 | tf_op jit(solution)/shard_map/ppermute | solution.py:700
  415.6 22.9 %collective-permute-start.57 = (bf16[256,2048]{1,0:T(8,128)(2,1)S(1)}, bf16[256,2048]{1,0:T(8,128)(2,1)S(1)}, u32[]{:S(2)}, u32[]{:S(2)}) collective-permute-start(bf16[256,2048]{1,0:T(8,128)(2,1)S(1)} %constant_dynamic-update-slice_fusion.35), channel_id=1, source_target_pairs={{0,4},{2,6},{4,0},{6,2},{8,12},{10,14},{12,8},{14,10},{16,20},{18,... | collective-permute-start | bytes 3145736 | tf_op jit(solution)/shard_map/ppermute | solution.py:700
  417.2 23.2 %collective-permute-start.56 = (bf16[256,2048]{1,0:T(8,128)(2,1)S(1)}, bf16[256,2048]{1,0:T(8,128)(2,1)S(1)}, u32[]{:S(2)}, u32[]{:S(2)}) collective-permute-start(bf16[256,2048]{1,0:T(8,128)(2,1)S(1)} %constant_dynamic-update-slice_fusion.35), channel_id=1, source_target_pairs={{0,2},{2,0},{4,6},{6,4},{8,10},{10,8},{12,14},{14,12},{16,18},{18,... | collective-permute-start | bytes 3145736 | tf_op jit(solution)/shard_map/ppermute | solution.py:700
  456.4 74.7 %all-to-all-start.2 = ((bf16[16,656,128]{2,1,0:T(8,128)(2,1)}), bf16[16,656,128]{2,1,0:T(8,128)(2,1)}, u32[]{:S(2)}, u32[]{:S(2)}) async-start(bf16[16,656,128]{2,1,0:T(8,128)(2,1)} %constant_dynamic-update-slice_fusion.44), calls=%async_computation.2 | async-start | bytes 5373952 | tf_op jit(solution)/shard_map/all_to_all | solution.py:708
  464.1 53.8 %collective-permute-start.64 = (bf16[1024,1024]{0,1:T(8,128)(2,1)S(1)}, bf16[1024,1024]{0,1:T(8,128)(2,1)S(1)}, u32[]{:S(2)}, u32[]{:S(2)}) collective-permute-start(bf16[1024,1024]{0,1:T(8,128)(2,1)S(1)} %bitcast.170), channel_id=1, source_target_pairs={{0,1},{1,0},{2,3},{3,2},{4,5},{5,4},{6,7},{7,6},{8,9},{9,8},{10,11... | collective-permute-start | bytes 6291464 | tf_op jit(solution)/shard_map/ppermute | solution.py:704
  531.1 55.2 %all-to-all-start.3 = ((bf16[16,64,896]{2,1,0:T(8,128)(2,1)}), bf16[16,64,896]{2,1,0:T(8,128)(2,1)S(1)}, u32[]{:S(2)}, u32[]{:S(2)}) async-start(bf16[16,64,896]{2,1,0:T(8,128)(2,1)} %add_convert_fusion.2), calls=%async_computation.3 | async-start | bytes 3670016 | tf_op jit(solution)/shard_map/all_to_all | solution.py:708
  544.6 41.6 %collective-permute-start.68 = (bf16[256,2048]{1,0:T(8,128)(2,1)}, bf16[256,2048]{1,0:T(8,128)(2,1)}, u32[]{:S(2)}, u32[]{:S(2)}) collective-permute-start(bf16[256,2048]{1,0:T(8,128)(2,1)} %pad_maximum_fusion.15), channel_id=1, source_target_pairs={{0,2},{2,0},{4,6},{6,4},{8,10},{10,8},{12,14},{14,12},{16,18},{18,... | collective-permute-start | bytes 3145736 | tf_op jit(solution)/shard_map/ppermute | solution.py:700
  547.6 38.6 %collective-permute-start.69 = (bf16[256,2048]{1,0:T(8,128)(2,1)}, bf16[256,2048]{1,0:T(8,128)(2,1)}, u32[]{:S(2)}, u32[]{:S(2)}) collective-permute-start(bf16[256,2048]{1,0:T(8,128)(2,1)} %pad_maximum_fusion.16), channel_id=1, source_target_pairs={{0,4},{2,6},{4,0},{6,2},{8,12},{10,14},{12,8},{14,10},{16,20},{18,... | collective-permute-start | bytes 3145736 | tf_op jit(solution)/shard_map/ppermute | solution.py:700
  589.6 26.5 %collective-permute-start.72 = (bf16[64,2048]{1,0:T(8,128)(2,1)}, bf16[64,2048]{1,0:T(8,128)(2,1)}, u32[]{:S(2)}, u32[]{:S(2)}) collective-permute-start(bf16[64,2048]{1,0:T(8,128)(2,1)} %get-tuple-element.441), channel_id=1, source_target_pairs={{0,8},{2,10},{4,12},{6,14},{8,16},{10,18},{12,20},{14,22},{16,24},... | collective-permute-start | bytes 786440 | tf_op jit(solution)/shard_map/ppermute | solution.py:700
  591.2 25.0 %collective-permute-start.71 = (bf16[64,2048]{1,0:T(8,128)(2,1)}, bf16[64,2048]{1,0:T(8,128)(2,1)}, u32[]{:S(2)}, u32[]{:S(2)}) collective-permute-start(bf16[64,2048]{1,0:T(8,128)(2,1)} %get-tuple-element.442), channel_id=1, source_target_pairs={{0,16},{2,18},{4,20},{6,22},{8,24},{10,26},{12,28},{14,30},{16,0},... | collective-permute-start | bytes 786440 | tf_op jit(solution)/shard_map/ppermute | solution.py:700
  593.4 22.7 %collective-permute-start.70 = (bf16[64,2048]{1,0:T(8,128)(2,1)}, bf16[64,2048]{1,0:T(8,128)(2,1)}, u32[]{:S(2)}, u32[]{:S(2)}) collective-permute-start(bf16[64,2048]{1,0:T(8,128)(2,1)} %get-tuple-element.443), channel_id=1, source_target_pairs={{0,24},{2,26},{4,28},{6,30},{8,0},{10,2},{12,4},{14,6},{16,8},{18,... | collective-permute-start | bytes 786440 | tf_op jit(solution)/shard_map/ppermute | solution.py:700
  (122 other events, 1173.0 us)
